TPU v7x, 32 devices: a whole 2x2x4 slice. The times are simulated.
32 devices in a mesh: groups: 2 (over x), blk: 16 (over z, y, core).
Axes of the slice: x: 2, y: 2, z: 4, core: 2. Of those that a mesh axis runs over, the one named last changes fastest.
Arguments:
- density: bfloat16 [256, 9, 128, 128], P(('groups', 'blk')), parts along dimension 0, may hold values from -0.25 to 0.25
- ao_values: bfloat16 [384, 4, 128, 256], P(('groups', 'blk')), parts along dimension 0, may hold values from -6 to 6
- kernel: bfloat16 [384, 256, 256], P(('groups', 'blk')), parts along dimension 0, may hold values from -0.375 to 0.375
- grid_weights: float32 [384, 256], P(('groups', 'blk')), parts along dimension 0, may hold values from 0.002 to 0.02
- centre: int32 [384], P(('groups', 'blk')), parts along dimension 0, may hold values from 2 to 125, as said below
- sig_offsets: int32 [384, 4], P(('groups', 'blk')), parts along dimension 0, may hold values from -2 to 2, as said below
- counts: int32 [384], P(('groups', 'blk')), parts along dimension 0, may hold values from 0 to 4, as said below
Outputs:
- exchange: float32 [256, 9, 128, 128], P(('groups', 'blk')), parts along dimension 0
There are 2 independent parts, one for each index of `groups`. A program takes and returns all parts, laid end to end along the dimension named above; each array names one. Nothing has to cross between parts.
Inputs may be any that keep to these rules, and one draw needn't show every extreme that they name: `centre`: the batches in the rows of one blk device have their atom block among that device's 8 blocks; the device's first batch slot has the lowest such block that the range allows, its slot 10 the highest. `sig_offsets`: the 4 offsets of a batch are distinct; those of a device's first slot and of its slot 10 include -2 and 2. `counts`: the first batch slot and slot 10 of each blk device have 4 live blocks and its last slot none.
All inputs are finite; a program needn't handle non-finite values.
Results may differ from a plain program's by a relative error of at most 0.0041.
Values may be sent and summed in bfloat16 or wider, within the bound.
No kernel may reach another device: no remote copies, remote signals or barrier semaphores. Data moves between devices by JAX's collectives and lax.ppermute only.
A program may use at most 128 MiB of HBM per device.

v0:
```python
import functools

import jax
import jax.numpy as jnp
from jax import lax
from jax.experimental import pallas as pl
from jax.experimental.pallas import tpu as pltpu
from jax.sharding import PartitionSpec as P

MIB = 1 << 20
GROUP = 2
LISTS = 6
BUDGET = 43
COST = (10, 7)
SMEM_SPEC = pl.BlockSpec(memory_space=pltpu.SMEM)
VMEM_SPEC = pl.BlockSpec(memory_space=pltpu.VMEM)
ANY_SPEC = pl.BlockSpec(memory_space=pl.ANY)


class Geometry:
    def __init__(self, rows, band, batches, slots):
        self.rows, self.band, self.batches, self.slots = rows, band, batches, slots
        self.half = half = (band - 1) // 2
        self.reach = reach = half // 2
        self.own = rows * band
        low = [(-m, reach + m, band) for m in range(reach, 0, -1)]
        high = [(rows + m, 0, 3 * reach - m) for m in range(reach)]
        self.halo = sum(stop - start for _, start, stop in low)
        low_cut = [half - row for row, _, _ in low]
        high_cut = [rows - row + half for row, _, _ in high]
        early = (
            [(row, cut, stop) for (row, _, stop), cut in zip(low, low_cut)],
            [(row, start, cut) for (row, start, _), cut in zip(high, high_cut)],
        )
        late = (
            [(row, start, cut) for (row, start, _), cut in zip(low, low_cut)],
            [(row, cut, stop) for (row, _, stop), cut in zip(high, high_cut)],
        )
        self.early = sum(stop - start for _, start, stop in early[0])
        self.late = self.halo - self.early
        self.first_at = self.own
        self.early_at = self.own + self.halo
        self.late_at = self.early_at + self.early
        self.spare = self.late_at + self.late
        self.halo_base = self.bases((low, high))
        self.early_base = self.bases(early)
        self.late_base = self.bases(late)
        shifts = (rows, -rows)
        self.packs = [self.places(*pair) for pair in zip((low, high), shifts)]
        self.early_packs = [self.places(*pair) for pair in zip(early, shifts)]
        self.late_packs = [self.places(*pair) for pair in zip(late, shifts)]
        self.quiet = [self.others(self.packs[1 - near]) for near in range(2)]
        self.list_size = batches + 2
        self.lengths_at = LISTS * self.list_size
        self.local_at = self.lengths_at + LISTS
        self.count_at = self.local_at + batches
        self.offsets_at = self.count_at + batches
        self.odd_at = self.offsets_at + slots * batches
        self.meta_size = self.odd_at + 1

    def bases(self, sides):
        found = {}
        for segments in sides:
            place = 0
            for row, start, stop in segments:
                found[row] = place - start
                place += stop - start
        return found

    def places(self, segments, shift):
        pack, place = ([], 0)
        for row, start, stop in segments:
            pack.append(((row + shift) * self.band + start, place, stop - start))
            place += stop - start
        return pack

    def others(self, pack):
        touched = set()
        for start, _, count in pack:
            touched.update(range(start, start + count))
        runs = []
        for index in range(self.own):
            if index in touched:
                continue
            if runs and sum(runs[-1]) == index:
                runs[-1] = (runs[-1][0], runs[-1][1] + 1)
            else:
                runs.append((index, 1))
        return runs

    def pick(self, bases, shift, row, otherwise):
        value = otherwise
        for at, base in bases.items():
            value = jnp.where(row == at, base + shift, value)
        return value


def run_copies(copies):
    for copy in copies:
        copy.start()
    for copy in copies:
        copy.wait()


def by_parity(odd, body, first, second):
    @pl.when(jnp.logical_not(odd))
    def _():
        body(first, second)

    @pl.when(odd)
    def _():
        body(second, first)


CROSS_MANY, CROSS_FEW, NEAR_MANY, NEAR_FEW, INNER_MANY, INNER_FEW = range(LISTS)


def build_lists(geo, index, centre_ref, offsets_ref, counts_ref, meta_ref):
    first = index * geo.rows
    odd = index % 2 == 1
    meta_ref[geo.odd_at] = odd.astype(jnp.int32)
    lengths = [jnp.int32(0)] * LISTS
    for b in range(geo.batches):
        local = centre_ref[b] - first
        count = counts_ref[b]
        meta_ref[geo.local_at + b] = local
        meta_ref[geo.count_at + b] = count
        low = high = jnp.bool_(False)
        for k in range(geo.slots):
            offset = offsets_ref[k, b]
            meta_ref[geo.offsets_at + k * geo.batches + b] = offset
            row = local + offset
            low = low | ((k < count) & (row < 0))
            high = high | ((k < count) & (row >= geo.rows))
        cross = (odd & high) | (jnp.logical_not(odd) & low)
        near = (odd & low) | (jnp.logical_not(odd) & high)
        inner = jnp.logical_not(low | high)
        many = count > 2
        few = (count > 0) & jnp.logical_not(many)
        kinds = [kind & size for kind in (cross, near, inner) for size in (many, few)]
        for which, member in enumerate(kinds):
            meta_ref[which * geo.list_size + lengths[which]] = b
            lengths[which] = lengths[which] + member.astype(jnp.int32)
    for which in range(LISTS):
        meta_ref[which * geo.list_size + lengths[which]] = geo.batches
        meta_ref[geo.lengths_at + which] = lengths[which]


def zone(geo, odd, cross):
    span = min(2 * geo.reach, geo.rows) * geo.band
    if not cross:
        span = geo.own - span
    return pl.ds(jnp.where(odd == cross, geo.own - span, 0), span)


def pack_kernel(
    geo, density_ref, centre_in, offsets_in, counts_in,
    near_ref, cross_ref, meta_ref, acc_ref,
    centre_ref, offsets_ref, counts_ref, sems,
):
    index = lax.axis_index("blk")
    odd = index % 2 == 1

    def copies(up, down):
        return [
            pltpu.make_async_copy(
                density_ref.at[pl.ds(start, count)], ref.at[pl.ds(place, count)], sems.at[side, i]
            )
            for side, (pack, ref) in enumerate(zip(geo.packs, (up, down)))
            for i, (start, place, count) in enumerate(pack)
        ]

    def start(up, down):
        for copy in copies(up, down):
            copy.start()

    by_parity(odd, start, near_ref, cross_ref)
    scalars = [
        pltpu.make_async_copy(*pair, sems.at[2, i])
        for i, pair in enumerate(
            ((centre_in, centre_ref), (offsets_in, offsets_ref), (counts_in, counts_ref))
        )
    ]
    for copy in scalars:
        copy.start()
    for where in (zone(geo, odd, False), pl.ds(geo.first_at, geo.halo), pl.ds(geo.late_at, geo.late)):
        acc_ref[where] = jnp.zeros_like(acc_ref[where])
    for copy in scalars:
        copy.wait()
    build_lists(geo, index, centre_ref, offsets_ref, counts_ref, meta_ref)
    for copy in copies(near_ref, cross_ref):
        copy.wait()


def group_count(geo, meta_ref, which):
    return (meta_ref[geo.lengths_at + which] + GROUP - 1) // GROUP


def inner_share(geo, meta_ref):
    room = BUDGET
    for which in (CROSS_MANY, CROSS_FEW, NEAR_MANY, NEAR_FEW):
        room = room - COST[which % 2] * group_count(geo, meta_ref, which)
    share = []
    for which in (INNER_MANY, INNER_FEW):
        cost = COST[which % 2]
        taken = jnp.minimum(jnp.maximum(room, 0) // cost, group_count(geo, meta_ref, which))
        room = room - cost * taken
        share.append(taken)
    return share


def each_group(geo, meta_ref, which, body, begin=0, end=None):
    length = meta_ref[geo.lengths_at + which]

    def step(i, carry):
        chosen = []
        for n in range(GROUP):
            place = i * GROUP + n
            there = place < length
            b = meta_ref[which * geo.list_size + jnp.minimum(place, length)]
            chosen.append((jnp.where(there, b, 0), there))
        body(chosen)
        return carry

    lax.fori_loop(begin, group_count(geo, meta_ref, which) if end is None else end, step, 0)


class Slots:
    def __init__(self, geo, meta_ref, b, there, width):
        local = meta_ref[geo.local_at + b]
        count = jnp.where(there, meta_ref[geo.count_at + b], 0)
        self.offset = [meta_ref[geo.offsets_at + k * geo.batches + b] for k in range(width)]
        self.local = local
        self.row = [local + offset for offset in self.offset]
        self.live = [k < count for k in range(width)]
        self.own = [(row >= 0) & (row < geo.rows) for row in self.row]
        self.width = width


def panels(slots, ao_ref, b):
    return jnp.concatenate(
        [
            ao_ref[b, k] * jnp.where(slots.live[k], 1.0, 0.0).astype(ao_ref.dtype)
            for k in range(slots.width)
        ],
        axis=0,
    )


def gathered(tiles_ref, places):
    return jnp.concatenate(
        [jnp.concatenate([tiles_ref[place] for place in row], axis=1) for row in places], axis=0
    )


def chain(xs, tiles, batches, kernel_ref, weights_ref):
    fs = [
        jnp.dot(t, x, preferred_element_type=jnp.float32).astype(jnp.bfloat16)
        for t, x in zip(tiles, xs)
    ]
    gs = [
        jnp.dot(f, kernel_ref[b], preferred_element_type=jnp.float32) for f, b in zip(fs, batches)
    ]
    hs = [(g * weights_ref[pl.ds(b, 1), :]).astype(jnp.bfloat16) for g, b in zip(gs, batches)]
    return [
        lax.dot_general(x, h, (((1,), (1,)), ((), ())), preferred_element_type=jnp.float32)
        for x, h in zip(xs, hs)
    ]


def scatter(part, target, nb, acc_ref):
    for k, row in enumerate(target):
        for j, place in enumerate(row):
            acc_ref[place] += part[k * nb : (k + 1) * nb, j * nb : (j + 1) * nb]


def add_whole(
    geo, chosen, width, meta_ref, tiles_ref, ao_ref, kernel_ref, weights_ref, acc_ref, halo_ref=None
):
    xs, tiles, targets = ([], [], [])
    for b, there in chosen:
        slots = Slots(geo, meta_ref, b, there, width)
        xs.append(panels(slots, ao_ref, b))
        rows, target = ([], [])
        for k in range(width):
            band = [slots.offset[j] - slots.offset[k] + geo.half for j in range(width)]
            own = slots.own[k]
            base = jnp.where(slots.live[k] & own, slots.row[k], 0) * geo.band
            row = jnp.concatenate([tiles_ref[base + o] for o in band], axis=1)
            if halo_ref is not None:
                away = slots.live[k] & jnp.logical_not(own)
                outside = jnp.where(away, geo.pick(geo.halo_base, 0, slots.row[k], 0), 0)
                other = [halo_ref[jnp.where(away, outside + o, 0)] for o in band]
                row = jnp.where(away, jnp.concatenate(other, axis=1), row)
                base = jnp.where(away, outside + geo.first_at, base)
            rows.append(row)
            target.append(
                [
                    jnp.where(slots.live[k] & slots.live[j], base + band[j], geo.spare)
                    for j in range(width)
                ]
            )
        tiles.append(jnp.concatenate(rows, axis=0))
        targets.append(target)
    parts = chain(xs, tiles, [b for b, _ in chosen], kernel_ref, weights_ref)
    for part, target in zip(parts, targets):
        scatter(part, target, ao_ref.shape[2], acc_ref)


def add_own(geo, chosen, width, meta_ref, tiles_ref, ao_ref, kernel_ref, weights_ref, acc_ref):
    xs, tiles, targets = ([], [], [])
    for b, there in chosen:
        slots = Slots(geo, meta_ref, b, there, width)
        xs.append(panels(slots, ao_ref, b))
        places, target = ([], [])
        for k in range(width):
            row = slots.row[k]
            band = [slots.offset[j] - slots.offset[k] + geo.half for j in range(width)]
            base = jnp.where(slots.own[k], row, 0) * geo.band
            places.append([base + o for o in band])
            base = geo.pick(geo.early_base, geo.early_at, row, base)
            target.append(
                [
                    jnp.where(
                        slots.live[k] & slots.live[j] & slots.own[j], base + band[j], geo.spare
                    )
                    for j in range(width)
                ]
            )
        tiles.append(gathered(tiles_ref, places))
        targets.append(target)
    parts = chain(xs, tiles, [b for b, _ in chosen], kernel_ref, weights_ref)
    for part, target in zip(parts, targets):
        scatter(part, target, ao_ref.shape[2], acc_ref)


def add_halo(geo, chosen, width, meta_ref, halo_ref, ao_ref, kernel_ref, weights_ref, acc_ref):
    outer = min(geo.reach, width)
    xs, tiles, targets = ([], [], [])
    for b, there in chosen:
        slots = Slots(geo, meta_ref, b, there, width)
        xs.append(panels(slots, ao_ref, b))
        found = jnp.int32(0)
        picked = [jnp.int32(0)] * outer
        for k in range(width):
            away = slots.live[k] & jnp.logical_not(slots.own[k])
            for i in range(outer):
                picked[i] = jnp.where(away & (found <= i), slots.offset[k], picked[i])
            found = found + away.astype(jnp.int32)
        places, target = ([], [[None] * outer for _ in range(width)])
        for i in range(outer):
            base = geo.pick(geo.halo_base, 0, slots.local + picked[i], 0)
            places.append(
                [
                    jnp.where(there, base + slots.offset[j] - picked[i] + geo.half, 0)
                    for j in range(width)
                ]
            )
        for k in range(width):
            row = slots.row[k]
            base = geo.pick(geo.late_base, geo.late_at, row, row * geo.band)
            for i in range(outer):
                target[k][i] = jnp.where(
                    slots.live[k] & (i < found),
                    base + picked[i] - slots.offset[k] + geo.half,
                    geo.spare,
                )
        tiles.append(gathered(halo_ref, places))
        targets.append(target)
    parts = chain(xs, tiles, [b for b, _ in chosen], kernel_ref, weights_ref)
    for part, target in zip(parts, targets):
        scatter(part, target, ao_ref.shape[2], acc_ref)


def early_kernel(
    geo, meta_ref, tiles_ref, ao_ref, kernel_ref, weights_ref, acc_in, acc_ref, early_out
):
    odd = meta_ref[geo.odd_at] == 1
    for where in (zone(geo, odd, True), pl.ds(geo.early_at, geo.early), pl.ds(geo.spare, 1)):
        acc_ref[where] = jnp.zeros_like(acc_ref[where])
    refs = (meta_ref, tiles_ref, ao_ref, kernel_ref, weights_ref, acc_ref)
    for which, width in ((CROSS_MANY, geo.slots), (CROSS_FEW, 2)):
        each_group(
            geo, meta_ref, which, lambda chosen, width=width: add_own(geo, chosen, width, *refs)
        )
    early_out[...] = acc_ref[pl.ds(geo.early_at, geo.early)].astype(early_out.dtype)


def near_kernel(
    geo, meta_ref, halo_ref, tiles_ref, ao_ref, kernel_ref, weights_ref, acc_in, acc_ref, first_out
):
    refs = (meta_ref, tiles_ref, ao_ref, kernel_ref, weights_ref, acc_ref, halo_ref)
    for which, width in ((NEAR_MANY, geo.slots), (NEAR_FEW, 2)):
        each_group(
            geo, meta_ref, which, lambda chosen, width=width: add_whole(geo, chosen, width, *refs)
        )
    first_out[...] = acc_ref[pl.ds(geo.first_at, geo.halo)].astype(first_out.dtype)
    share = inner_share(geo, meta_ref)
    for which, width, end in ((INNER_MANY, geo.slots, share[0]), (INNER_FEW, 2, share[1])):
        each_group(
            geo,
            meta_ref,
            which,
            lambda chosen, width=width: add_whole(geo, chosen, width, *refs[:-1]),
            end=end,
        )


def late_kernel(
    geo, meta_ref, halo_ref, ao_ref, kernel_ref, weights_ref, acc_in, acc_ref, late_out
):
    refs = (meta_ref, halo_ref, ao_ref, kernel_ref, weights_ref, acc_ref)
    for which, width in ((CROSS_MANY, geo.slots), (CROSS_FEW, 2)):
        each_group(
            geo, meta_ref, which, lambda chosen, width=width: add_halo(geo, chosen, width, *refs)
        )
    late_out[...] = acc_ref[pl.ds(geo.late_at, geo.late)].astype(late_out.dtype)


def inner_kernel(
    geo, meta_ref, first_ref, tiles_ref, ao_ref, kernel_ref, weights_ref, acc_in,
    acc_ref, out_ref, sems,
):
    refs = (meta_ref, tiles_ref, ao_ref, kernel_ref, weights_ref, acc_ref)
    share = inner_share(geo, meta_ref)
    for which, width, begin in ((INNER_MANY, geo.slots, share[0]), (INNER_FEW, 2, share[1])):
        each_group(
            geo,
            meta_ref,
            which,
            lambda chosen, width=width: add_whole(geo, chosen, width, *refs),
            begin=begin,
        )

    def finish_near(up, down):
        near = 0 if up else 1
        for start, place, count in geo.packs[near]:
            acc_ref[pl.ds(start, count)] += first_ref[pl.ds(place, count)].astype(jnp.float32)
        run_copies(
            [
                pltpu.make_async_copy(
                    acc_ref.at[pl.ds(start, count)], out_ref.at[pl.ds(start, count)], sems.at[i]
                )
                for i, (start, count) in enumerate(geo.quiet[near])
            ]
        )

    by_parity(meta_ref[geo.odd_at] == 1, finish_near, True, False)


def finish_kernel(geo, meta_ref, early_ref, late_ref, acc_ref, out_in, out_ref, total, sems):
    def add(up, down):
        copies = []
        for packs, ref in ((geo.early_packs, early_ref), (geo.late_packs, late_ref)):
            for start, place, count in packs[0 if up else 1]:
                spot = pl.ds(len(copies) * geo.band, count)
                total[spot] = acc_ref[pl.ds(start, count)] + ref[pl.ds(place, count)].astype(
                    jnp.float32
                )
                copy = pltpu.make_async_copy(
                    total.at[spot], out_ref.at[pl.ds(start, count)], sems.at[len(copies)]
                )
                copy.start()
                copies.append(copy)
        for copy in copies:
            copy.wait()

    by_parity(meta_ref[geo.odd_at] == 1, add, False, True)


def call(kernel, out_shape, in_specs, out_specs, scratch, aliases=None, cost=None):
    return pl.pallas_call(
        kernel,
        out_shape=out_shape,
        in_specs=in_specs,
        out_specs=out_specs,
        scratch_shapes=scratch,
        input_output_aliases=aliases or {},
        cost_estimate=cost,
        compiler_params=pltpu.CompilerParams(vmem_limit_bytes=16 * MIB),
    )


def to_first(x, size):
    pairs = [(i, i + 1) for i in range(0, size - 1, 2)]
    got = lax.ppermute(x, "blk", pairs + [(j, i) for i, j in pairs])
    return pltpu.with_memory_space_constraint(got, pltpu.VMEM)


def to_second(x, size):
    pairs = [(i, i + 1) for i in range(1, size - 1, 2)]
    got = lax.ppermute(x, "blk", pairs + [(j, i) for i, j in pairs])
    return pltpu.with_memory_space_constraint(got, pltpu.VMEM)


def local(density, ao_values, kernel, grid_weights, centre, sig_offsets, counts):
    rows, band, nb, _ = density.shape
    batches, slots, _, pts = ao_values.shape
    size = lax.axis_size("blk")
    geo = Geometry(rows, band, batches, slots)
    in_hbm = lambda x: pltpu.with_memory_space_constraint(x, pltpu.HBM)
    tiles = density.reshape(geo.own, nb, nb)
    pack = lambda count: pltpu.VMEM((count, nb, nb), jnp.bfloat16)
    dma = pltpu.SemaphoreType.DMA
    acc_type = pltpu.VMEM((geo.spare + 1, nb, nb), jnp.float32)

    near_halo, cross_halo, meta, acc = call(
        functools.partial(pack_kernel, geo),
        (pack(geo.halo),) * 2 + (pltpu.SMEM((geo.meta_size,), jnp.int32), acc_type),
        [ANY_SPEC] * 4,
        (VMEM_SPEC,) * 2 + (SMEM_SPEC, VMEM_SPEC),
        [
            pltpu.SMEM((batches,), jnp.int32),
            pltpu.SMEM((slots, batches), jnp.int32),
            pltpu.SMEM((batches,), jnp.int32),
            dma((3, max(geo.reach, 3))),
        ],
        cost=pl.CostEstimate(flops=10**10, bytes_accessed=10**8, transcendentals=0),
    )(in_hbm(tiles), in_hbm(centre), in_hbm(sig_offsets.T), in_hbm(counts))
    cross_halo = to_second(cross_halo, size)
    near_halo = to_first(near_halo, size)

    panel = (tiles, ao_values, kernel, grid_weights)
    acc, early = call(
        functools.partial(early_kernel, geo),
        (acc_type, pack(geo.early)),
        [SMEM_SPEC] + [VMEM_SPEC] * 5,
        (VMEM_SPEC,) * 2,
        [],
        {5: 0},
    )(meta, *panel, acc)
    early = to_second(early, size)

    acc, first = call(
        functools.partial(near_kernel, geo),
        (acc_type, pack(geo.halo)),
        [SMEM_SPEC] + [VMEM_SPEC] * 6,
        (VMEM_SPEC,) * 2,
        [],
        {6: 0},
    )(meta, near_halo, *panel, acc)
    first = to_first(first, size)

    acc, late = call(
        functools.partial(late_kernel, geo),
        (acc_type, pack(geo.late)),
        [SMEM_SPEC] + [VMEM_SPEC] * 5,
        (VMEM_SPEC,) * 2,
        [],
        {5: 0},
    )(meta, cross_halo, *panel[1:], acc)
    late = to_second(late, size)

    whole = jax.ShapeDtypeStruct((geo.own, nb, nb), jnp.float32)
    acc, out = call(
        functools.partial(inner_kernel, geo),
        (acc_type, whole),
        [SMEM_SPEC] + [VMEM_SPEC] * 6,
        (VMEM_SPEC, ANY_SPEC),
        [dma((max(len(runs) for runs in geo.quiet),))],
        {6: 0},
    )(meta, first, *panel, acc)

    parts = 2 * geo.reach
    out = call(
        functools.partial(finish_kernel, geo),
        whole,
        [SMEM_SPEC] + [VMEM_SPEC] * 3 + [ANY_SPEC],
        ANY_SPEC,
        [pltpu.VMEM((parts * band, nb, nb), jnp.float32), dma((parts,))],
        {4: 0},
    )(meta, early, late, acc, out)
    return out.reshape(rows, band, nb, nb)


def solution(mesh):
    placed = (
        P(("groups", "blk"), None, None, None),
        P(("groups", "blk"), None, None, None),
        P(("groups", "blk"), None, None),
        P(("groups", "blk"), None),
        P(("groups", "blk")),
        P(("groups", "blk"), None),
        P(("groups", "blk")),
    )
    return jax.shard_map(
        local,
        mesh=mesh,
        in_specs=placed,
        out_specs=P(("groups", "blk"), None, None, None),
        check_vma=False,
    )
```

profile of v0, /device:TPU:9, one launch (start us, length us, event | category | flops | bytes accessed | tf_op | source)
XLA Modules:
  0.0 25.5 jit_solution(657052987012478392)
XLA Ops:
  0.0 0.0 copy-start
  0.0 0.0 copy-start.1
  0.0 0.0 copy-start.2
  0.0 0.0 copy-start.3
  0.0 1.4 %shard_map.73 = (bf16[11,128,128]{2,1,0:T(8,128)(2,1)S(1)}, bf16[11,128,128]{2,1,0:T(8,128)(2,1)S(1)}, s32[163]{0:T(256)S(4)}, f32[95,128,128]{2,1,0:T(8,128)S(1)}) custom-call(bf16[72,128,128]{2,1,0:T(8,128)(2,1)} %bitcast.3, s32[12]{0:T(128)} %centre_in.1, s32[4,12]{1,0:T(4,128)} %bitcast.7, s32[12]{0:T(128)} %counts_in.1), custom_call_target="tpu_custom_call" | custom-call | flops 10000000000 | bytes 100000000 | tf_op jit(solution)/shard_map/pallas_call | solution.py:507
  1.5 0.7 %collective-permute-start.2 = (bf16[11,128,128]{2,1,0:T(8,128)(2,1)S(1)}, bf16[11,128,128]{2,1,0:T(8,128)(2,1)S(1)}, u32[]{:S(2)}, u32[]{:S(2)}) collective-permute-start(bf16[11,128,128]{2,1,0:T(8,128)(2,1)S(1)} %get-tuple-element.21), channel_id=1, source_target_pairs={{0,1},{2,3},{4,5},{6,7},{8,9},{10,11},{12,13},{14,15},{1,0},{3,2},... | collective-permute-start | bytes 1081352 | tf_op jit(solution)/shard_map/ppermute | solution.py:486
  2.2 3.3 %collective-permute-start.1 = (bf16[11,128,128]{2,1,0:T(8,128)(2,1)S(1)}, bf16[11,128,128]{2,1,0:T(8,128)(2,1)S(1)}, u32[]{:S(2)}, u32[]{:S(2)}) collective-permute-start(bf16[11,128,128]{2,1,0:T(8,128)(2,1)S(1)} %get-tuple-element.20), channel_id=1, source_target_pairs={{1,2},{3,4},{5,6},{7,8},{9,10},{11,12},{13,14},{2,1},{4,3},{6,5},{... | collective-permute-start | bytes 1081352 | tf_op jit(solution)/shard_map/ppermute | solution.py:492
  5.5 0.0 copy-done
  5.5 0.0 copy-done.1
  5.5 0.0 copy-done.2
  5.5 0.0 copy-done.3
  5.5 2.2 %shard_map.74 = (f32[95,128,128]{2,1,0:T(8,128)S(1)}, bf16[7,128,128]{2,1,0:T(8,128)(2,1)S(1)}) custom-call(s32[163]{0:T(256)S(4)} %get-tuple-element.17.meta_ref, bf16[72,128,128]{2,1,0:T(8,128)(2,1)S(1)} %bitcast.4, bf16[12,4,128,256]{3,2,1,0:T(8,128)(2,1)S(1)} %copy-done, bf16[12,256,256]{2,1,0:T(8,128)(2,1)S(1)} %copy-done.1, ...), custom_call_target="tpu_custom_call", output_to_operand_aliasing={{0}: (5, {})} | custom-call | tf_op jit(solution)/shard_map/pallas_call | solution.py:524
  7.8 0.0 collective-permute-done.2.halo_ref
  7.8 1.7 %shard_map.75 = (f32[95,128,128]{2,1,0:T(8,128)S(1)}, bf16[11,128,128]{2,1,0:T(8,128)(2,1)S(1)}) custom-call(s32[163]{0:T(256)S(4)} %get-tuple-element.17.meta_ref, bf16[11,128,128]{2,1,0:T(8,128)(2,1)S(1)} %collective-permute-done.2.halo_ref, bf16[72,128,128]{2,1,0:T(8,128)(2,1)S(1)} %bitcast.5, ...), custom_call_target="tpu_custom_call", output_to_operand_aliasing={{0}: (6, {})} | custom-call | tf_op jit(solution)/shard_map/pallas_call | solution.py:534
  9.6 0.3 %collective-permute-start.4 = (bf16[11,128,128]{2,1,0:T(8,128)(2,1)S(1)}, bf16[11,128,128]{2,1,0:T(8,128)(2,1)S(1)}, u32[]{:S(2)}, u32[]{:S(2)}) collective-permute-start(bf16[11,128,128]{2,1,0:T(8,128)(2,1)S(1)} %get-tuple-element.25), channel_id=1, source_target_pairs={{0,1},{2,3},{4,5},{6,7},{8,9},{10,11},{12,13},{14,15},{1,0},{3,2},... | collective-permute-start | bytes 1081352 | tf_op jit(solution)/shard_map/ppermute | solution.py:486
  9.9 3.7 %collective-permute-start = (bf16[7,128,128]{2,1,0:T(8,128)(2,1)S(1)}, bf16[7,128,128]{2,1,0:T(8,128)(2,1)S(1)}, u32[]{:S(2)}, u32[]{:S(2)}) collective-permute-start(bf16[7,128,128]{2,1,0:T(8,128)(2,1)S(1)} %get-tuple-element.19), channel_id=1, source_target_pairs={{1,2},{3,4},{5,6},{7,8},{9,10},{11,12},{13,14},{2,1},{4,3},{6,5},{... | collective-permute-start | bytes 688136 | tf_op jit(solution)/shard_map/ppermute | solution.py:492
  13.6 1.4 %collective-permute-done.1.halo_ref = bf16[11,128,128]{2,1,0:T(8,128)(2,1)S(1)} collective-permute-done((bf16[11,128,128]{2,1,0:T(8,128)(2,1)S(1)}, bf16[11,128,128]{2,1,0:T(8,128)(2,1)S(1)}, u32[]{:S(2)}, u32[]{:S(2)}) %collective-permute-start.1) | collective-permute-done | bytes 360480 | tf_op jit(solution)/shard_map/ppermute | solution.py:492
  14.9 1.7 %shard_map.76 = (f32[95,128,128]{2,1,0:T(8,128)S(1)}, bf16[4,128,128]{2,1,0:T(8,128)(2,1)S(1)}) custom-call(s32[163]{0:T(256)S(4)} %get-tuple-element.17.meta_ref, bf16[11,128,128]{2,1,0:T(8,128)(2,1)S(1)} %collective-permute-done.1.halo_ref, bf16[12,4,128,256]{3,2,1,0:T(8,128)(2,1)S(1)} %copy-done, ...), custom_call_target="tpu_custom_call", output_to_operand_aliasing={{0}: (5, {})} | custom-call | tf_op jit(solution)/shard_map/pallas_call | solution.py:544
  16.7 2.9 %collective-permute-start.3 = (bf16[4,128,128]{2,1,0:T(8,128)(2,1)S(1)}, bf16[4,128,128]{2,1,0:T(8,128)(2,1)S(1)}, u32[]{:S(2)}, u32[]{:S(2)}) collective-permute-start(bf16[4,128,128]{2,1,0:T(8,128)(2,1)S(1)} %get-tuple-element.24), channel_id=1, source_target_pairs={{1,2},{3,4},{5,6},{7,8},{9,10},{11,12},{13,14},{2,1},{4,3},{6,5},{... | collective-permute-start | bytes 393224 | tf_op jit(solution)/shard_map/ppermute | solution.py:492
  19.6 0.0 collective-permute-done.4.first_ref
  19.6 4.9 %shard_map.77 = (f32[95,128,128]{2,1,0:T(8,128)S(1)}, f32[72,128,128]{2,1,0:T(8,128)}) custom-call(s32[163]{0:T(256)S(4)} %get-tuple-element.17.meta_ref, bf16[11,128,128]{2,1,0:T(8,128)(2,1)S(1)} %collective-permute-done.4.first_ref, bf16[72,128,128]{2,1,0:T(8,128)(2,1)S(1)} %bitcast.6, ...), custom_call_target="tpu_custom_call", output_to_operand_aliasing={{0}: (6, {})} | custom-call | tf_op jit(solution)/shard_map/pallas_call | solution.py:555
  24.5 0.0 collective-permute-done.early_ref
  24.5 0.0 collective-permute-done.3.late_ref
  24.6 0.9 %shard_map.78 = f32[72,128,128]{2,1,0:T(8,128)} custom-call(s32[163]{0:T(256)S(4)} %get-tuple-element.17.meta_ref, bf16[7,128,128]{2,1,0:T(8,128)(2,1)S(1)} %collective-permute-done.early_ref, bf16[4,128,128]{2,1,0:T(8,128)(2,1)S(1)} %collective-permute-done.3.late_ref, ...), custom_call_target="tpu_custom_call", output_to_operand_aliasing={{}: (4, {})} | custom-call | tf_op jit(solution)/shard_map/pallas_call | solution.py:565
Async XLA Ops:
  0.0 5.5 %copy-start = (bf16[12,4,128,256]{3,2,1,0:T(8,128)(2,1)S(1)}, bf16[12,4,128,256]{3,2,1,0:T(8,128)(2,1)}, u32[]{:S(2)}) copy-start(bf16[12,4,128,256]{3,2,1,0:T(8,128)(2,1)} %ao_ref.7) | copy-start | bytes 9437188
  0.0 5.5 %copy-start.1 = (bf16[12,256,256]{2,1,0:T(8,128)(2,1)S(1)}, bf16[12,256,256]{2,1,0:T(8,128)(2,1)}, u32[]{:S(2)}) copy-start(bf16[12,256,256]{2,1,0:T(8,128)(2,1)} %kernel_ref.7) | copy-start | bytes 4718596
  0.0 5.5 %copy-start.2 = (bf16[8,9,128,128]{3,2,1,0:T(8,128)(2,1)S(1)}, bf16[8,9,128,128]{3,2,1,0:T(8,128)(2,1)}, u32[]{:S(2)}) copy-start(bf16[8,9,128,128]{3,2,1,0:T(8,128)(2,1)} %param.7) | copy-start | bytes 7077892
  0.0 5.5 %copy-start.3 = (f32[12,256]{1,0:T(8,128)S(1)}, f32[12,256]{1,0:T(8,128)}, u32[]{:S(2)}) copy-start(f32[12,256]{1,0:T(8,128)} %weights_ref.7) | copy-start | bytes 36868
  1.5 6.4 %collective-permute-start.2 = (bf16[11,128,128]{2,1,0:T(8,128)(2,1)S(1)}, bf16[11,128,128]{2,1,0:T(8,128)(2,1)S(1)}, u32[]{:S(2)}, u32[]{:S(2)}) collective-permute-start(bf16[11,128,128]{2,1,0:T(8,128)(2,1)S(1)} %get-tuple-element.21), channel_id=1, source_target_pairs={{0,1},{2,3},{4,5},{6,7},{8,9},{10,11},{12,13},{14,15},{1,0},{3,2},... | collective-permute-start | bytes 1081352 | tf_op jit(solution)/shard_map/ppermute | solution.py:486
  2.2 12.7 %collective-permute-start.1 = (bf16[11,128,128]{2,1,0:T(8,128)(2,1)S(1)}, bf16[11,128,128]{2,1,0:T(8,128)(2,1)S(1)}, u32[]{:S(2)}, u32[]{:S(2)}) collective-permute-start(bf16[11,128,128]{2,1,0:T(8,128)(2,1)S(1)} %get-tuple-element.20), channel_id=1, source_target_pairs={{1,2},{3,4},{5,6},{7,8},{9,10},{11,12},{13,14},{2,1},{4,3},{6,5},{... | collective-permute-start | bytes 1081352 | tf_op jit(solution)/shard_map/ppermute | solution.py:492
  9.6 10.1 %collective-permute-start.4 = (bf16[11,128,128]{2,1,0:T(8,128)(2,1)S(1)}, bf16[11,128,128]{2,1,0:T(8,128)(2,1)S(1)}, u32[]{:S(2)}, u32[]{:S(2)}) collective-permute-start(bf16[11,128,128]{2,1,0:T(8,128)(2,1)S(1)} %get-tuple-element.25), channel_id=1, source_target_pairs={{0,1},{2,3},{4,5},{6,7},{8,9},{10,11},{12,13},{14,15},{1,0},{3,2},... | collective-permute-start | bytes 1081352 | tf_op jit(solution)/shard_map/ppermute | solution.py:486
  9.9 14.7 %collective-permute-start = (bf16[7,128,128]{2,1,0:T(8,128)(2,1)S(1)}, bf16[7,128,128]{2,1,0:T(8,128)(2,1)S(1)}, u32[]{:S(2)}, u32[]{:S(2)}) collective-permute-start(bf16[7,128,128]{2,1,0:T(8,128)(2,1)S(1)} %get-tuple-element.19), channel_id=1, source_target_pairs={{1,2},{3,4},{5,6},{7,8},{9,10},{11,12},{13,14},{2,1},{4,3},{6,5},{... | collective-permute-start | bytes 688136 | tf_op jit(solution)/shard_map/ppermute | solution.py:492
  16.7 7.9 %collective-permute-start.3 = (bf16[4,128,128]{2,1,0:T(8,128)(2,1)S(1)}, bf16[4,128,128]{2,1,0:T(8,128)(2,1)S(1)}, u32[]{:S(2)}, u32[]{:S(2)}) collective-permute-start(bf16[4,128,128]{2,1,0:T(8,128)(2,1)S(1)} %get-tuple-element.24), channel_id=1, source_target_pairs={{1,2},{3,4},{5,6},{7,8},{9,10},{11,12},{13,14},{2,1},{4,3},{6,5},{... | collective-permute-start | bytes 393224 | tf_op jit(solution)/shard_map/ppermute | solution.py:492
where the time goes:
time: 25.5 us
  Pallas kernels  13 us (51%)
  starting transfers between devices  11 us (43%)
  waiting for transfers between devices  1.36 us (5%)
    ppermute x3, starting transfers between devices, to_second(): got = lax.ppermute(x, 'blk', pairs + [(j, i) for i, j in pairs])  9.94 us
    pallas_call x1, Pallas kernels, local(): call(functools.partial(inner_kernel, geo), (acc_type, whole), [SMEM_SPEC]...  4.92 us
    pallas_call x1, Pallas kernels, local(): call(functools.partial(early_kernel, geo), (acc_type, pack(geo.early)), [...  2.25 us
    pallas_call x1, Pallas kernels, local(): call(functools.partial(late_kernel, geo), (acc_type, pack(geo.late)), [SM...  1.75 us
    pallas_call x1, Pallas kernels, local(): call(functools.partial(near_kernel, geo), (acc_type, pack(geo.halo)), [SM...  1.73 us
    pallas_call x1, Pallas kernels, local(): call(functools.partial(pack_kernel, geo), (pack(geo.halo),) * 2 + (pltpu....  1.43 us
    ppermute x3, waiting for transfers between devices, to_second(): got = lax.ppermute(x, 'blk', pairs + [(j, i) for i, j in pairs])  1.36 us
    ppermute x2, starting transfers between devices, to_first(): got = lax.ppermute(x, 'blk', pairs + [(j, i) for i, j in pairs])  1.04 us
  transfers between devices with their start and end apart: 5, of which 1 were waited for; matrix products, arithmetic and copies ran while one was open for 0% of the time, Pallas kernels for 42%

commit v1 on v0

--- a/solution.py
+++ b/solution.py
@@ -9,7 +9,8 @@
 
 MIB = 1 << 20
 GROUP = 2
-LISTS = 6
+LATE_GROUP = 4
+LISTS = 7
 BUDGET = 43
 COST = (10, 7)
 SMEM_SPEC = pl.BlockSpec(memory_space=pltpu.SMEM)
@@ -40,16 +41,18 @@
         self.late = self.halo - self.early
         self.first_at = self.own
         self.early_at = self.own + self.halo
-        self.late_at = self.early_at + self.early
-        self.spare = self.late_at + self.late
+        self.spare = self.early_at + self.early
         self.halo_base = self.bases((low, high))
         self.early_base = self.bases(early)
-        self.late_base = self.bases(late)
         shifts = (rows, -rows)
         self.packs = [self.places(*pair) for pair in zip((low, high), shifts)]
         self.early_packs = [self.places(*pair) for pair in zip(early, shifts)]
         self.late_packs = [self.places(*pair) for pair in zip(late, shifts)]
-        self.quiet = [self.others(self.packs[1 - near]) for near in range(2)]
+        self.span = min(2 * reach, rows) * band
+        self.quiet = [
+            self.others(self.packs[1], 0, self.span),
+            self.others(self.packs[0], self.own - self.span, self.own),
+        ]
         self.list_size = batches + 2
         self.lengths_at = LISTS * self.list_size
         self.local_at = self.lengths_at + LISTS
@@ -74,12 +77,12 @@
             place += stop - start
         return pack
 
-    def others(self, pack):
+    def others(self, pack, begin, end):
         touched = set()
         for start, _, count in pack:
             touched.update(range(start, start + count))
         runs = []
-        for index in range(self.own):
+        for index in range(begin, end):
             if index in touched:
                 continue
             if runs and sum(runs[-1]) == index:
@@ -112,7 +115,7 @@
         body(second, first)
 
 
-CROSS_MANY, CROSS_FEW, NEAR_MANY, NEAR_FEW, INNER_MANY, INNER_FEW = range(LISTS)
+CROSS_MANY, CROSS_FEW, NEAR_MANY, NEAR_FEW, INNER_MANY, INNER_FEW, CROSS = range(LISTS)
 
 
 def build_lists(geo, index, centre_ref, offsets_ref, counts_ref, meta_ref):
@@ -138,7 +141,7 @@
         many = count > 2
         few = (count > 0) & jnp.logical_not(many)
         kinds = [kind & size for kind in (cross, near, inner) for size in (many, few)]
-        for which, member in enumerate(kinds):
+        for which, member in enumerate(kinds + [cross]):
             meta_ref[which * geo.list_size + lengths[which]] = b
             lengths[which] = lengths[which] + member.astype(jnp.int32)
     for which in range(LISTS):
@@ -147,9 +150,7 @@
 
 
 def zone(geo, odd, cross):
-    span = min(2 * geo.reach, geo.rows) * geo.band
-    if not cross:
-        span = geo.own - span
+    span = geo.span if cross else geo.own - geo.span
     return pl.ds(jnp.where(odd == cross, geo.own - span, 0), span)
 
 
@@ -183,7 +184,7 @@
     ]
     for copy in scalars:
         copy.start()
-    for where in (zone(geo, odd, False), pl.ds(geo.first_at, geo.halo), pl.ds(geo.late_at, geo.late)):
+    for where in (zone(geo, odd, False), pl.ds(geo.first_at, geo.halo)):
         acc_ref[where] = jnp.zeros_like(acc_ref[where])
     for copy in scalars:
         copy.wait()
@@ -209,20 +210,20 @@
     return share
 
 
-def each_group(geo, meta_ref, which, body, begin=0, end=None):
+def each_group(geo, meta_ref, which, body, size=GROUP, begin=0, end=None):
     length = meta_ref[geo.lengths_at + which]
 
     def step(i, carry):
         chosen = []
-        for n in range(GROUP):
-            place = i * GROUP + n
+        for n in range(size):
+            place = i * size + n
             there = place < length
             b = meta_ref[which * geo.list_size + jnp.minimum(place, length)]
             chosen.append((jnp.where(there, b, 0), there))
         body(chosen)
         return carry
 
-    lax.fori_loop(begin, group_count(geo, meta_ref, which) if end is None else end, step, 0)
+    lax.fori_loop(begin, (length + size - 1) // size if end is None else end, step, 0)
 
 
 class Slots:
@@ -253,19 +254,24 @@
     )
 
 
-def chain(xs, tiles, batches, kernel_ref, weights_ref):
+def potentials(xs, tiles, batches, kernel_ref):
     fs = [
         jnp.dot(t, x, preferred_element_type=jnp.float32).astype(jnp.bfloat16)
         for t, x in zip(tiles, xs)
     ]
-    gs = [
+    return [
         jnp.dot(f, kernel_ref[b], preferred_element_type=jnp.float32) for f, b in zip(fs, batches)
     ]
+
+
+def outer_product(x, h):
+    return lax.dot_general(x, h, (((1,), (1,)), ((), ())), preferred_element_type=jnp.float32)
+
+
+def chain(xs, tiles, batches, kernel_ref, weights_ref):
+    gs = potentials(xs, tiles, batches, kernel_ref)
     hs = [(g * weights_ref[pl.ds(b, 1), :]).astype(jnp.bfloat16) for g, b in zip(gs, batches)]
-    return [
-        lax.dot_general(x, h, (((1,), (1,)), ((), ())), preferred_element_type=jnp.float32)
-        for x, h in zip(xs, hs)
-    ]
+    return [outer_product(x, h) for x, h in zip(xs, hs)]
 
 
 def scatter(part, target, nb, acc_ref):
@@ -334,40 +340,78 @@
         scatter(part, target, ao_ref.shape[2], acc_ref)
 
 
-def add_halo(geo, chosen, width, meta_ref, halo_ref, ao_ref, kernel_ref, weights_ref, acc_ref):
-    outer = min(geo.reach, width)
-    xs, tiles, targets = ([], [], [])
+def halo_rows(geo, meta_ref, slots):
+    odd = meta_ref[geo.odd_at] == 1
+    rows, places, present = ([], [], [])
+    for i in range(geo.reach):
+        row = jnp.where(odd, geo.rows + i, i - geo.reach)
+        place, found = (jnp.int32(0), jnp.bool_(False))
+        for k in range(slots.width):
+            hit = slots.live[k] & (slots.row[k] == row)
+            place = jnp.where(hit, k, place)
+            found = found | hit
+        rows.append(row)
+        places.append(place)
+        present.append(found)
+    return rows, places, present
+
+
+def add_corner(geo, chosen, meta_ref, halo_ref, ao_ref, kernel_ref, weights_ref, h_ref, total_ref):
+    nb = ao_ref.shape[2]
+    factor = lambda flag: jnp.where(flag, 1.0, 0.0)
+    xs, sides, tiles, masks = ([], [], [], [])
+    for b, there in chosen:
+        slots = Slots(geo, meta_ref, b, there, geo.slots)
+        rows, places, present = halo_rows(geo, meta_ref, slots)
+        xs.append(panels(slots, ao_ref, b))
+        sides.append(
+            jnp.concatenate(
+                [
+                    ao_ref[b, place] * factor(found).astype(ao_ref.dtype)
+                    for place, found in zip(places, present)
+                ],
+                axis=0,
+            )
+        )
+        picked = []
+        for row, found in zip(rows, present):
+            base = geo.pick(geo.halo_base, 0, row, 0) - row + geo.half
+            picked.append([jnp.where(found, base + column, 0) for column in slots.row])
+        tiles.append(gathered(halo_ref, picked))
+        masks.append([factor(found) for found in present])
+    gs = potentials(xs, tiles, [b for b, _ in chosen], kernel_ref)
+    hs = []
+    for g, mask, (b, there) in zip(gs, masks, chosen):
+        weights = weights_ref[pl.ds(b, 1), :]
+        h = jnp.concatenate(
+            [g[i * nb : (i + 1) * nb] * (weights * mask[i]) for i in range(geo.reach)], axis=0
+        ).astype(jnp.bfloat16)
+        h_ref[jnp.where(there, b, geo.batches)] = h
+        hs.append(h)
+    total_ref[...] += outer_product(
+        jnp.concatenate(sides, axis=1), jnp.concatenate(hs, axis=1)
+    )
+
+
+def add_columns(geo, chosen, width, meta_ref, ao_ref, h_ref, acc_ref):
+    parts, targets = ([], [])
     for b, there in chosen:
         slots = Slots(geo, meta_ref, b, there, width)
-        xs.append(panels(slots, ao_ref, b))
-        found = jnp.int32(0)
-        picked = [jnp.int32(0)] * outer
-        for k in range(width):
-            away = slots.live[k] & jnp.logical_not(slots.own[k])
-            for i in range(outer):
-                picked[i] = jnp.where(away & (found <= i), slots.offset[k], picked[i])
-            found = found + away.astype(jnp.int32)
-        places, target = ([], [[None] * outer for _ in range(width)])
-        for i in range(outer):
-            base = geo.pick(geo.halo_base, 0, slots.local + picked[i], 0)
-            places.append(
+        rows, _, present = halo_rows(geo, meta_ref, slots)
+        parts.append(outer_product(ao_ref[b, pl.ds(0, width)].reshape(-1, ao_ref.shape[3]), h_ref[b]))
+        targets.append(
+            [
                 [
-                    jnp.where(there, base + slots.offset[j] - picked[i] + geo.half, 0)
-                    for j in range(width)
+                    jnp.where(
+                        slots.live[k] & slots.own[k] & found,
+                        slots.row[k] * geo.band + row - slots.row[k] + geo.half,
+                        geo.spare,
+                    )
+                    for row, found in zip(rows, present)
                 ]
-            )
-        for k in range(width):
-            row = slots.row[k]
-            base = geo.pick(geo.late_base, geo.late_at, row, row * geo.band)
-            for i in range(outer):
-                target[k][i] = jnp.where(
-                    slots.live[k] & (i < found),
-                    base + picked[i] - slots.offset[k] + geo.half,
-                    geo.spare,
-                )
-        tiles.append(gathered(halo_ref, places))
-        targets.append(target)
-    parts = chain(xs, tiles, [b for b, _ in chosen], kernel_ref, weights_ref)
+                for k in range(width)
+            ]
+        )
     for part, target in zip(parts, targets):
         scatter(part, target, ao_ref.shape[2], acc_ref)
 
@@ -407,20 +451,31 @@
 
 
 def late_kernel(
-    geo, meta_ref, halo_ref, ao_ref, kernel_ref, weights_ref, acc_in, acc_ref, late_out
+    geo, meta_ref, halo_ref, ao_ref, kernel_ref, weights_ref, h_ref, late_out, total_ref
 ):
-    refs = (meta_ref, halo_ref, ao_ref, kernel_ref, weights_ref, acc_ref)
-    for which, width in ((CROSS_MANY, geo.slots), (CROSS_FEW, 2)):
-        each_group(
-            geo, meta_ref, which, lambda chosen, width=width: add_halo(geo, chosen, width, *refs)
-        )
-    late_out[...] = acc_ref[pl.ds(geo.late_at, geo.late)].astype(late_out.dtype)
+    nb = ao_ref.shape[2]
+    total_ref[...] = jnp.zeros_like(total_ref)
+
+    def work(chosen):
+        add_corner(
+            geo, chosen, meta_ref, halo_ref, ao_ref, kernel_ref, weights_ref, h_ref, total_ref
+        )
+
+    groups = (meta_ref[geo.lengths_at + CROSS] + 1) // LATE_GROUP
+    each_group(geo, meta_ref, CROSS, work, size=LATE_GROUP, end=groups)
+    each_group(geo, meta_ref, CROSS, work, size=LATE_GROUP // 2, begin=2 * groups)
+    for i in range(geo.reach):
+        for j in range(geo.reach):
+            late_out[i * geo.reach + j] = total_ref[
+                i * nb : (i + 1) * nb, j * nb : (j + 1) * nb
+            ].astype(late_out.dtype)
 
 
 def inner_kernel(
-    geo, meta_ref, first_ref, tiles_ref, ao_ref, kernel_ref, weights_ref, acc_in,
+    geo, meta_ref, first_ref, tiles_ref, ao_ref, kernel_ref, weights_ref, h_ref, acc_in,
     acc_ref, out_ref, sems,
 ):
+    odd = meta_ref[geo.odd_at] == 1
     refs = (meta_ref, tiles_ref, ao_ref, kernel_ref, weights_ref, acc_ref)
     share = inner_share(geo, meta_ref)
     for which, width, begin in ((INNER_MANY, geo.slots, share[0]), (INNER_FEW, 2, share[1])):
@@ -432,20 +487,36 @@
             begin=begin,
         )
 
-    def finish_near(up, down):
-        near = 0 if up else 1
-        for start, place, count in geo.packs[near]:
+    def add_near(up, down):
+        for start, place, count in geo.packs[0 if up else 1]:
             acc_ref[pl.ds(start, count)] += first_ref[pl.ds(place, count)].astype(jnp.float32)
+
+    by_parity(odd, add_near, True, False)
+    done = zone(geo, odd, False)
+    copy = pltpu.make_async_copy(acc_ref.at[done], out_ref.at[done], sems.at[0])
+    copy.start()
+    for which, width in ((CROSS_MANY, geo.slots), (CROSS_FEW, 2)):
+        each_group(
+            geo,
+            meta_ref,
+            which,
+            lambda chosen, width=width: add_columns(
+                geo, chosen, width, meta_ref, ao_ref, h_ref, acc_ref
+            ),
+        )
+
+    def write_quiet(up, down):
         run_copies(
             [
                 pltpu.make_async_copy(
-                    acc_ref.at[pl.ds(start, count)], out_ref.at[pl.ds(start, count)], sems.at[i]
+                    acc_ref.at[pl.ds(start, count)], out_ref.at[pl.ds(start, count)], sems.at[1 + i]
                 )
-                for i, (start, count) in enumerate(geo.quiet[near])
+                for i, (start, count) in enumerate(geo.quiet[0 if up else 1])
             ]
         )
 
-    by_parity(meta_ref[geo.odd_at] == 1, finish_near, True, False)
+    by_parity(odd, write_quiet, True, False)
+    copy.wait()
 
 
 def finish_kernel(geo, meta_ref, early_ref, late_ref, acc_ref, out_in, out_ref, total, sems):
@@ -541,25 +612,25 @@
     )(meta, near_halo, *panel, acc)
     first = to_first(first, size)
 
-    acc, late = call(
+    h_type = pltpu.VMEM((batches + 1, geo.reach * nb, pts), jnp.bfloat16)
+    h, late = call(
         functools.partial(late_kernel, geo),
-        (acc_type, pack(geo.late)),
-        [SMEM_SPEC] + [VMEM_SPEC] * 5,
+        (h_type, pack(geo.late)),
+        [SMEM_SPEC] + [VMEM_SPEC] * 4,
         (VMEM_SPEC,) * 2,
-        [],
-        {5: 0},
-    )(meta, cross_halo, *panel[1:], acc)
+        [pltpu.VMEM((geo.reach * nb, geo.reach * nb), jnp.float32)],
+    )(meta, cross_halo, *panel[1:])
     late = to_second(late, size)
 
     whole = jax.ShapeDtypeStruct((geo.own, nb, nb), jnp.float32)
     acc, out = call(
         functools.partial(inner_kernel, geo),
         (acc_type, whole),
-        [SMEM_SPEC] + [VMEM_SPEC] * 6,
+        [SMEM_SPEC] + [VMEM_SPEC] * 7,
         (VMEM_SPEC, ANY_SPEC),
-        [dma((max(len(runs) for runs in geo.quiet),))],
-        {6: 0},
-    )(meta, first, *panel, acc)
+        [dma((1 + max(len(runs) for runs in geo.quiet),))],
+        {7: 0},
+    )(meta, first, *panel, h, acc)
 
     parts = 2 * geo.reach
     out = call(

time: 25.5 us -> 25.7 us (level)
  the two profiles are of different devices: /device:TPU:9 before, /device:TPU:1 now
where the time goes in v1:
time: 25.7 us; the launch traced here: 25.4 us
  starting transfers between devices  14.2 us (55%)
  Pallas kernels  10.8 us (42%)
    ppermute x3, starting transfers between devices, to_second(): got = lax.ppermute(x, 'blk', pairs + [(j, i) for i, j in pairs])  14 us
    pallas_call x1, Pallas kernels, local(): call(functools.partial(inner_kernel, geo), (acc_type, whole), [SMEM_SPEC]...  3.72 us
    pallas_call x1, Pallas kernels, local(): call(functools.partial(near_kernel, geo), (acc_type, pack(geo.halo)), [SM...  2.75 us
    pallas_call x1, Pallas kernels, local(): call(functools.partial(pack_kernel, geo), (pack(geo.halo),) * 2 + (pltpu....  1.43 us
    pallas_call x1, Pallas kernels, local(): call(functools.partial(early_kernel, geo), (acc_type, pack(geo.early)), [...  1.24 us
    pallas_call x1, Pallas kernels, local(): call(functools.partial(finish_kernel, geo), whole, [SMEM_SPEC] + [VMEM_SP...  0.92 us
    pallas_call x1, Pallas kernels, local(): call(functools.partial(late_kernel, geo), (h_type, pack(geo.late)), [SMEM...  0.75 us
  transfers between devices with their start and end apart: 5, of which 1 were waited for; matrix products, arithmetic and copies ran while one was open for 0% of the time, Pallas kernels for 33%

profile of v1, /device:TPU:1, one launch (start us, length us, event | category | flops | bytes accessed | tf_op | source)
XLA Modules:
  0.0 25.4 jit_solution(13225990839357947565)
XLA Ops:
  0.0 0.0 copy-start
  0.0 0.0 copy-start.1
  0.0 0.0 copy-start.2
  0.0 0.0 copy-start.3
  0.0 1.4 %shard_map.73 = (bf16[11,128,128]{2,1,0:T(8,128)(2,1)S(1)}, bf16[11,128,128]{2,1,0:T(8,128)(2,1)S(1)}, s32[178]{0:T(256)S(4)}, f32[91,128,128]{2,1,0:T(8,128)S(1)}) custom-call(bf16[72,128,128]{2,1,0:T(8,128)(2,1)} %bitcast.3, s32[12]{0:T(128)} %centre_in.1, s32[4,12]{1,0:T(4,128)} %bitcast.7, s32[12]{0:T(128)} %counts_in.1), custom_call_target="tpu_custom_call" | custom-call | flops 10000000000 | bytes 100000000 | tf_op jit(solution)/shard_map/pallas_call | solution.py:578
  1.5 0.1 collective-permute-start.3
  1.6 4.8 %collective-permute-start.1 = (bf16[11,128,128]{2,1,0:T(8,128)(2,1)S(1)}, bf16[11,128,128]{2,1,0:T(8,128)(2,1)S(1)}, u32[]{:S(2)}, u32[]{:S(2)}) collective-permute-start(bf16[11,128,128]{2,1,0:T(8,128)(2,1)S(1)} %get-tuple-element.20), channel_id=1, source_target_pairs={{1,2},{3,4},{5,6},{7,8},{9,10},{11,12},{13,14},{2,1},{4,3},{6,5},{... | collective-permute-start | bytes 1081352 | tf_op jit(solution)/shard_map/ppermute | solution.py:563
  6.3 0.0 copy-done
  6.3 0.0 copy-done.1
  6.4 0.0 copy-done.2
  6.4 0.0 copy-done.3
  6.4 1.2 %shard_map.74 = (f32[91,128,128]{2,1,0:T(8,128)S(1)}, bf16[7,128,128]{2,1,0:T(8,128)(2,1)S(1)}) custom-call(s32[178]{0:T(256)S(4)} %get-tuple-element.17.meta_ref, bf16[72,128,128]{2,1,0:T(8,128)(2,1)S(1)} %bitcast.4, bf16[12,4,128,256]{3,2,1,0:T(8,128)(2,1)S(1)} %copy-done, bf16[12,256,256]{2,1,0:T(8,128)(2,1)S(1)} %copy-done.1, ...), custom_call_target="tpu_custom_call", output_to_operand_aliasing={{0}: (5, {})} | custom-call | tf_op jit(solution)/shard_map/pallas_call | solution.py:595
  7.6 0.0 collective-permute-done.3.halo_ref
  7.6 2.7 %shard_map.76 = (f32[91,128,128]{2,1,0:T(8,128)S(1)}, bf16[11,128,128]{2,1,0:T(8,128)(2,1)S(1)}) custom-call(s32[178]{0:T(256)S(4)} %get-tuple-element.17.meta_ref, bf16[11,128,128]{2,1,0:T(8,128)(2,1)S(1)} %collective-permute-done.3.halo_ref, bf16[72,128,128]{2,1,0:T(8,128)(2,1)S(1)} %bitcast.5, ...), custom_call_target="tpu_custom_call", output_to_operand_aliasing={{0}: (6, {})} | custom-call | tf_op jit(solution)/shard_map/pallas_call | solution.py:605
  10.4 0.1 collective-permute-start.4
  10.5 3.9 %collective-permute-start = (bf16[7,128,128]{2,1,0:T(8,128)(2,1)S(1)}, bf16[7,128,128]{2,1,0:T(8,128)(2,1)S(1)}, u32[]{:S(2)}, u32[]{:S(2)}) collective-permute-start(bf16[7,128,128]{2,1,0:T(8,128)(2,1)S(1)} %get-tuple-element.19), channel_id=1, source_target_pairs={{1,2},{3,4},{5,6},{7,8},{9,10},{11,12},{13,14},{2,1},{4,3},{6,5},{... | collective-permute-start | bytes 688136 | tf_op jit(solution)/shard_map/ppermute | solution.py:563
  14.4 0.2 collective-permute-done.1.halo_ref
  14.6 0.7 %shard_map.75 = (bf16[13,256,256]{2,1,0:T(8,128)(2,1)S(1)}, bf16[4,128,128]{2,1,0:T(8,128)(2,1)S(1)}) custom-call(s32[178]{0:T(256)S(4)} %get-tuple-element.17.meta_ref, bf16[11,128,128]{2,1,0:T(8,128)(2,1)S(1)} %collective-permute-done.1.halo_ref, bf16[12,4,128,256]{3,2,1,0:T(8,128)(2,1)S(1)} %copy-done, bf16[12,256,256]{2,1,0:T(8,128)(2,1)S(1)} %copy-done.1, ...), custom_call_target="tpu_custom_call" | custom-call | tf_op jit(solution)/shard_map/pallas_call | solution.py:616
  15.3 5.4 %collective-permute-start.2 = (bf16[4,128,128]{2,1,0:T(8,128)(2,1)S(1)}, bf16[4,128,128]{2,1,0:T(8,128)(2,1)S(1)}, u32[]{:S(2)}, u32[]{:S(2)}) collective-permute-start(bf16[4,128,128]{2,1,0:T(8,128)(2,1)S(1)} %get-tuple-element.21), channel_id=1, source_target_pairs={{1,2},{3,4},{5,6},{7,8},{9,10},{11,12},{13,14},{2,1},{4,3},{6,5},{... | collective-permute-start | bytes 393224 | tf_op jit(solution)/shard_map/ppermute | solution.py:563
  20.7 0.0 collective-permute-done.4.first_ref
  20.7 3.7 %shard_map.77 = (f32[91,128,128]{2,1,0:T(8,128)S(1)}, f32[72,128,128]{2,1,0:T(8,128)}) custom-call(s32[178]{0:T(256)S(4)} %get-tuple-element.17.meta_ref, bf16[11,128,128]{2,1,0:T(8,128)(2,1)S(1)} %collective-permute-done.4.first_ref, bf16[72,128,128]{2,1,0:T(8,128)(2,1)S(1)} %bitcast.6, ...), custom_call_target="tpu_custom_call", output_to_operand_aliasing={{0}: (7, {})} | custom-call | tf_op jit(solution)/shard_map/pallas_call | solution.py:626
  24.4 0.0 collective-permute-done.early_ref
  24.4 0.0 collective-permute-done.2.late_ref
  24.4 0.9 %shard_map.78 = f32[72,128,128]{2,1,0:T(8,128)} custom-call(s32[178]{0:T(256)S(4)} %get-tuple-element.17.meta_ref, bf16[7,128,128]{2,1,0:T(8,128)(2,1)S(1)} %collective-permute-done.early_ref, bf16[4,128,128]{2,1,0:T(8,128)(2,1)S(1)} %collective-permute-done.2.late_ref, ...), custom_call_target="tpu_custom_call", output_to_operand_aliasing={{}: (4, {})} | custom-call | tf_op jit(solution)/shard_map/pallas_call | solution.py:636
Async XLA Ops:
  0.0 6.3 %copy-start = (bf16[12,4,128,256]{3,2,1,0:T(8,128)(2,1)S(1)}, bf16[12,4,128,256]{3,2,1,0:T(8,128)(2,1)}, u32[]{:S(2)}) copy-start(bf16[12,4,128,256]{3,2,1,0:T(8,128)(2,1)} %ao_ref.7) | copy-start | bytes 9437188
  0.0 6.3 %copy-start.1 = (bf16[12,256,256]{2,1,0:T(8,128)(2,1)S(1)}, bf16[12,256,256]{2,1,0:T(8,128)(2,1)}, u32[]{:S(2)}) copy-start(bf16[12,256,256]{2,1,0:T(8,128)(2,1)} %kernel_ref.7) | copy-start | bytes 4718596
  0.0 6.4 %copy-start.2 = (bf16[8,9,128,128]{3,2,1,0:T(8,128)(2,1)S(1)}, bf16[8,9,128,128]{3,2,1,0:T(8,128)(2,1)}, u32[]{:S(2)}) copy-start(bf16[8,9,128,128]{3,2,1,0:T(8,128)(2,1)} %param.7) | copy-start | bytes 7077892
  0.0 6.4 %copy-start.3 = (f32[12,256]{1,0:T(8,128)S(1)}, f32[12,256]{1,0:T(8,128)}, u32[]{:S(2)}) copy-start(f32[12,256]{1,0:T(8,128)} %weights_ref.7) | copy-start | bytes 36868
  1.5 6.2 %collective-permute-start.3 = (bf16[11,128,128]{2,1,0:T(8,128)(2,1)S(1)}, bf16[11,128,128]{2,1,0:T(8,128)(2,1)S(1)}, u32[]{:S(2)}, u32[]{:S(2)}) collective-permute-start(bf16[11,128,128]{2,1,0:T(8,128)(2,1)S(1)} %get-tuple-element.22), channel_id=1, source_target_pairs={{0,1},{2,3},{4,5},{6,7},{8,9},{10,11},{12,13},{14,15},{1,0},{3,2},... | collective-permute-start | bytes 1081352 | tf_op jit(solution)/shard_map/ppermute | solution.py:557
  1.6 13.0 %collective-permute-start.1 = (bf16[11,128,128]{2,1,0:T(8,128)(2,1)S(1)}, bf16[11,128,128]{2,1,0:T(8,128)(2,1)S(1)}, u32[]{:S(2)}, u32[]{:S(2)}) collective-permute-start(bf16[11,128,128]{2,1,0:T(8,128)(2,1)S(1)} %get-tuple-element.20), channel_id=1, source_target_pairs={{1,2},{3,4},{5,6},{7,8},{9,10},{11,12},{13,14},{2,1},{4,3},{6,5},{... | collective-permute-start | bytes 1081352 | tf_op jit(solution)/shard_map/ppermute | solution.py:563
  10.4 10.3 %collective-permute-start.4 = (bf16[11,128,128]{2,1,0:T(8,128)(2,1)S(1)}, bf16[11,128,128]{2,1,0:T(8,128)(2,1)S(1)}, u32[]{:S(2)}, u32[]{:S(2)}) collective-permute-start(bf16[11,128,128]{2,1,0:T(8,128)(2,1)S(1)} %get-tuple-element.24), channel_id=1, source_target_pairs={{0,1},{2,3},{4,5},{6,7},{8,9},{10,11},{12,13},{14,15},{1,0},{3,2},... | collective-permute-start | bytes 1081352 | tf_op jit(solution)/shard_map/ppermute | solution.py:557
  10.5 14.0 %collective-permute-start = (bf16[7,128,128]{2,1,0:T(8,128)(2,1)S(1)}, bf16[7,128,128]{2,1,0:T(8,128)(2,1)S(1)}, u32[]{:S(2)}, u32[]{:S(2)}) collective-permute-start(bf16[7,128,128]{2,1,0:T(8,128)(2,1)S(1)} %get-tuple-element.19), channel_id=1, source_target_pairs={{1,2},{3,4},{5,6},{7,8},{9,10},{11,12},{13,14},{2,1},{4,3},{6,5},{... | collective-permute-start | bytes 688136 | tf_op jit(solution)/shard_map/ppermute | solution.py:563
  15.3 9.1 %collective-permute-start.2 = (bf16[4,128,128]{2,1,0:T(8,128)(2,1)S(1)}, bf16[4,128,128]{2,1,0:T(8,128)(2,1)S(1)}, u32[]{:S(2)}, u32[]{:S(2)}) collective-permute-start(bf16[4,128,128]{2,1,0:T(8,128)(2,1)S(1)} %get-tuple-element.21), channel_id=1, source_target_pairs={{1,2},{3,4},{5,6},{7,8},{9,10},{11,12},{13,14},{2,1},{4,3},{6,5},{... | collective-permute-start | bytes 393224 | tf_op jit(solution)/shard_map/ppermute | solution.py:563

commit v2 on v1

--- a/solution.py
+++ b/solution.py
@@ -12,6 +12,7 @@
 LATE_GROUP = 4
 LISTS = 7
 BUDGET = 43
+EXTRA = 8
 COST = (10, 7)
 SMEM_SPEC = pl.BlockSpec(memory_space=pltpu.SMEM)
 VMEM_SPEC = pl.BlockSpec(memory_space=pltpu.VMEM)
@@ -54,12 +55,10 @@
             self.others(self.packs[0], self.own - self.span, self.own),
         ]
         self.list_size = batches + 2
-        self.lengths_at = LISTS * self.list_size
-        self.local_at = self.lengths_at + LISTS
-        self.count_at = self.local_at + batches
-        self.offsets_at = self.count_at + batches
-        self.odd_at = self.offsets_at + slots * batches
-        self.meta_size = self.odd_at + 1
+        self.lengths_at = (LISTS + 1) * self.list_size
+        self.odd_at = self.lengths_at + LISTS + 1
+        self.origin_at = self.odd_at + 1
+        self.meta_size = self.origin_at + 1
 
     def bases(self, sides):
         found = {}
@@ -118,35 +117,39 @@
 CROSS_MANY, CROSS_FEW, NEAR_MANY, NEAR_FEW, INNER_MANY, INNER_FEW, CROSS = range(LISTS)
 
 
-def build_lists(geo, index, centre_ref, offsets_ref, counts_ref, meta_ref):
+class Info:
+    def __init__(self, meta_ref, centre_ref, offsets_ref, counts_ref):
+        self.meta, self.centre, self.offsets, self.counts = meta_ref, centre_ref, offsets_ref, counts_ref
+
+
+def build_lists(geo, index, info):
+    meta = info.meta
     first = index * geo.rows
-    odd = index % 2 == 1
-    meta_ref[geo.odd_at] = odd.astype(jnp.int32)
-    lengths = [jnp.int32(0)] * LISTS
+    odd = index % 2
+    meta[geo.odd_at] = odd
+    meta[geo.origin_at] = first
+    for which in range(LISTS + 1):
+        meta[geo.lengths_at + which] = 0
+    crossing = jnp.int32(0)
     for b in range(geo.batches):
-        local = centre_ref[b] - first
-        count = counts_ref[b]
-        meta_ref[geo.local_at + b] = local
-        meta_ref[geo.count_at + b] = count
-        low = high = jnp.bool_(False)
+        local = info.centre[b] - first
+        count = info.counts[b]
+        lowest = highest = local
         for k in range(geo.slots):
-            offset = offsets_ref[k, b]
-            meta_ref[geo.offsets_at + k * geo.batches + b] = offset
-            row = local + offset
-            low = low | ((k < count) & (row < 0))
-            high = high | ((k < count) & (row >= geo.rows))
-        cross = (odd & high) | (jnp.logical_not(odd) & low)
-        near = (odd & low) | (jnp.logical_not(odd) & high)
-        inner = jnp.logical_not(low | high)
-        many = count > 2
-        few = (count > 0) & jnp.logical_not(many)
-        kinds = [kind & size for kind in (cross, near, inner) for size in (many, few)]
-        for which, member in enumerate(kinds + [cross]):
-            meta_ref[which * geo.list_size + lengths[which]] = b
-            lengths[which] = lengths[which] + member.astype(jnp.int32)
-    for which in range(LISTS):
-        meta_ref[which * geo.list_size + lengths[which]] = geo.batches
-        meta_ref[geo.lengths_at + which] = lengths[which]
+            row = jnp.where(k < count, local + info.offsets[k, b], local)
+            lowest = jnp.minimum(lowest, row)
+            highest = jnp.maximum(highest, row)
+        low, high = lowest < 0, highest >= geo.rows
+        edge = low | high
+        cross = edge & (high == (odd == 1))
+        kind = jnp.where(edge, jnp.where(cross, CROSS_MANY, NEAR_MANY), INNER_MANY)
+        which = jnp.where(count > 0, kind + (count <= 2).astype(jnp.int32), LISTS)
+        length = meta[geo.lengths_at + which]
+        meta[which * geo.list_size + length] = b
+        meta[geo.lengths_at + which] = length + 1
+        meta[CROSS * geo.list_size + crossing] = b
+        crossing = crossing + cross.astype(jnp.int32)
+    meta[geo.lengths_at + CROSS] = crossing
 
 
 def zone(geo, odd, cross):
@@ -156,8 +159,7 @@
 
 def pack_kernel(
     geo, density_ref, centre_in, offsets_in, counts_in,
-    near_ref, cross_ref, meta_ref, acc_ref,
-    centre_ref, offsets_ref, counts_ref, sems,
+    near_ref, cross_ref, meta_ref, centre_ref, offsets_ref, counts_ref, acc_ref, sems,
 ):
     index = lax.axis_index("blk")
     odd = index % 2 == 1
@@ -173,9 +175,8 @@
 
     def start(up, down):
         for copy in copies(up, down):
-            copy.start()
-
-    by_parity(odd, start, near_ref, cross_ref)
+            copy.start(priority=1)
+
     scalars = [
         pltpu.make_async_copy(*pair, sems.at[2, i])
         for i, pair in enumerate(
@@ -184,41 +185,43 @@
     ]
     for copy in scalars:
         copy.start()
+    by_parity(odd, start, near_ref, cross_ref)
+    for copy in scalars:
+        copy.wait()
+    build_lists(geo, index, Info(meta_ref, centre_ref, offsets_ref, counts_ref))
     for where in (zone(geo, odd, False), pl.ds(geo.first_at, geo.halo)):
         acc_ref[where] = jnp.zeros_like(acc_ref[where])
-    for copy in scalars:
-        copy.wait()
-    build_lists(geo, index, centre_ref, offsets_ref, counts_ref, meta_ref)
     for copy in copies(near_ref, cross_ref):
         copy.wait()
 
 
-def group_count(geo, meta_ref, which):
-    return (meta_ref[geo.lengths_at + which] + GROUP - 1) // GROUP
-
-
-def inner_share(geo, meta_ref):
-    room = BUDGET
+def group_count(geo, info, which):
+    return (info.meta[geo.lengths_at + which] + GROUP - 1) // GROUP
+
+
+def inner_share(geo, info):
+    index = info.meta[geo.origin_at] // geo.rows
+    room = BUDGET + jnp.where((index + 1) // 2 % 2 == 0, EXTRA, 0)
     for which in (CROSS_MANY, CROSS_FEW, NEAR_MANY, NEAR_FEW):
-        room = room - COST[which % 2] * group_count(geo, meta_ref, which)
+        room = room - COST[which % 2] * group_count(geo, info, which)
     share = []
     for which in (INNER_MANY, INNER_FEW):
         cost = COST[which % 2]
-        taken = jnp.minimum(jnp.maximum(room, 0) // cost, group_count(geo, meta_ref, which))
+        taken = jnp.minimum(jnp.maximum(room, 0) // cost, group_count(geo, info, which))
         room = room - cost * taken
         share.append(taken)
     return share
 
 
-def each_group(geo, meta_ref, which, body, size=GROUP, begin=0, end=None):
-    length = meta_ref[geo.lengths_at + which]
+def each_group(geo, info, which, body, size=GROUP, begin=0, end=None):
+    length = info.meta[geo.lengths_at + which]
 
     def step(i, carry):
         chosen = []
         for n in range(size):
             place = i * size + n
             there = place < length
-            b = meta_ref[which * geo.list_size + jnp.minimum(place, length)]
+            b = info.meta[which * geo.list_size + jnp.where(there, place, 0)]
             chosen.append((jnp.where(there, b, 0), there))
         body(chosen)
         return carry
@@ -227,10 +230,10 @@
 
 
 class Slots:
-    def __init__(self, geo, meta_ref, b, there, width):
-        local = meta_ref[geo.local_at + b]
-        count = jnp.where(there, meta_ref[geo.count_at + b], 0)
-        self.offset = [meta_ref[geo.offsets_at + k * geo.batches + b] for k in range(width)]
+    def __init__(self, geo, info, b, there, width):
+        local = info.centre[b] - info.meta[geo.origin_at]
+        count = jnp.where(there, info.counts[b], 0)
+        self.offset = [info.offsets[k, b] for k in range(width)]
         self.local = local
         self.row = [local + offset for offset in self.offset]
         self.live = [k < count for k in range(width)]
@@ -281,11 +284,11 @@
 
 
 def add_whole(
-    geo, chosen, width, meta_ref, tiles_ref, ao_ref, kernel_ref, weights_ref, acc_ref, halo_ref=None
+    geo, chosen, width, info, tiles_ref, ao_ref, kernel_ref, weights_ref, acc_ref, halo_ref=None
 ):
     xs, tiles, targets = ([], [], [])
     for b, there in chosen:
-        slots = Slots(geo, meta_ref, b, there, width)
+        slots = Slots(geo, info, b, there, width)
         xs.append(panels(slots, ao_ref, b))
         rows, target = ([], [])
         for k in range(width):
@@ -313,10 +316,10 @@
         scatter(part, target, ao_ref.shape[2], acc_ref)
 
 
-def add_own(geo, chosen, width, meta_ref, tiles_ref, ao_ref, kernel_ref, weights_ref, acc_ref):
+def add_own(geo, chosen, width, info, tiles_ref, ao_ref, kernel_ref, weights_ref, acc_ref):
     xs, tiles, targets = ([], [], [])
     for b, there in chosen:
-        slots = Slots(geo, meta_ref, b, there, width)
+        slots = Slots(geo, info, b, there, width)
         xs.append(panels(slots, ao_ref, b))
         places, target = ([], [])
         for k in range(width):
@@ -340,8 +343,8 @@
         scatter(part, target, ao_ref.shape[2], acc_ref)
 
 
-def halo_rows(geo, meta_ref, slots):
-    odd = meta_ref[geo.odd_at] == 1
+def halo_rows(geo, info, slots):
+    odd = info.meta[geo.odd_at] == 1
     rows, places, present = ([], [], [])
     for i in range(geo.reach):
         row = jnp.where(odd, geo.rows + i, i - geo.reach)
@@ -356,13 +359,13 @@
     return rows, places, present
 
 
-def add_corner(geo, chosen, meta_ref, halo_ref, ao_ref, kernel_ref, weights_ref, h_ref, total_ref):
+def add_corner(geo, chosen, info, halo_ref, ao_ref, kernel_ref, weights_ref, h_ref, total_ref):
     nb = ao_ref.shape[2]
     factor = lambda flag: jnp.where(flag, 1.0, 0.0)
     xs, sides, tiles, masks = ([], [], [], [])
     for b, there in chosen:
-        slots = Slots(geo, meta_ref, b, there, geo.slots)
-        rows, places, present = halo_rows(geo, meta_ref, slots)
+        slots = Slots(geo, info, b, there, geo.slots)
+        rows, places, present = halo_rows(geo, info, slots)
         xs.append(panels(slots, ao_ref, b))
         sides.append(
             jnp.concatenate(
@@ -393,11 +396,11 @@
     )
 
 
-def add_columns(geo, chosen, width, meta_ref, ao_ref, h_ref, acc_ref):
+def add_columns(geo, chosen, width, info, ao_ref, h_ref, acc_ref):
     parts, targets = ([], [])
     for b, there in chosen:
-        slots = Slots(geo, meta_ref, b, there, width)
-        rows, _, present = halo_rows(geo, meta_ref, slots)
+        slots = Slots(geo, info, b, there, width)
+        rows, _, present = halo_rows(geo, info, slots)
         parts.append(outer_product(ao_ref[b, pl.ds(0, width)].reshape(-1, ao_ref.shape[3]), h_ref[b]))
         targets.append(
             [
@@ -417,33 +420,37 @@
 
 
 def early_kernel(
-    geo, meta_ref, tiles_ref, ao_ref, kernel_ref, weights_ref, acc_in, acc_ref, early_out
+    geo, meta_ref, centre_ref, offsets_ref, counts_ref, tiles_ref, ao_ref, kernel_ref, weights_ref,
+    acc_in, acc_ref, early_out,
 ):
-    odd = meta_ref[geo.odd_at] == 1
+    info = Info(meta_ref, centre_ref, offsets_ref, counts_ref)
+    odd = info.meta[geo.odd_at] == 1
     for where in (zone(geo, odd, True), pl.ds(geo.early_at, geo.early), pl.ds(geo.spare, 1)):
         acc_ref[where] = jnp.zeros_like(acc_ref[where])
-    refs = (meta_ref, tiles_ref, ao_ref, kernel_ref, weights_ref, acc_ref)
+    refs = (info, tiles_ref, ao_ref, kernel_ref, weights_ref, acc_ref)
     for which, width in ((CROSS_MANY, geo.slots), (CROSS_FEW, 2)):
         each_group(
-            geo, meta_ref, which, lambda chosen, width=width: add_own(geo, chosen, width, *refs)
+            geo, info, which, lambda chosen, width=width: add_own(geo, chosen, width, *refs)
         )
     early_out[...] = acc_ref[pl.ds(geo.early_at, geo.early)].astype(early_out.dtype)
 
 
 def near_kernel(
-    geo, meta_ref, halo_ref, tiles_ref, ao_ref, kernel_ref, weights_ref, acc_in, acc_ref, first_out
+    geo, meta_ref, centre_ref, offsets_ref, counts_ref, halo_ref, tiles_ref, ao_ref, kernel_ref,
+    weights_ref, acc_in, acc_ref, first_out,
 ):
-    refs = (meta_ref, tiles_ref, ao_ref, kernel_ref, weights_ref, acc_ref, halo_ref)
+    info = Info(meta_ref, centre_ref, offsets_ref, counts_ref)
+    refs = (info, tiles_ref, ao_ref, kernel_ref, weights_ref, acc_ref, halo_ref)
     for which, width in ((NEAR_MANY, geo.slots), (NEAR_FEW, 2)):
         each_group(
-            geo, meta_ref, which, lambda chosen, width=width: add_whole(geo, chosen, width, *refs)
+            geo, info, which, lambda chosen, width=width: add_whole(geo, chosen, width, *refs)
         )
     first_out[...] = acc_ref[pl.ds(geo.first_at, geo.halo)].astype(first_out.dtype)
-    share = inner_share(geo, meta_ref)
+    share = inner_share(geo, info)
     for which, width, end in ((INNER_MANY, geo.slots, share[0]), (INNER_FEW, 2, share[1])):
         each_group(
             geo,
-            meta_ref,
+            info,
             which,
             lambda chosen, width=width: add_whole(geo, chosen, width, *refs[:-1]),
             end=end,
@@ -451,19 +458,21 @@
 
 
 def late_kernel(
-    geo, meta_ref, halo_ref, ao_ref, kernel_ref, weights_ref, h_ref, late_out, total_ref
+    geo, meta_ref, centre_ref, offsets_ref, counts_ref, halo_ref, ao_ref, kernel_ref, weights_ref,
+    h_ref, late_out, total_ref,
 ):
+    info = Info(meta_ref, centre_ref, offsets_ref, counts_ref)
     nb = ao_ref.shape[2]
     total_ref[...] = jnp.zeros_like(total_ref)
 
     def work(chosen):
         add_corner(
-            geo, chosen, meta_ref, halo_ref, ao_ref, kernel_ref, weights_ref, h_ref, total_ref
-        )
-
-    groups = (meta_ref[geo.lengths_at + CROSS] + 1) // LATE_GROUP
-    each_group(geo, meta_ref, CROSS, work, size=LATE_GROUP, end=groups)
-    each_group(geo, meta_ref, CROSS, work, size=LATE_GROUP // 2, begin=2 * groups)
+            geo, chosen, info, halo_ref, ao_ref, kernel_ref, weights_ref, h_ref, total_ref
+        )
+
+    groups = (info.meta[geo.lengths_at + CROSS] + 1) // LATE_GROUP
+    each_group(geo, info, CROSS, work, size=LATE_GROUP, end=groups)
+    each_group(geo, info, CROSS, work, size=LATE_GROUP // 2, begin=2 * groups)
     for i in range(geo.reach):
         for j in range(geo.reach):
             late_out[i * geo.reach + j] = total_ref[
@@ -472,16 +481,17 @@
 
 
 def inner_kernel(
-    geo, meta_ref, first_ref, tiles_ref, ao_ref, kernel_ref, weights_ref, h_ref, acc_in,
-    acc_ref, out_ref, sems,
+    geo, meta_ref, centre_ref, offsets_ref, counts_ref, first_ref, tiles_ref, ao_ref, kernel_ref,
+    weights_ref, h_ref, acc_in, acc_ref, out_ref, sems,
 ):
-    odd = meta_ref[geo.odd_at] == 1
-    refs = (meta_ref, tiles_ref, ao_ref, kernel_ref, weights_ref, acc_ref)
-    share = inner_share(geo, meta_ref)
+    info = Info(meta_ref, centre_ref, offsets_ref, counts_ref)
+    odd = info.meta[geo.odd_at] == 1
+    refs = (info, tiles_ref, ao_ref, kernel_ref, weights_ref, acc_ref)
+    share = inner_share(geo, info)
     for which, width, begin in ((INNER_MANY, geo.slots, share[0]), (INNER_FEW, 2, share[1])):
         each_group(
             geo,
-            meta_ref,
+            info,
             which,
             lambda chosen, width=width: add_whole(geo, chosen, width, *refs),
             begin=begin,
@@ -498,10 +508,10 @@
     for which, width in ((CROSS_MANY, geo.slots), (CROSS_FEW, 2)):
         each_group(
             geo,
-            meta_ref,
+            info,
             which,
             lambda chosen, width=width: add_columns(
-                geo, chosen, width, meta_ref, ao_ref, h_ref, acc_ref
+                geo, chosen, width, info, ao_ref, h_ref, acc_ref
             ),
         )
 
@@ -575,17 +585,14 @@
     dma = pltpu.SemaphoreType.DMA
     acc_type = pltpu.VMEM((geo.spare + 1, nb, nb), jnp.float32)
 
-    near_halo, cross_halo, meta, acc = call(
+    smem = lambda *shape: pltpu.SMEM(shape, jnp.int32)
+    near_halo, cross_halo, *info, acc = call(
         functools.partial(pack_kernel, geo),
-        (pack(geo.halo),) * 2 + (pltpu.SMEM((geo.meta_size,), jnp.int32), acc_type),
+        (pack(geo.halo),) * 2
+        + (smem(geo.meta_size), smem(batches), smem(slots, batches), smem(batches), acc_type),
         [ANY_SPEC] * 4,
-        (VMEM_SPEC,) * 2 + (SMEM_SPEC, VMEM_SPEC),
-        [
-            pltpu.SMEM((batches,), jnp.int32),
-            pltpu.SMEM((slots, batches), jnp.int32),
-            pltpu.SMEM((batches,), jnp.int32),
-            dma((3, max(geo.reach, 3))),
-        ],
+        (VMEM_SPEC,) * 2 + (SMEM_SPEC,) * 4 + (VMEM_SPEC,),
+        [dma((3, max(geo.reach, 3)))],
         cost=pl.CostEstimate(flops=10**10, bytes_accessed=10**8, transcendentals=0),
     )(in_hbm(tiles), in_hbm(centre), in_hbm(sig_offsets.T), in_hbm(counts))
     cross_halo = to_second(cross_halo, size)
@@ -595,42 +602,42 @@
     acc, early = call(
         functools.partial(early_kernel, geo),
         (acc_type, pack(geo.early)),
-        [SMEM_SPEC] + [VMEM_SPEC] * 5,
+        [SMEM_SPEC] * 4 + [VMEM_SPEC] * 5,
         (VMEM_SPEC,) * 2,
         [],
-        {5: 0},
-    )(meta, *panel, acc)
+        {8: 0},
+    )(*info, *panel, acc)
     early = to_second(early, size)
 
     acc, first = call(
         functools.partial(near_kernel, geo),
         (acc_type, pack(geo.halo)),
-        [SMEM_SPEC] + [VMEM_SPEC] * 6,
+        [SMEM_SPEC] * 4 + [VMEM_SPEC] * 6,
         (VMEM_SPEC,) * 2,
         [],
-        {6: 0},
-    )(meta, near_halo, *panel, acc)
+        {9: 0},
+    )(*info, near_halo, *panel, acc)
     first = to_first(first, size)
 
     h_type = pltpu.VMEM((batches + 1, geo.reach * nb, pts), jnp.bfloat16)
     h, late = call(
         functools.partial(late_kernel, geo),
         (h_type, pack(geo.late)),
-        [SMEM_SPEC] + [VMEM_SPEC] * 4,
+        [SMEM_SPEC] * 4 + [VMEM_SPEC] * 4,
         (VMEM_SPEC,) * 2,
         [pltpu.VMEM((geo.reach * nb, geo.reach * nb), jnp.float32)],
-    )(meta, cross_halo, *panel[1:])
+    )(*info, cross_halo, *panel[1:])
     late = to_second(late, size)
 
     whole = jax.ShapeDtypeStruct((geo.own, nb, nb), jnp.float32)
     acc, out = call(
         functools.partial(inner_kernel, geo),
         (acc_type, whole),
-        [SMEM_SPEC] + [VMEM_SPEC] * 7,
+        [SMEM_SPEC] * 4 + [VMEM_SPEC] * 7,
         (VMEM_SPEC, ANY_SPEC),
         [dma((1 + max(len(runs) for runs in geo.quiet),))],
-        {7: 0},
-    )(meta, first, *panel, h, acc)
+        {10: 0},
+    )(*info, first, *panel, h, acc)
 
     parts = 2 * geo.reach
     out = call(
@@ -640,7 +647,7 @@
         ANY_SPEC,
         [pltpu.VMEM((parts * band, nb, nb), jnp.float32), dma((parts,))],
         {4: 0},
-    )(meta, early, late, acc, out)
+    )(info[0], early, late, acc, out)
     return out.reshape(rows, band, nb, nb)
 
 

time: 25.7 us -> 24.8 us (0.965)
  the two profiles are of different devices: /device:TPU:1 before, /device:TPU:9 now
where the time goes in v2:
time: 24.8 us; the launch traced here: 24.4 us
  starting transfers between devices  11.9 us (48%)
  Pallas kernels  10.4 us (42%)
  waiting for transfers between devices  1.95 us (8%)
    ppermute x3, starting transfers between devices, to_second(): got = lax.ppermute(x, 'blk', pairs + [(j, i) for i, j in pairs])  9.8 us
    pallas_call x1, Pallas kernels, local(): call(functools.partial(inner_kernel, geo), (acc_type, whole), [SMEM_SPEC]...  3.36 us
    pallas_call x1, Pallas kernels, local(): call(functools.partial(near_kernel, geo), (acc_type, pack(geo.halo)), [SM...  2.74 us
    ppermute x2, starting transfers between devices, to_first(): got = lax.ppermute(x, 'blk', pairs + [(j, i) for i, j in pairs])  2.06 us
    ppermute x3, waiting for transfers between devices, to_second(): got = lax.ppermute(x, 'blk', pairs + [(j, i) for i, j in pairs])  1.95 us
    pallas_call x1, Pallas kernels, local(): call(functools.partial(pack_kernel, geo), (pack(geo.halo),) * 2 + (smem(g...  1.43 us
    pallas_call x1, Pallas kernels, local(): call(functools.partial(early_kernel, geo), (acc_type, pack(geo.early)), [...  1.23 us
    pallas_call x1, Pallas kernels, local(): call(functools.partial(finish_kernel, geo), whole, [SMEM_SPEC] + [VMEM_SP...  0.9 us
  transfers between devices with their start and end apart: 5, of which 2 were waited for; matrix products, arithmetic and copies ran while one was open for 0% of the time, Pallas kernels for 33%

profile of v2, /device:TPU:9, one launch (start us, length us, event | category | flops | bytes accessed | tf_op | source)
XLA Modules:
  0.0 24.4 jit_solution(15533554086000017005)
XLA Ops:
  0.0 0.0 copy-start
  0.0 0.0 copy-start.1
  0.0 0.0 copy-start.2
  0.0 0.0 copy-start.3
  0.0 1.4 %shard_map.73 = (bf16[11,128,128]{2,1,0:T(8,128)(2,1)S(1)}, bf16[11,128,128]{2,1,0:T(8,128)(2,1)S(1)}, s32[122]{0:T(128)S(4)}, s32[12]{0:T(128)S(4)}, s32[4,12]{...) custom-call(bf16[72,128,128]{2,1,0:T(8,128)(2,1)} %bitcast.3, s32[12]{0:T(128)} %centre_in.1, ...), custom_call_target="tpu_custom_call" | custom-call | flops 10000000000 | bytes 100000000 | tf_op jit(solution)/shard_map/pallas_call | solution.py:589
  1.5 0.7 %collective-permute-start.3 = (bf16[11,128,128]{2,1,0:T(8,128)(2,1)S(1)}, bf16[11,128,128]{2,1,0:T(8,128)(2,1)S(1)}, u32[]{:S(2)}, u32[]{:S(2)}) collective-permute-start(bf16[11,128,128]{2,1,0:T(8,128)(2,1)S(1)} %get-tuple-element.28), channel_id=1, source_target_pairs={{0,1},{2,3},{4,5},{6,7},{8,9},{10,11},{12,13},{14,15},{1,0},{3,2},... | collective-permute-start | bytes 1081352 | tf_op jit(solution)/shard_map/ppermute | solution.py:567
  2.2 3.3 %collective-permute-start.1 = (bf16[11,128,128]{2,1,0:T(8,128)(2,1)S(1)}, bf16[11,128,128]{2,1,0:T(8,128)(2,1)S(1)}, u32[]{:S(2)}, u32[]{:S(2)}) collective-permute-start(bf16[11,128,128]{2,1,0:T(8,128)(2,1)S(1)} %get-tuple-element.26), channel_id=1, source_target_pairs={{1,2},{3,4},{5,6},{7,8},{9,10},{11,12},{13,14},{2,1},{4,3},{6,5},{... | collective-permute-start | bytes 1081352 | tf_op jit(solution)/shard_map/ppermute | solution.py:573
  5.5 0.0 copy-done
  5.5 0.0 copy-done.1
  5.5 0.0 copy-done.2
  5.5 0.0 copy-done.3
  5.6 1.2 %shard_map.74 = (f32[91,128,128]{2,1,0:T(8,128)S(1)}, bf16[7,128,128]{2,1,0:T(8,128)(2,1)S(1)}) custom-call(s32[122]{0:T(128)S(4)} %get-tuple-element.20.meta_ref, s32[12]{0:T(128)S(4)} %get-tuple-element.21.centre_ref, s32[4,12]{1,0:T(4,128)S(4)} %get-tuple-element.22.offsets_ref, ...), custom_call_target="tpu_custom_call", output_to_operand_aliasing={{0}: (8, {})} | custom-call | tf_op jit(solution)/shard_map/pallas_call | solution.py:602
  6.8 0.0 collective-permute-done.3.halo_ref
  6.8 2.7 %shard_map.76 = (f32[91,128,128]{2,1,0:T(8,128)S(1)}, bf16[11,128,128]{2,1,0:T(8,128)(2,1)S(1)}) custom-call(s32[122]{0:T(128)S(4)} %get-tuple-element.20.meta_ref, s32[12]{0:T(128)S(4)} %get-tuple-element.21.centre_ref, s32[4,12]{1,0:T(4,128)S(4)} %get-tuple-element.22.offsets_ref, ...), custom_call_target="tpu_custom_call", output_to_operand_aliasing={{0}: (9, {})} | custom-call | tf_op jit(solution)/shard_map/pallas_call | solution.py:612
  9.5 1.3 %collective-permute-start.4 = (bf16[11,128,128]{2,1,0:T(8,128)(2,1)S(1)}, bf16[11,128,128]{2,1,0:T(8,128)(2,1)S(1)}, u32[]{:S(2)}, u32[]{:S(2)}) collective-permute-start(bf16[11,128,128]{2,1,0:T(8,128)(2,1)S(1)} %get-tuple-element.30), channel_id=1, source_target_pairs={{0,1},{2,3},{4,5},{6,7},{8,9},{10,11},{12,13},{14,15},{1,0},{3,2},... | collective-permute-start | bytes 1081352 | tf_op jit(solution)/shard_map/ppermute | solution.py:567
  10.9 3.3 %collective-permute-start = (bf16[7,128,128]{2,1,0:T(8,128)(2,1)S(1)}, bf16[7,128,128]{2,1,0:T(8,128)(2,1)S(1)}, u32[]{:S(2)}, u32[]{:S(2)}) collective-permute-start(bf16[7,128,128]{2,1,0:T(8,128)(2,1)S(1)} %get-tuple-element.25), channel_id=1, source_target_pairs={{1,2},{3,4},{5,6},{7,8},{9,10},{11,12},{13,14},{2,1},{4,3},{6,5},{... | collective-permute-start | bytes 688136 | tf_op jit(solution)/shard_map/ppermute | solution.py:573
  14.2 0.7 %collective-permute-done.1.halo_ref = bf16[11,128,128]{2,1,0:T(8,128)(2,1)S(1)} collective-permute-done((bf16[11,128,128]{2,1,0:T(8,128)(2,1)S(1)}, bf16[11,128,128]{2,1,0:T(8,128)(2,1)S(1)}, u32[]{:S(2)}, u32[]{:S(2)}) %collective-permute-start.1) | collective-permute-done | bytes 360480 | tf_op jit(solution)/shard_map/ppermute | solution.py:573
  14.9 0.7 %shard_map.75 = (bf16[13,256,256]{2,1,0:T(8,128)(2,1)S(1)}, bf16[4,128,128]{2,1,0:T(8,128)(2,1)S(1)}) custom-call(s32[122]{0:T(128)S(4)} %get-tuple-element.20.meta_ref, s32[12]{0:T(128)S(4)} %get-tuple-element.21.centre_ref, s32[4,12]{1,0:T(4,128)S(4)} %get-tuple-element.22.offsets_ref, s32[12]{0:T(128)S(4)} %get-tuple-element.23.counts_ref, ...), custom_call_target="tpu_custom_call" | custom-call | tf_op jit(solution)/shard_map/pallas_call | solution.py:623
  15.7 3.2 %collective-permute-start.2 = (bf16[4,128,128]{2,1,0:T(8,128)(2,1)S(1)}, bf16[4,128,128]{2,1,0:T(8,128)(2,1)S(1)}, u32[]{:S(2)}, u32[]{:S(2)}) collective-permute-start(bf16[4,128,128]{2,1,0:T(8,128)(2,1)S(1)} %get-tuple-element.27), channel_id=1, source_target_pairs={{1,2},{3,4},{5,6},{7,8},{9,10},{11,12},{13,14},{2,1},{4,3},{6,5},{... | collective-permute-start | bytes 393224 | tf_op jit(solution)/shard_map/ppermute | solution.py:573
  18.9 0.0 collective-permute-done.4.first_ref
  18.9 3.4 %shard_map.77 = (f32[91,128,128]{2,1,0:T(8,128)S(1)}, f32[72,128,128]{2,1,0:T(8,128)}) custom-call(s32[122]{0:T(128)S(4)} %get-tuple-element.20.meta_ref, s32[12]{0:T(128)S(4)} %get-tuple-element.21.centre_ref, s32[4,12]{1,0:T(4,128)S(4)} %get-tuple-element.22.offsets_ref, s32[12]{0:T(128)S(4)} %get-tuple-element.23.counts_ref, ...), custom_call_target="tpu_custom_call", output_to_operand_aliasing={{0}: (10, {})} | custom-call | tf_op jit(solution)/shard_map/pallas_call | solution.py:633
  22.3 0.0 collective-permute-done.early_ref
  22.3 1.2 %collective-permute-done.2.late_ref = bf16[4,128,128]{2,1,0:T(8,128)(2,1)S(1)} collective-permute-done((bf16[4,128,128]{2,1,0:T(8,128)(2,1)S(1)}, bf16[4,128,128]{2,1,0:T(8,128)(2,1)S(1)}, u32[]{:S(2)}, u32[]{:S(2)}) %collective-permute-start.2) | collective-permute-done | bytes 131104 | tf_op jit(solution)/shard_map/ppermute | solution.py:573
  23.5 0.9 %shard_map.78 = f32[72,128,128]{2,1,0:T(8,128)} custom-call(s32[122]{0:T(128)S(4)} %get-tuple-element.20.meta_ref, bf16[7,128,128]{2,1,0:T(8,128)(2,1)S(1)} %collective-permute-done.early_ref, bf16[4,128,128]{2,1,0:T(8,128)(2,1)S(1)} %collective-permute-done.2.late_ref, ...), custom_call_target="tpu_custom_call", output_to_operand_aliasing={{}: (4, {})} | custom-call | tf_op jit(solution)/shard_map/pallas_call | solution.py:643
Async XLA Ops:
  0.0 5.5 %copy-start = (bf16[12,4,128,256]{3,2,1,0:T(8,128)(2,1)S(1)}, bf16[12,4,128,256]{3,2,1,0:T(8,128)(2,1)}, u32[]{:S(2)}) copy-start(bf16[12,4,128,256]{3,2,1,0:T(8,128)(2,1)} %ao_ref.7) | copy-start | bytes 9437188
  0.0 5.5 %copy-start.1 = (bf16[12,256,256]{2,1,0:T(8,128)(2,1)S(1)}, bf16[12,256,256]{2,1,0:T(8,128)(2,1)}, u32[]{:S(2)}) copy-start(bf16[12,256,256]{2,1,0:T(8,128)(2,1)} %kernel_ref.7) | copy-start | bytes 4718596
  0.0 5.5 %copy-start.2 = (bf16[8,9,128,128]{3,2,1,0:T(8,128)(2,1)S(1)}, bf16[8,9,128,128]{3,2,1,0:T(8,128)(2,1)}, u32[]{:S(2)}) copy-start(bf16[8,9,128,128]{3,2,1,0:T(8,128)(2,1)} %param.7) | copy-start | bytes 7077892
  0.0 5.5 %copy-start.3 = (f32[12,256]{1,0:T(8,128)S(1)}, f32[12,256]{1,0:T(8,128)}, u32[]{:S(2)}) copy-start(f32[12,256]{1,0:T(8,128)} %weights_ref.7) | copy-start | bytes 36868
  1.5 5.3 %collective-permute-start.3 = (bf16[11,128,128]{2,1,0:T(8,128)(2,1)S(1)}, bf16[11,128,128]{2,1,0:T(8,128)(2,1)S(1)}, u32[]{:S(2)}, u32[]{:S(2)}) collective-permute-start(bf16[11,128,128]{2,1,0:T(8,128)(2,1)S(1)} %get-tuple-element.28), channel_id=1, source_target_pairs={{0,1},{2,3},{4,5},{6,7},{8,9},{10,11},{12,13},{14,15},{1,0},{3,2},... | collective-permute-start | bytes 1081352 | tf_op jit(solution)/shard_map/ppermute | solution.py:567
  2.2 12.7 %collective-permute-start.1 = (bf16[11,128,128]{2,1,0:T(8,128)(2,1)S(1)}, bf16[11,128,128]{2,1,0:T(8,128)(2,1)S(1)}, u32[]{:S(2)}, u32[]{:S(2)}) collective-permute-start(bf16[11,128,128]{2,1,0:T(8,128)(2,1)S(1)} %get-tuple-element.26), channel_id=1, source_target_pairs={{1,2},{3,4},{5,6},{7,8},{9,10},{11,12},{13,14},{2,1},{4,3},{6,5},{... | collective-permute-start | bytes 1081352 | tf_op jit(solution)/shard_map/ppermute | solution.py:573
  9.5 9.3 %collective-permute-start.4 = (bf16[11,128,128]{2,1,0:T(8,128)(2,1)S(1)}, bf16[11,128,128]{2,1,0:T(8,128)(2,1)S(1)}, u32[]{:S(2)}, u32[]{:S(2)}) collective-permute-start(bf16[11,128,128]{2,1,0:T(8,128)(2,1)S(1)} %get-tuple-element.30), channel_id=1, source_target_pairs={{0,1},{2,3},{4,5},{6,7},{8,9},{10,11},{12,13},{14,15},{1,0},{3,2},... | collective-permute-start | bytes 1081352 | tf_op jit(solution)/shard_map/ppermute | solution.py:567
  10.9 11.4 %collective-permute-start = (bf16[7,128,128]{2,1,0:T(8,128)(2,1)S(1)}, bf16[7,128,128]{2,1,0:T(8,128)(2,1)S(1)}, u32[]{:S(2)}, u32[]{:S(2)}) collective-permute-start(bf16[7,128,128]{2,1,0:T(8,128)(2,1)S(1)} %get-tuple-element.25), channel_id=1, source_target_pairs={{1,2},{3,4},{5,6},{7,8},{9,10},{11,12},{13,14},{2,1},{4,3},{6,5},{... | collective-permute-start | bytes 688136 | tf_op jit(solution)/shard_map/ppermute | solution.py:573
  15.7 7.8 %collective-permute-start.2 = (bf16[4,128,128]{2,1,0:T(8,128)(2,1)S(1)}, bf16[4,128,128]{2,1,0:T(8,128)(2,1)S(1)}, u32[]{:S(2)}, u32[]{:S(2)}) collective-permute-start(bf16[4,128,128]{2,1,0:T(8,128)(2,1)S(1)} %get-tuple-element.27), channel_id=1, source_target_pairs={{1,2},{3,4},{5,6},{7,8},{9,10},{11,12},{13,14},{2,1},{4,3},{6,5},{... | collective-permute-start | bytes 393224 | tf_op jit(solution)/shard_map/ppermute | solution.py:573

commit v3 on v1

--- a/solution.py
+++ b/solution.py
@@ -11,7 +11,7 @@
 GROUP = 2
 LATE_GROUP = 4
 LISTS = 7
-BUDGET = 43
+BUDGET = 37
 COST = (10, 7)
 SMEM_SPEC = pl.BlockSpec(memory_space=pltpu.SMEM)
 VMEM_SPEC = pl.BlockSpec(memory_space=pltpu.VMEM)
@@ -42,6 +42,8 @@
         self.first_at = self.own
         self.early_at = self.own + self.halo
         self.spare = self.early_at + self.early
+        cut = (self.halo + 1) // 2
+        self.pieces = ((0, cut), (cut, self.halo - cut))
         self.halo_base = self.bases((low, high))
         self.early_base = self.bases(early)
         shifts = (rows, -rows)
@@ -90,6 +92,18 @@
             else:
                 runs.append((index, 1))
         return runs
+
+    def near_packs(self, piece):
+        begin, count = self.pieces[piece]
+        found = []
+        for pack in self.packs:
+            part = []
+            for start, place, size in pack:
+                low, high = max(place, begin), min(place + size, begin + count)
+                if low < high:
+                    part.append((start + low - place, low - begin, high - low))
+            found.append(part)
+        return found
 
     def pick(self, bases, shift, row, otherwise):
         value = otherwise
@@ -154,43 +168,62 @@
     return pl.ds(jnp.where(odd == cross, geo.own - span, 0), span)
 
 
-def pack_kernel(
-    geo, density_ref, centre_in, offsets_in, counts_in,
-    near_ref, cross_ref, meta_ref, acc_ref,
+def pack_kernel(geo, density_ref, cross_ref, sems):
+    odd = lax.axis_index("blk") % 2 == 1
+
+    def fill(up, down):
+        pack = geo.packs[0 if up else 1]
+        run_copies(
+            [
+                pltpu.make_async_copy(
+                    density_ref.at[pl.ds(start, count)], cross_ref.at[pl.ds(place, count)], sems.at[i]
+                )
+                for i, (start, place, count) in enumerate(pack)
+            ]
+        )
+
+    by_parity(odd, fill, False, True)
+
+
+def setup_kernel(
+    geo, cross_ref, density_ref, centre_in, offsets_in, counts_in,
+    near_a, near_b, meta_ref, acc_ref,
     centre_ref, offsets_ref, counts_ref, sems,
 ):
     index = lax.axis_index("blk")
     odd = index % 2 == 1
-
-    def copies(up, down):
-        return [
-            pltpu.make_async_copy(
-                density_ref.at[pl.ds(start, count)], ref.at[pl.ds(place, count)], sems.at[side, i]
-            )
-            for side, (pack, ref) in enumerate(zip(geo.packs, (up, down)))
-            for i, (start, place, count) in enumerate(pack)
-        ]
-
-    def start(up, down):
-        for copy in copies(up, down):
-            copy.start()
-
-    by_parity(odd, start, near_ref, cross_ref)
     scalars = [
-        pltpu.make_async_copy(*pair, sems.at[2, i])
+        pltpu.make_async_copy(*pair, sems.at[0, i])
         for i, pair in enumerate(
             ((centre_in, centre_ref), (offsets_in, offsets_ref), (counts_in, counts_ref))
         )
     ]
     for copy in scalars:
         copy.start()
+
+    def each_copy(act):
+        def go(up, down):
+            near, number = (0 if up else 1), 0
+            for piece, ref in enumerate((near_a, near_b)):
+                for start, place, count in geo.near_packs(piece)[near]:
+                    act(
+                        pltpu.make_async_copy(
+                            density_ref.at[pl.ds(start, count)],
+                            ref.at[pl.ds(place, count)],
+                            sems.at[1, number],
+                        )
+                    )
+                    number += 1
+
+        by_parity(odd, go, True, False)
+
+    each_copy(lambda copy: copy.start())
     for where in (zone(geo, odd, False), pl.ds(geo.first_at, geo.halo)):
         acc_ref[where] = jnp.zeros_like(acc_ref[where])
     for copy in scalars:
         copy.wait()
     build_lists(geo, index, centre_ref, offsets_ref, counts_ref, meta_ref)
-    for copy in copies(near_ref, cross_ref):
-        copy.wait()
+    each_copy(lambda copy: copy.wait())
 
 
 def group_count(geo, meta_ref, which):
@@ -199,7 +232,7 @@
 
 def inner_share(geo, meta_ref):
     room = BUDGET
-    for which in (CROSS_MANY, CROSS_FEW, NEAR_MANY, NEAR_FEW):
+    for which in (CROSS_MANY, CROSS_FEW):
         room = room - COST[which % 2] * group_count(geo, meta_ref, which)
     share = []
     for which in (INNER_MANY, INNER_FEW):
@@ -428,26 +461,30 @@
             geo, meta_ref, which, lambda chosen, width=width: add_own(geo, chosen, width, *refs)
         )
     early_out[...] = acc_ref[pl.ds(geo.early_at, geo.early)].astype(early_out.dtype)
-
-
-def near_kernel(
-    geo, meta_ref, halo_ref, tiles_ref, ao_ref, kernel_ref, weights_ref, acc_in, acc_ref, first_out
-):
-    refs = (meta_ref, tiles_ref, ao_ref, kernel_ref, weights_ref, acc_ref, halo_ref)
-    for which, width in ((NEAR_MANY, geo.slots), (NEAR_FEW, 2)):
-        each_group(
-            geo, meta_ref, which, lambda chosen, width=width: add_whole(geo, chosen, width, *refs)
-        )
-    first_out[...] = acc_ref[pl.ds(geo.first_at, geo.halo)].astype(first_out.dtype)
     share = inner_share(geo, meta_ref)
     for which, width, end in ((INNER_MANY, geo.slots, share[0]), (INNER_FEW, 2, share[1])):
         each_group(
             geo,
             meta_ref,
             which,
-            lambda chosen, width=width: add_whole(geo, chosen, width, *refs[:-1]),
+            lambda chosen, width=width: add_whole(geo, chosen, width, *refs),
             end=end,
         )
+
+
+def near_kernel(
+    geo, meta_ref, halo_a, halo_b, tiles_ref, ao_ref, kernel_ref, weights_ref, acc_in,
+    acc_ref, out_a, out_b, halo_ref,
+):
+    for ref, (start, count) in zip((halo_a, halo_b), geo.pieces):
+        halo_ref[pl.ds(start, count)] = ref[...]
+    refs = (meta_ref, tiles_ref, ao_ref, kernel_ref, weights_ref, acc_ref, halo_ref)
+    for which, width in ((NEAR_MANY, geo.slots), (NEAR_FEW, 2)):
+        each_group(
+            geo, meta_ref, which, lambda chosen, width=width: add_whole(geo, chosen, width, *refs)
+        )
+    for out, (start, count) in zip((out_a, out_b), geo.pieces):
+        out[...] = acc_ref[pl.ds(geo.first_at + start, count)].astype(out.dtype)
 
 
 def late_kernel(
@@ -472,7 +509,7 @@
 
 
 def inner_kernel(
-    geo, meta_ref, first_ref, tiles_ref, ao_ref, kernel_ref, weights_ref, h_ref, acc_in,
+    geo, meta_ref, first_a, first_b, tiles_ref, ao_ref, kernel_ref, weights_ref, h_ref, acc_in,
     acc_ref, out_ref, sems,
 ):
     odd = meta_ref[geo.odd_at] == 1
@@ -488,8 +525,9 @@
         )
 
     def add_near(up, down):
-        for start, place, count in geo.packs[0 if up else 1]:
-            acc_ref[pl.ds(start, count)] += first_ref[pl.ds(place, count)].astype(jnp.float32)
+        for piece, ref in enumerate((first_a, first_b)):
+            for start, place, count in geo.near_packs(piece)[0 if up else 1]:
+                acc_ref[pl.ds(start, count)] += ref[pl.ds(place, count)].astype(jnp.float32)
 
     by_parity(odd, add_near, True, False)
     done = zone(geo, odd, False)
@@ -575,22 +613,30 @@
     dma = pltpu.SemaphoreType.DMA
     acc_type = pltpu.VMEM((geo.spare + 1, nb, nb), jnp.float32)
 
-    near_halo, cross_halo, meta, acc = call(
+    hbm_tiles = in_hbm(tiles)
+    cross = call(
         functools.partial(pack_kernel, geo),
-        (pack(geo.halo),) * 2 + (pltpu.SMEM((geo.meta_size,), jnp.int32), acc_type),
-        [ANY_SPEC] * 4,
+        pack(geo.halo),
+        [ANY_SPEC],
+        VMEM_SPEC,
+        [dma((geo.reach,))],
+        cost=pl.CostEstimate(flops=10**10, bytes_accessed=10**8, transcendentals=0),
+    )(hbm_tiles)
+    cross_halo = to_second(cross, size)
+    pieces = tuple(pack(count) for _, count in geo.pieces)
+    *near_halo, meta, acc = call(
+        functools.partial(setup_kernel, geo),
+        pieces + (pltpu.SMEM((geo.meta_size,), jnp.int32), acc_type),
+        [VMEM_SPEC] + [ANY_SPEC] * 4,
         (VMEM_SPEC,) * 2 + (SMEM_SPEC, VMEM_SPEC),
         [
             pltpu.SMEM((batches,), jnp.int32),
             pltpu.SMEM((slots, batches), jnp.int32),
             pltpu.SMEM((batches,), jnp.int32),
-            dma((3, max(geo.reach, 3))),
+            dma((2, 2 * geo.reach + 1)),
         ],
-        cost=pl.CostEstimate(flops=10**10, bytes_accessed=10**8, transcendentals=0),
-    )(in_hbm(tiles), in_hbm(centre), in_hbm(sig_offsets.T), in_hbm(counts))
-    cross_halo = to_second(cross_halo, size)
-    near_halo = to_first(near_halo, size)
-
+    )(cross, hbm_tiles, in_hbm(centre), in_hbm(sig_offsets.T), in_hbm(counts))
+    near_halo = [to_first(piece, size) for piece in near_halo]
     panel = (tiles, ao_values, kernel, grid_weights)
     acc, early = call(
         functools.partial(early_kernel, geo),
@@ -602,15 +648,15 @@
     )(meta, *panel, acc)
     early = to_second(early, size)
 
-    acc, first = call(
+    acc, *first = call(
         functools.partial(near_kernel, geo),
-        (acc_type, pack(geo.halo)),
-        [SMEM_SPEC] + [VMEM_SPEC] * 6,
-        (VMEM_SPEC,) * 2,
-        [],
-        {6: 0},
-    )(meta, near_halo, *panel, acc)
-    first = to_first(first, size)
+        (acc_type,) + pieces,
+        [SMEM_SPEC] + [VMEM_SPEC] * 7,
+        (VMEM_SPEC,) * 3,
+        [pack(geo.halo)],
+        {7: 0},
+    )(meta, *near_halo, *panel, acc)
+    first = [to_first(piece, size) for piece in first]
 
     h_type = pltpu.VMEM((batches + 1, geo.reach * nb, pts), jnp.bfloat16)
     h, late = call(
@@ -626,11 +672,11 @@
     acc, out = call(
         functools.partial(inner_kernel, geo),
         (acc_type, whole),
-        [SMEM_SPEC] + [VMEM_SPEC] * 7,
+        [SMEM_SPEC] + [VMEM_SPEC] * 8,
         (VMEM_SPEC, ANY_SPEC),
         [dma((1 + max(len(runs) for runs in geo.quiet),))],
-        {7: 0},
-    )(meta, first, *panel, h, acc)
+        {8: 0},
+    )(meta, *first, *panel, h, acc)
 
     parts = 2 * geo.reach
     out = call(

time: 25.7 us -> 26.5 us (1.031)
  the two profiles are of different devices: /device:TPU:1 before, /device:TPU:27 now
where the time goes in v3:
time: 26.5 us; the launch traced here: 26.2 us
  Pallas kernels  11.6 us (44%)
  starting transfers between devices  11.4 us (43%)
  waiting for transfers between devices  3.02 us (11%)
    ppermute x3, starting transfers between devices, to_second(): got = lax.ppermute(x, 'blk', pairs + [(j, i) for i, j in pairs])  8.22 us
    ppermute x4, starting transfers between devices, to_first(): got = lax.ppermute(x, 'blk', pairs + [(j, i) for i, j in pairs])  3.22 us
    pallas_call x1, Pallas kernels, local(): call(functools.partial(early_kernel, geo), (acc_type, pack(geo.early)), [...  3.08 us
    ppermute x3, waiting for transfers between devices, to_second(): got = lax.ppermute(x, 'blk', pairs + [(j, i) for i, j in pairs])  3.01 us
    pallas_call x1, Pallas kernels, local(): call(functools.partial(inner_kernel, geo), (acc_type, whole), [SMEM_SPEC]...  2.72 us
    pallas_call x1, Pallas kernels, local(): call(functools.partial(near_kernel, geo), (acc_type,) + pieces, [SMEM_SPE...  1.7 us
    pallas_call x1, Pallas kernels, local(): call(functools.partial(setup_kernel, geo), pieces + (pltpu.SMEM((geo.meta...  1.24 us
    pallas_call x1, Pallas kernels, local(): call(functools.partial(pack_kernel, geo), pack(geo.halo), [ANY_SPEC], VME...  1.19 us
  transfers between devices with their start and end apart: 7, of which 1 were waited for; matrix products, arithmetic and copies ran while one was open for 0% of the time, Pallas kernels for 36%

profile of v3, /device:TPU:27, one launch (start us, length us, event | category | flops | bytes accessed | tf_op | source)
XLA Modules:
  0.0 26.2 jit_solution(9795370152593735488)
XLA Ops:
  0.0 0.0 copy-start
  0.0 0.0 copy-start.1
  0.0 0.0 copy-start.2
  0.0 0.0 copy-start.3
  0.0 1.2 %shard_map.73.cross_ref = bf16[11,128,128]{2,1,0:T(8,128)(2,1)S(1)} custom-call(bf16[72,128,128]{2,1,0:T(8,128)(2,1)} %bitcast.3), custom_call_target="tpu_custom_call" | custom-call | flops 10000000000 | bytes 100000000 | tf_op jit(solution)/shard_map/pallas_call | solution.py:617
  1.2 4.0 %collective-permute-start.1 = (bf16[11,128,128]{2,1,0:T(8,128)(2,1)S(1)}, bf16[11,128,128]{2,1,0:T(8,128)(2,1)S(1)}, u32[]{:S(2)}, u32[]{:S(2)}) collective-permute-start(bf16[11,128,128]{2,1,0:T(8,128)(2,1)S(1)} %shard_map.73.cross_ref), channel_id=1, source_target_pairs={{1,2},{3,4},{5,6},{7,8},{9,10},{11,12},{13,14},{2,1},{4,3},{6,5},{... | collective-permute-start | bytes 1081352 | tf_op jit(solution)/shard_map/ppermute | solution.py:601
  5.2 1.2 %shard_map.74 = (bf16[6,128,128]{2,1,0:T(8,128)(2,1)S(1)}, bf16[5,128,128]{2,1,0:T(8,128)(2,1)S(1)}, s32[178]{0:T(256)S(4)}, f32[91,128,128]{2,1,0:T(8,128)S(1)}) custom-call(bf16[11,128,128]{2,1,0:T(8,128)(2,1)S(1)} %shard_map.73.cross_ref, bf16[72,128,128]{2,1,0:T(8,128)(2,1)} %bitcast.4, s32[12]{0:T(128)} %centre_in.1, s32[4,12]{1,0:T(4,128)} %bitcast.8, ...), custom_call_target="tpu_custom_call" | custom-call | tf_op jit(solution)/shard_map/pallas_call | solution.py:627
  6.4 0.1 collective-permute-start.3
  6.5 0.5 %collective-permute-start.4 = (bf16[5,128,128]{2,1,0:T(8,128)(2,1)S(1)}, bf16[5,128,128]{2,1,0:T(8,128)(2,1)S(1)}, u32[]{:S(2)}, u32[]{:S(2)}) collective-permute-start(bf16[5,128,128]{2,1,0:T(8,128)(2,1)S(1)} %get-tuple-element.23), channel_id=1, source_target_pairs={{0,1},{2,3},{4,5},{6,7},{8,9},{10,11},{12,13},{14,15},{1,0},{3,2},... | collective-permute-start | bytes 491528 | tf_op jit(solution)/shard_map/ppermute | solution.py:595
  7.0 0.0 copy-done
  7.0 0.0 copy-done.1
  7.0 0.0 copy-done.2
  7.0 0.0 copy-done.3
  7.0 3.1 %shard_map.75 = (f32[91,128,128]{2,1,0:T(8,128)S(1)}, bf16[7,128,128]{2,1,0:T(8,128)(2,1)S(1)}) custom-call(s32[178]{0:T(256)S(4)} %get-tuple-element.18.meta_ref, bf16[72,128,128]{2,1,0:T(8,128)(2,1)S(1)} %bitcast.5, bf16[12,4,128,256]{3,2,1,0:T(8,128)(2,1)S(1)} %copy-done, bf16[12,256,256]{2,1,0:T(8,128)(2,1)S(1)} %copy-done.2, ...), custom_call_target="tpu_custom_call", output_to_operand_aliasing={{0}: (5, {})} | custom-call | tf_op jit(solution)/shard_map/pallas_call | solution.py:641
  10.1 2.3 %collective-permute-start = (bf16[7,128,128]{2,1,0:T(8,128)(2,1)S(1)}, bf16[7,128,128]{2,1,0:T(8,128)(2,1)S(1)}, u32[]{:S(2)}, u32[]{:S(2)}) collective-permute-start(bf16[7,128,128]{2,1,0:T(8,128)(2,1)S(1)} %get-tuple-element.20), channel_id=1, source_target_pairs={{1,2},{3,4},{5,6},{7,8},{9,10},{11,12},{13,14},{2,1},{4,3},{6,5},{... | collective-permute-start | bytes 688136 | tf_op jit(solution)/shard_map/ppermute | solution.py:601
  12.5 0.0 collective-permute-done.4.halo_b
  12.5 0.0 collective-permute-done.3.halo_a
  12.5 1.7 %shard_map.77 = (f32[91,128,128]{2,1,0:T(8,128)S(1)}, bf16[6,128,128]{2,1,0:T(8,128)(2,1)S(1)}, bf16[5,128,128]{2,1,0:T(8,128)(2,1)S(1)}) custom-call(s32[178]{0:T(256)S(4)} %get-tuple-element.18.meta_ref, bf16[6,128,128]{2,1,0:T(8,128)(2,1)S(1)} %collective-permute-done.3.halo_a, ...), custom_call_target="tpu_custom_call", output_to_operand_aliasing={{0}: (7, {})} | custom-call | tf_op jit(solution)/shard_map/pallas_call | solution.py:651
  14.2 2.6 %collective-permute-start.5 = (bf16[6,128,128]{2,1,0:T(8,128)(2,1)S(1)}, bf16[6,128,128]{2,1,0:T(8,128)(2,1)S(1)}, u32[]{:S(2)}, u32[]{:S(2)}) collective-permute-start(bf16[6,128,128]{2,1,0:T(8,128)(2,1)S(1)} %get-tuple-element.25), channel_id=1, source_target_pairs={{0,1},{2,3},{4,5},{6,7},{8,9},{10,11},{12,13},{14,15},{1,0},{3,2},... | collective-permute-start | bytes 589832 | tf_op jit(solution)/shard_map/ppermute | solution.py:595
  16.8 0.1 collective-permute-start.6
  16.8 0.0 collective-permute-done.1.halo_ref
  16.8 0.7 %shard_map.76 = (bf16[13,256,256]{2,1,0:T(8,128)(2,1)S(1)}, bf16[4,128,128]{2,1,0:T(8,128)(2,1)S(1)}) custom-call(s32[178]{0:T(256)S(4)} %get-tuple-element.18.meta_ref, bf16[11,128,128]{2,1,0:T(8,128)(2,1)S(1)} %collective-permute-done.1.halo_ref, bf16[12,4,128,256]{3,2,1,0:T(8,128)(2,1)S(1)} %copy-done, bf16[12,256,256]{2,1,0:T(8,128)(2,1)S(1)} %copy-done.2, ...), custom_call_target="tpu_custom_call" | custom-call | tf_op jit(solution)/shard_map/pallas_call | solution.py:662
  17.6 1.9 %collective-permute-start.2 = (bf16[4,128,128]{2,1,0:T(8,128)(2,1)S(1)}, bf16[4,128,128]{2,1,0:T(8,128)(2,1)S(1)}, u32[]{:S(2)}, u32[]{:S(2)}) collective-permute-start(bf16[4,128,128]{2,1,0:T(8,128)(2,1)S(1)} %get-tuple-element.21), channel_id=1, source_target_pairs={{1,2},{3,4},{5,6},{7,8},{9,10},{11,12},{13,14},{2,1},{4,3},{6,5},{... | collective-permute-start | bytes 393224 | tf_op jit(solution)/shard_map/ppermute | solution.py:601
  19.5 0.0 collective-permute-done.6.first_b
  19.5 0.0 collective-permute-done.5.first_a
  19.5 2.7 %shard_map.78 = (f32[91,128,128]{2,1,0:T(8,128)S(1)}, f32[72,128,128]{2,1,0:T(8,128)}) custom-call(s32[178]{0:T(256)S(4)} %get-tuple-element.18.meta_ref, bf16[6,128,128]{2,1,0:T(8,128)(2,1)S(1)} %collective-permute-done.5.first_a, bf16[5,128,128]{2,1,0:T(8,128)(2,1)S(1)} %collective-permute-done.6.first_b, ...), custom_call_target="tpu_custom_call", output_to_operand_aliasing={{0}: (8, {})} | custom-call | tf_op jit(solution)/shard_map/pallas_call | solution.py:672
  22.3 0.0 collective-permute-done.early_ref
  22.3 3.0 %collective-permute-done.2.late_ref = bf16[4,128,128]{2,1,0:T(8,128)(2,1)S(1)} collective-permute-done((bf16[4,128,128]{2,1,0:T(8,128)(2,1)S(1)}, bf16[4,128,128]{2,1,0:T(8,128)(2,1)S(1)}, u32[]{:S(2)}, u32[]{:S(2)}) %collective-permute-start.2) | collective-permute-done | bytes 131104 | tf_op jit(solution)/shard_map/ppermute | solution.py:601
  25.3 0.9 %shard_map.79 = f32[72,128,128]{2,1,0:T(8,128)} custom-call(s32[178]{0:T(256)S(4)} %get-tuple-element.18.meta_ref, bf16[7,128,128]{2,1,0:T(8,128)(2,1)S(1)} %collective-permute-done.early_ref, bf16[4,128,128]{2,1,0:T(8,128)(2,1)S(1)} %collective-permute-done.2.late_ref, ...), custom_call_target="tpu_custom_call", output_to_operand_aliasing={{}: (4, {})} | custom-call | tf_op jit(solution)/shard_map/pallas_call | solution.py:682
Async XLA Ops:
  0.0 7.0 %copy-start = (bf16[12,4,128,256]{3,2,1,0:T(8,128)(2,1)S(1)}, bf16[12,4,128,256]{3,2,1,0:T(8,128)(2,1)}, u32[]{:S(2)}) copy-start(bf16[12,4,128,256]{3,2,1,0:T(8,128)(2,1)} %ao_ref.7) | copy-start | bytes 9437188
  0.0 7.0 %copy-start.1 = (bf16[8,9,128,128]{3,2,1,0:T(8,128)(2,1)S(1)}, bf16[8,9,128,128]{3,2,1,0:T(8,128)(2,1)}, u32[]{:S(2)}) copy-start(bf16[8,9,128,128]{3,2,1,0:T(8,128)(2,1)} %param.7) | copy-start | bytes 7077892
  0.0 7.0 %copy-start.2 = (bf16[12,256,256]{2,1,0:T(8,128)(2,1)S(1)}, bf16[12,256,256]{2,1,0:T(8,128)(2,1)}, u32[]{:S(2)}) copy-start(bf16[12,256,256]{2,1,0:T(8,128)(2,1)} %kernel_ref.7) | copy-start | bytes 4718596
  0.0 7.0 %copy-start.3 = (f32[12,256]{1,0:T(8,128)S(1)}, f32[12,256]{1,0:T(8,128)}, u32[]{:S(2)}) copy-start(f32[12,256]{1,0:T(8,128)} %weights_ref.7) | copy-start | bytes 36868
  1.2 15.6 %collective-permute-start.1 = (bf16[11,128,128]{2,1,0:T(8,128)(2,1)S(1)}, bf16[11,128,128]{2,1,0:T(8,128)(2,1)S(1)}, u32[]{:S(2)}, u32[]{:S(2)}) collective-permute-start(bf16[11,128,128]{2,1,0:T(8,128)(2,1)S(1)} %shard_map.73.cross_ref), channel_id=1, source_target_pairs={{1,2},{3,4},{5,6},{7,8},{9,10},{11,12},{13,14},{2,1},{4,3},{6,5},{... | collective-permute-start | bytes 1081352 | tf_op jit(solution)/shard_map/ppermute | solution.py:601
  6.4 6.0 %collective-permute-start.3 = (bf16[6,128,128]{2,1,0:T(8,128)(2,1)S(1)}, bf16[6,128,128]{2,1,0:T(8,128)(2,1)S(1)}, u32[]{:S(2)}, u32[]{:S(2)}) collective-permute-start(bf16[6,128,128]{2,1,0:T(8,128)(2,1)S(1)} %get-tuple-element.22), channel_id=1, source_target_pairs={{0,1},{2,3},{4,5},{6,7},{8,9},{10,11},{12,13},{14,15},{1,0},{3,2},... | collective-permute-start | bytes 589832 | tf_op jit(solution)/shard_map/ppermute | solution.py:595
  6.5 5.9 %collective-permute-start.4 = (bf16[5,128,128]{2,1,0:T(8,128)(2,1)S(1)}, bf16[5,128,128]{2,1,0:T(8,128)(2,1)S(1)}, u32[]{:S(2)}, u32[]{:S(2)}) collective-permute-start(bf16[5,128,128]{2,1,0:T(8,128)(2,1)S(1)} %get-tuple-element.23), channel_id=1, source_target_pairs={{0,1},{2,3},{4,5},{6,7},{8,9},{10,11},{12,13},{14,15},{1,0},{3,2},... | collective-permute-start | bytes 491528 | tf_op jit(solution)/shard_map/ppermute | solution.py:595
  10.1 12.2 %collective-permute-start = (bf16[7,128,128]{2,1,0:T(8,128)(2,1)S(1)}, bf16[7,128,128]{2,1,0:T(8,128)(2,1)S(1)}, u32[]{:S(2)}, u32[]{:S(2)}) collective-permute-start(bf16[7,128,128]{2,1,0:T(8,128)(2,1)S(1)} %get-tuple-element.20), channel_id=1, source_target_pairs={{1,2},{3,4},{5,6},{7,8},{9,10},{11,12},{13,14},{2,1},{4,3},{6,5},{... | collective-permute-start | bytes 688136 | tf_op jit(solution)/shard_map/ppermute | solution.py:601
  14.2 5.3 %collective-permute-start.5 = (bf16[6,128,128]{2,1,0:T(8,128)(2,1)S(1)}, bf16[6,128,128]{2,1,0:T(8,128)(2,1)S(1)}, u32[]{:S(2)}, u32[]{:S(2)}) collective-permute-start(bf16[6,128,128]{2,1,0:T(8,128)(2,1)S(1)} %get-tuple-element.25), channel_id=1, source_target_pairs={{0,1},{2,3},{4,5},{6,7},{8,9},{10,11},{12,13},{14,15},{1,0},{3,2},... | collective-permute-start | bytes 589832 | tf_op jit(solution)/shard_map/ppermute | solution.py:595
  16.8 2.8 %collective-permute-start.6 = (bf16[5,128,128]{2,1,0:T(8,128)(2,1)S(1)}, bf16[5,128,128]{2,1,0:T(8,128)(2,1)S(1)}, u32[]{:S(2)}, u32[]{:S(2)}) collective-permute-start(bf16[5,128,128]{2,1,0:T(8,128)(2,1)S(1)} %get-tuple-element.26), channel_id=1, source_target_pairs={{0,1},{2,3},{4,5},{6,7},{8,9},{10,11},{12,13},{14,15},{1,0},{3,2},... | collective-permute-start | bytes 491528 | tf_op jit(solution)/shard_map/ppermute | solution.py:595
  17.6 7.7 %collective-permute-start.2 = (bf16[4,128,128]{2,1,0:T(8,128)(2,1)S(1)}, bf16[4,128,128]{2,1,0:T(8,128)(2,1)S(1)}, u32[]{:S(2)}, u32[]{:S(2)}) collective-permute-start(bf16[4,128,128]{2,1,0:T(8,128)(2,1)S(1)} %get-tuple-element.21), channel_id=1, source_target_pairs={{1,2},{3,4},{5,6},{7,8},{9,10},{11,12},{13,14},{2,1},{4,3},{6,5},{... | collective-permute-start | bytes 393224 | tf_op jit(solution)/shard_map/ppermute | solution.py:601

commit v4 on v2

--- a/solution.py
+++ b/solution.py
@@ -10,9 +10,9 @@
 MIB = 1 << 20
 GROUP = 2
 LATE_GROUP = 4
+PIECE = 2
 LISTS = 7
 BUDGET = 43
-EXTRA = 8
 COST = (10, 7)
 SMEM_SPEC = pl.BlockSpec(memory_space=pltpu.SMEM)
 VMEM_SPEC = pl.BlockSpec(memory_space=pltpu.VMEM)
@@ -164,18 +164,27 @@
     index = lax.axis_index("blk")
     odd = index % 2 == 1
 
-    def copies(up, down):
-        return [
-            pltpu.make_async_copy(
-                density_ref.at[pl.ds(start, count)], ref.at[pl.ds(place, count)], sems.at[side, i]
-            )
-            for side, (pack, ref) in enumerate(zip(geo.packs, (up, down)))
-            for i, (start, place, count) in enumerate(pack)
-        ]
+    def copies(up, down, near_first):
+        found = []
+        for side, (pack, ref) in enumerate(zip(geo.packs, (up, down))):
+            number = 0
+            for start, place, count in pack:
+                for at in range(0, count, PIECE):
+                    size = min(PIECE, count - at)
+                    found.append(
+                        pltpu.make_async_copy(
+                            density_ref.at[pl.ds(start + at, size)],
+                            ref.at[pl.ds(place + at, size)],
+                            sems.at[side, number],
+                        )
+                    )
+                    number += 1
+        half = len(found) // 2
+        return found[half:] + found[:half] if near_first else found
 
     def start(up, down):
-        for copy in copies(up, down):
-            copy.start(priority=1)
+        for copy in copies(up, down, up is near_ref):
+            copy.start()
 
     scalars = [
         pltpu.make_async_copy(*pair, sems.at[2, i])
@@ -191,7 +200,7 @@
     build_lists(geo, index, Info(meta_ref, centre_ref, offsets_ref, counts_ref))
     for where in (zone(geo, odd, False), pl.ds(geo.first_at, geo.halo)):
         acc_ref[where] = jnp.zeros_like(acc_ref[where])
-    for copy in copies(near_ref, cross_ref):
+    for copy in copies(near_ref, cross_ref, False):
         copy.wait()
 
 
@@ -200,8 +209,7 @@
 
 
 def inner_share(geo, info):
-    index = info.meta[geo.origin_at] // geo.rows
-    room = BUDGET + jnp.where((index + 1) // 2 % 2 == 0, EXTRA, 0)
+    room = BUDGET
     for which in (CROSS_MANY, CROSS_FEW, NEAR_MANY, NEAR_FEW):
         room = room - COST[which % 2] * group_count(geo, info, which)
     share = []
@@ -592,7 +600,7 @@
         + (smem(geo.meta_size), smem(batches), smem(slots, batches), smem(batches), acc_type),
         [ANY_SPEC] * 4,
         (VMEM_SPEC,) * 2 + (SMEM_SPEC,) * 4 + (VMEM_SPEC,),
-        [dma((3, max(geo.reach, 3)))],
+        [dma((3, max(geo.halo, 3)))],
         cost=pl.CostEstimate(flops=10**10, bytes_accessed=10**8, transcendentals=0),
     )(in_hbm(tiles), in_hbm(centre), in_hbm(sig_offsets.T), in_hbm(counts))
     cross_halo = to_second(cross_halo, size)

time: 24.8 us -> 24.7 us (level)
  the two profiles are of different devices: /device:TPU:9 before, /device:TPU:1 now
where the time goes in v4:
time: 24.7 us; the launch traced here: 25 us
  starting transfers between devices  12.7 us (51%)
  Pallas kernels  11.6 us (47%)
  waiting for transfers between devices  0.58 us (2%)
    ppermute x3, starting transfers between devices, to_second(): got = lax.ppermute(x, 'blk', pairs + [(j, i) for i, j in pairs])  12.5 us
    pallas_call x1, Pallas kernels, local(): call(functools.partial(inner_kernel, geo), (acc_type, whole), [SMEM_SPEC]...  4.35 us
    pallas_call x1, Pallas kernels, local(): call(functools.partial(near_kernel, geo), (acc_type, pack(geo.halo)), [SM...  2.74 us
    pallas_call x1, Pallas kernels, local(): call(functools.partial(pack_kernel, geo), (pack(geo.halo),) * 2 + (smem(g...  1.59 us
    pallas_call x1, Pallas kernels, local(): call(functools.partial(early_kernel, geo), (acc_type, pack(geo.early)), [...  1.23 us
    pallas_call x1, Pallas kernels, local(): call(functools.partial(finish_kernel, geo), whole, [SMEM_SPEC] + [VMEM_SP...  0.92 us
    pallas_call x1, Pallas kernels, local(): call(functools.partial(late_kernel, geo), (h_type, pack(geo.late)), [SMEM...  0.74 us
    ppermute x3, waiting for transfers between devices, to_second(): got = lax.ppermute(x, 'blk', pairs + [(j, i) for i, j in pairs])  0.58 us
  transfers between devices with their start and end apart: 5, of which 1 were waited for; matrix products, arithmetic and copies ran while one was open for 0% of the time, Pallas kernels for 36%

profile of v4, /device:TPU:1, one launch (start us, length us, event | category | flops | bytes accessed | tf_op | source)
XLA Modules:
  0.0 25.0 jit_solution(8300411131990026502)
XLA Ops:
  0.0 0.0 copy-start
  0.0 0.0 copy-start.1
  0.0 0.0 copy-start.2
  0.0 0.0 copy-start.3
  0.0 1.6 %shard_map.73 = (bf16[11,128,128]{2,1,0:T(8,128)(2,1)S(1)}, bf16[11,128,128]{2,1,0:T(8,128)(2,1)S(1)}, s32[122]{0:T(128)S(4)}, s32[12]{0:T(128)S(4)}, s32[4,12]{...) custom-call(bf16[72,128,128]{2,1,0:T(8,128)(2,1)} %bitcast.3, s32[12]{0:T(128)} %centre_in.1, ...), custom_call_target="tpu_custom_call" | custom-call | flops 10000000000 | bytes 100000000 | tf_op jit(solution)/shard_map/pallas_call | solution.py:597
  1.6 0.1 collective-permute-start.3
  1.7 4.6 %collective-permute-start.1 = (bf16[11,128,128]{2,1,0:T(8,128)(2,1)S(1)}, bf16[11,128,128]{2,1,0:T(8,128)(2,1)S(1)}, u32[]{:S(2)}, u32[]{:S(2)}) collective-permute-start(bf16[11,128,128]{2,1,0:T(8,128)(2,1)S(1)} %get-tuple-element.26), channel_id=1, source_target_pairs={{1,2},{3,4},{5,6},{7,8},{9,10},{11,12},{13,14},{2,1},{4,3},{6,5},{... | collective-permute-start | bytes 1081352 | tf_op jit(solution)/shard_map/ppermute | solution.py:581
  6.4 0.0 copy-done
  6.4 0.0 copy-done.1
  6.4 0.0 copy-done.2
  6.4 0.0 copy-done.3
  6.4 1.2 %shard_map.74 = (f32[91,128,128]{2,1,0:T(8,128)S(1)}, bf16[7,128,128]{2,1,0:T(8,128)(2,1)S(1)}) custom-call(s32[122]{0:T(128)S(4)} %get-tuple-element.20.meta_ref, s32[12]{0:T(128)S(4)} %get-tuple-element.21.centre_ref, s32[4,12]{1,0:T(4,128)S(4)} %get-tuple-element.22.offsets_ref, ...), custom_call_target="tpu_custom_call", output_to_operand_aliasing={{0}: (8, {})} | custom-call | tf_op jit(solution)/shard_map/pallas_call | solution.py:610
  7.7 0.0 collective-permute-done.3.halo_ref
  7.7 2.7 %shard_map.76 = (f32[91,128,128]{2,1,0:T(8,128)S(1)}, bf16[11,128,128]{2,1,0:T(8,128)(2,1)S(1)}) custom-call(s32[122]{0:T(128)S(4)} %get-tuple-element.20.meta_ref, s32[12]{0:T(128)S(4)} %get-tuple-element.21.centre_ref, s32[4,12]{1,0:T(4,128)S(4)} %get-tuple-element.22.offsets_ref, ...), custom_call_target="tpu_custom_call", output_to_operand_aliasing={{0}: (9, {})} | custom-call | tf_op jit(solution)/shard_map/pallas_call | solution.py:620
  10.4 0.1 collective-permute-start.4
  10.5 3.5 %collective-permute-start = (bf16[7,128,128]{2,1,0:T(8,128)(2,1)S(1)}, bf16[7,128,128]{2,1,0:T(8,128)(2,1)S(1)}, u32[]{:S(2)}, u32[]{:S(2)}) collective-permute-start(bf16[7,128,128]{2,1,0:T(8,128)(2,1)S(1)} %get-tuple-element.25), channel_id=1, source_target_pairs={{1,2},{3,4},{5,6},{7,8},{9,10},{11,12},{13,14},{2,1},{4,3},{6,5},{... | collective-permute-start | bytes 688136 | tf_op jit(solution)/shard_map/ppermute | solution.py:581
  14.0 0.6 %collective-permute-done.1.halo_ref = bf16[11,128,128]{2,1,0:T(8,128)(2,1)S(1)} collective-permute-done((bf16[11,128,128]{2,1,0:T(8,128)(2,1)S(1)}, bf16[11,128,128]{2,1,0:T(8,128)(2,1)S(1)}, u32[]{:S(2)}, u32[]{:S(2)}) %collective-permute-start.1) | collective-permute-done | bytes 360480 | tf_op jit(solution)/shard_map/ppermute | solution.py:581
  14.6 0.7 %shard_map.75 = (bf16[13,256,256]{2,1,0:T(8,128)(2,1)S(1)}, bf16[4,128,128]{2,1,0:T(8,128)(2,1)S(1)}) custom-call(s32[122]{0:T(128)S(4)} %get-tuple-element.20.meta_ref, s32[12]{0:T(128)S(4)} %get-tuple-element.21.centre_ref, s32[4,12]{1,0:T(4,128)S(4)} %get-tuple-element.22.offsets_ref, s32[12]{0:T(128)S(4)} %get-tuple-element.23.counts_ref, ...), custom_call_target="tpu_custom_call" | custom-call | tf_op jit(solution)/shard_map/pallas_call | solution.py:631
  15.3 4.4 %collective-permute-start.2 = (bf16[4,128,128]{2,1,0:T(8,128)(2,1)S(1)}, bf16[4,128,128]{2,1,0:T(8,128)(2,1)S(1)}, u32[]{:S(2)}, u32[]{:S(2)}) collective-permute-start(bf16[4,128,128]{2,1,0:T(8,128)(2,1)S(1)} %get-tuple-element.27), channel_id=1, source_target_pairs={{1,2},{3,4},{5,6},{7,8},{9,10},{11,12},{13,14},{2,1},{4,3},{6,5},{... | collective-permute-start | bytes 393224 | tf_op jit(solution)/shard_map/ppermute | solution.py:581
  19.7 0.0 collective-permute-done.4.first_ref
  19.7 4.4 %shard_map.77 = (f32[91,128,128]{2,1,0:T(8,128)S(1)}, f32[72,128,128]{2,1,0:T(8,128)}) custom-call(s32[122]{0:T(128)S(4)} %get-tuple-element.20.meta_ref, s32[12]{0:T(128)S(4)} %get-tuple-element.21.centre_ref, s32[4,12]{1,0:T(4,128)S(4)} %get-tuple-element.22.offsets_ref, s32[12]{0:T(128)S(4)} %get-tuple-element.23.counts_ref, ...), custom_call_target="tpu_custom_call", output_to_operand_aliasing={{0}: (10, {})} | custom-call | tf_op jit(solution)/shard_map/pallas_call | solution.py:641
  24.1 0.0 collective-permute-done.early_ref
  24.1 0.0 collective-permute-done.2.late_ref
  24.1 0.9 %shard_map.78 = f32[72,128,128]{2,1,0:T(8,128)} custom-call(s32[122]{0:T(128)S(4)} %get-tuple-element.20.meta_ref, bf16[7,128,128]{2,1,0:T(8,128)(2,1)S(1)} %collective-permute-done.early_ref, bf16[4,128,128]{2,1,0:T(8,128)(2,1)S(1)} %collective-permute-done.2.late_ref, ...), custom_call_target="tpu_custom_call", output_to_operand_aliasing={{}: (4, {})} | custom-call | tf_op jit(solution)/shard_map/pallas_call | solution.py:651
Async XLA Ops:
  0.0 6.4 %copy-start = (bf16[12,4,128,256]{3,2,1,0:T(8,128)(2,1)S(1)}, bf16[12,4,128,256]{3,2,1,0:T(8,128)(2,1)}, u32[]{:S(2)}) copy-start(bf16[12,4,128,256]{3,2,1,0:T(8,128)(2,1)} %ao_ref.7) | copy-start | bytes 9437188
  0.0 6.4 %copy-start.1 = (bf16[12,256,256]{2,1,0:T(8,128)(2,1)S(1)}, bf16[12,256,256]{2,1,0:T(8,128)(2,1)}, u32[]{:S(2)}) copy-start(bf16[12,256,256]{2,1,0:T(8,128)(2,1)} %kernel_ref.7) | copy-start | bytes 4718596
  0.0 6.4 %copy-start.2 = (bf16[8,9,128,128]{3,2,1,0:T(8,128)(2,1)S(1)}, bf16[8,9,128,128]{3,2,1,0:T(8,128)(2,1)}, u32[]{:S(2)}) copy-start(bf16[8,9,128,128]{3,2,1,0:T(8,128)(2,1)} %param.7) | copy-start | bytes 7077892
  0.0 6.4 %copy-start.3 = (f32[12,256]{1,0:T(8,128)S(1)}, f32[12,256]{1,0:T(8,128)}, u32[]{:S(2)}) copy-start(f32[12,256]{1,0:T(8,128)} %weights_ref.7) | copy-start | bytes 36868
  1.6 6.0 %collective-permute-start.3 = (bf16[11,128,128]{2,1,0:T(8,128)(2,1)S(1)}, bf16[11,128,128]{2,1,0:T(8,128)(2,1)S(1)}, u32[]{:S(2)}, u32[]{:S(2)}) collective-permute-start(bf16[11,128,128]{2,1,0:T(8,128)(2,1)S(1)} %get-tuple-element.28), channel_id=1, source_target_pairs={{0,1},{2,3},{4,5},{6,7},{8,9},{10,11},{12,13},{14,15},{1,0},{3,2},... | collective-permute-start | bytes 1081352 | tf_op jit(solution)/shard_map/ppermute | solution.py:575
  1.7 12.9 %collective-permute-start.1 = (bf16[11,128,128]{2,1,0:T(8,128)(2,1)S(1)}, bf16[11,128,128]{2,1,0:T(8,128)(2,1)S(1)}, u32[]{:S(2)}, u32[]{:S(2)}) collective-permute-start(bf16[11,128,128]{2,1,0:T(8,128)(2,1)S(1)} %get-tuple-element.26), channel_id=1, source_target_pairs={{1,2},{3,4},{5,6},{7,8},{9,10},{11,12},{13,14},{2,1},{4,3},{6,5},{... | collective-permute-start | bytes 1081352 | tf_op jit(solution)/shard_map/ppermute | solution.py:581
  10.4 9.3 %collective-permute-start.4 = (bf16[11,128,128]{2,1,0:T(8,128)(2,1)S(1)}, bf16[11,128,128]{2,1,0:T(8,128)(2,1)S(1)}, u32[]{:S(2)}, u32[]{:S(2)}) collective-permute-start(bf16[11,128,128]{2,1,0:T(8,128)(2,1)S(1)} %get-tuple-element.30), channel_id=1, source_target_pairs={{0,1},{2,3},{4,5},{6,7},{8,9},{10,11},{12,13},{14,15},{1,0},{3,2},... | collective-permute-start | bytes 1081352 | tf_op jit(solution)/shard_map/ppermute | solution.py:575
  10.5 13.6 %collective-permute-start = (bf16[7,128,128]{2,1,0:T(8,128)(2,1)S(1)}, bf16[7,128,128]{2,1,0:T(8,128)(2,1)S(1)}, u32[]{:S(2)}, u32[]{:S(2)}) collective-permute-start(bf16[7,128,128]{2,1,0:T(8,128)(2,1)S(1)} %get-tuple-element.25), channel_id=1, source_target_pairs={{1,2},{3,4},{5,6},{7,8},{9,10},{11,12},{13,14},{2,1},{4,3},{6,5},{... | collective-permute-start | bytes 688136 | tf_op jit(solution)/shard_map/ppermute | solution.py:581
  15.3 8.8 %collective-permute-start.2 = (bf16[4,128,128]{2,1,0:T(8,128)(2,1)S(1)}, bf16[4,128,128]{2,1,0:T(8,128)(2,1)S(1)}, u32[]{:S(2)}, u32[]{:S(2)}) collective-permute-start(bf16[4,128,128]{2,1,0:T(8,128)(2,1)S(1)} %get-tuple-element.27), channel_id=1, source_target_pairs={{1,2},{3,4},{5,6},{7,8},{9,10},{11,12},{13,14},{2,1},{4,3},{6,5},{... | collective-permute-start | bytes 393224 | tf_op jit(solution)/shard_map/ppermute | solution.py:581

commit v5 on v1

--- a/solution.py
+++ b/solution.py
@@ -12,6 +12,7 @@
 LATE_GROUP = 4
 LISTS = 7
 BUDGET = 43
+WAIT = 18
 COST = (10, 7)
 SMEM_SPEC = pl.BlockSpec(memory_space=pltpu.SMEM)
 VMEM_SPEC = pl.BlockSpec(memory_space=pltpu.VMEM)
@@ -198,16 +199,33 @@
 
 
 def inner_share(geo, meta_ref):
-    room = BUDGET
+    before = BUDGET
     for which in (CROSS_MANY, CROSS_FEW, NEAR_MANY, NEAR_FEW):
-        room = room - COST[which % 2] * group_count(geo, meta_ref, which)
+        before = before - COST[which % 2] * group_count(geo, meta_ref, which)
+    waiting = jnp.where((lax.axis_index("blk") + 1) // 2 % 2 == 1, WAIT, 0)
     share = []
     for which in (INNER_MANY, INNER_FEW):
-        cost = COST[which % 2]
-        taken = jnp.minimum(jnp.maximum(room, 0) // cost, group_count(geo, meta_ref, which))
-        room = room - cost * taken
-        share.append(taken)
+        cost, count = COST[which % 2], group_count(geo, meta_ref, which)
+        first = jnp.minimum(jnp.maximum(before, 0) // cost, count)
+        second = jnp.minimum(jnp.maximum(waiting, 0) // cost, count - first)
+        before = before - cost * first
+        waiting = waiting - cost * second
+        share.append((0, first, first + second, count))
     return share
+
+
+def inner_part(geo, meta_ref, stage, refs):
+    for which, width, bounds in zip(
+        (INNER_MANY, INNER_FEW), (geo.slots, 2), inner_share(geo, meta_ref)
+    ):
+        each_group(
+            geo,
+            meta_ref,
+            which,
+            lambda chosen, width=width: add_whole(geo, chosen, width, *refs),
+            begin=bounds[stage],
+            end=bounds[stage + 1],
+        )
 
 
 def each_group(geo, meta_ref, which, body, size=GROUP, begin=0, end=None):
@@ -439,19 +457,18 @@
             geo, meta_ref, which, lambda chosen, width=width: add_whole(geo, chosen, width, *refs)
         )
     first_out[...] = acc_ref[pl.ds(geo.first_at, geo.halo)].astype(first_out.dtype)
-    share = inner_share(geo, meta_ref)
-    for which, width, end in ((INNER_MANY, geo.slots, share[0]), (INNER_FEW, 2, share[1])):
-        each_group(
-            geo,
-            meta_ref,
-            which,
-            lambda chosen, width=width: add_whole(geo, chosen, width, *refs[:-1]),
-            end=end,
-        )
+    inner_part(geo, meta_ref, 0, refs[:-1])
+
+
+def waiting_kernel(
+    geo, meta_ref, tiles_ref, ao_ref, kernel_ref, weights_ref, acc_in, acc_ref, done_ref
+):
+    inner_part(geo, meta_ref, 1, (meta_ref, tiles_ref, ao_ref, kernel_ref, weights_ref, acc_ref))
+    done_ref[0] = 1
 
 
 def late_kernel(
-    geo, meta_ref, halo_ref, ao_ref, kernel_ref, weights_ref, h_ref, late_out, total_ref
+    geo, meta_ref, done_ref, halo_ref, ao_ref, kernel_ref, weights_ref, h_ref, late_out, total_ref
 ):
     nb = ao_ref.shape[2]
     total_ref[...] = jnp.zeros_like(total_ref)
@@ -477,15 +494,7 @@
 ):
     odd = meta_ref[geo.odd_at] == 1
     refs = (meta_ref, tiles_ref, ao_ref, kernel_ref, weights_ref, acc_ref)
-    share = inner_share(geo, meta_ref)
-    for which, width, begin in ((INNER_MANY, geo.slots, share[0]), (INNER_FEW, 2, share[1])):
-        each_group(
-            geo,
-            meta_ref,
-            which,
-            lambda chosen, width=width: add_whole(geo, chosen, width, *refs),
-            begin=begin,
-        )
+    inner_part(geo, meta_ref, 2, refs)
 
     def add_near(up, down):
         for start, place, count in geo.packs[0 if up else 1]:
@@ -612,14 +621,23 @@
     )(meta, near_halo, *panel, acc)
     first = to_first(first, size)
 
+    acc, done = call(
+        functools.partial(waiting_kernel, geo),
+        (acc_type, pltpu.SMEM((1,), jnp.int32)),
+        [SMEM_SPEC] + [VMEM_SPEC] * 5,
+        (VMEM_SPEC, SMEM_SPEC),
+        [],
+        {5: 0},
+    )(meta, *panel, acc)
+
     h_type = pltpu.VMEM((batches + 1, geo.reach * nb, pts), jnp.bfloat16)
     h, late = call(
         functools.partial(late_kernel, geo),
         (h_type, pack(geo.late)),
-        [SMEM_SPEC] + [VMEM_SPEC] * 4,
+        [SMEM_SPEC] * 2 + [VMEM_SPEC] * 4,
         (VMEM_SPEC,) * 2,
         [pltpu.VMEM((geo.reach * nb, geo.reach * nb), jnp.float32)],
-    )(meta, cross_halo, *panel[1:])
+    )(meta, done, cross_halo, *panel[1:])
     late = to_second(late, size)
 
     whole = jax.ShapeDtypeStruct((geo.own, nb, nb), jnp.float32)

time: 25.7 us -> 24.2 us (0.942)
  starting transfers between devices: 14.2 us -> 12.1 us
  waiting for transfers between devices: 0.19 us -> 1.07 us
  Pallas kernels: 10.8 us -> 10.5 us
    ppermute x3, starting transfers between devices: 14 us -> 11.9 us  [to_second(): got = lax.ppermute(x, 'blk', pairs + [(j, i) for i, j in pairs])]
    pallas_call x1, Pallas kernels: 3.72 us -> 2.12 us  [local(): call(functools.partial(inner_kernel, geo), (acc_type, whole), [SMEM_SPEC]...]
    pallas_call x0 -> x1, Pallas kernels: none -> 1.3 us  [local(): call(functools.partial(waiting_kernel, geo), (acc_type, pltpu.SMEM((1,),...]
    ppermute x3, waiting for transfers between devices: 0.18 us -> 1.07 us  [to_second(): got = lax.ppermute(x, 'blk', pairs + [(j, i) for i, j in pairs])]
  transfers between devices with their start and end apart: 5 -> 5, of which waited for: 1 -> 1; matrix products, arithmetic and copies ran while one was open for 0% -> 0% of each run, Pallas kernels for 33% -> 34%
where the time goes in v5:
time: 24.2 us; the launch traced here: 23.8 us
  starting transfers between devices  12.1 us (50%)
  Pallas kernels  10.5 us (43%)
  waiting for transfers between devices  1.07 us (4%)
    ppermute x3, starting transfers between devices, to_second(): got = lax.ppermute(x, 'blk', pairs + [(j, i) for i, j in pairs])  11.9 us
    pallas_call x1, Pallas kernels, local(): call(functools.partial(near_kernel, geo), (acc_type, pack(geo.halo)), [SM...  2.72 us
    pallas_call x1, Pallas kernels, local(): call(functools.partial(inner_kernel, geo), (acc_type, whole), [SMEM_SPEC]...  2.12 us
    pallas_call x1, Pallas kernels, local(): call(functools.partial(pack_kernel, geo), (pack(geo.halo),) * 2 + (pltpu....  1.43 us
    pallas_call x1, Pallas kernels, local(): call(functools.partial(waiting_kernel, geo), (acc_type, pltpu.SMEM((1,),...  1.3 us
    pallas_call x1, Pallas kernels, local(): call(functools.partial(early_kernel, geo), (acc_type, pack(geo.early)), [...  1.24 us
    ppermute x3, waiting for transfers between devices, to_second(): got = lax.ppermute(x, 'blk', pairs + [(j, i) for i, j in pairs])  1.07 us
    pallas_call x1, Pallas kernels, local(): call(functools.partial(finish_kernel, geo), whole, [SMEM_SPEC] + [VMEM_SP...  0.9 us
  transfers between devices with their start and end apart: 5, of which 1 were waited for; matrix products, arithmetic and copies ran while one was open for 0% of the time, Pallas kernels for 34%

profile of v5, /device:TPU:1, one launch (start us, length us, event | category | flops | bytes accessed | tf_op | source)
XLA Modules:
  0.0 23.8 jit_solution(10252997339610576751)
XLA Ops:
  0.0 0.0 copy-start
  0.0 0.0 copy-start.1
  0.0 0.0 copy-start.2
  0.0 0.0 copy-start.3
  0.0 1.4 %shard_map.73 = (bf16[11,128,128]{2,1,0:T(8,128)(2,1)S(1)}, bf16[11,128,128]{2,1,0:T(8,128)(2,1)S(1)}, s32[178]{0:T(256)S(4)}, f32[91,128,128]{2,1,0:T(8,128)S(1)}) custom-call(bf16[72,128,128]{2,1,0:T(8,128)(2,1)} %bitcast.3, s32[12]{0:T(128)} %centre_in.1, s32[4,12]{1,0:T(4,128)} %bitcast.8, s32[12]{0:T(128)} %counts_in.1), custom_call_target="tpu_custom_call" | custom-call | flops 10000000000 | bytes 100000000 | tf_op jit(solution)/shard_map/pallas_call | solution.py:587
  1.5 0.1 collective-permute-start.1
  1.6 4.8 %collective-permute-start.2 = (bf16[11,128,128]{2,1,0:T(8,128)(2,1)S(1)}, bf16[11,128,128]{2,1,0:T(8,128)(2,1)S(1)}, u32[]{:S(2)}, u32[]{:S(2)}) collective-permute-start(bf16[11,128,128]{2,1,0:T(8,128)(2,1)S(1)} %get-tuple-element.26), channel_id=1, source_target_pairs={{1,2},{3,4},{5,6},{7,8},{9,10},{11,12},{13,14},{2,1},{4,3},{6,5},{... | collective-permute-start | bytes 1081352 | tf_op jit(solution)/shard_map/ppermute | solution.py:572
  6.3 0.0 copy-done
  6.3 0.0 copy-done.1
  6.4 0.0 copy-done.2
  6.4 0.0 copy-done.3
  6.4 1.2 %shard_map.74 = (f32[91,128,128]{2,1,0:T(8,128)S(1)}, bf16[7,128,128]{2,1,0:T(8,128)(2,1)S(1)}) custom-call(s32[178]{0:T(256)S(4)} %get-tuple-element.19.meta_ref, bf16[72,128,128]{2,1,0:T(8,128)(2,1)S(1)} %bitcast.4, bf16[12,4,128,256]{3,2,1,0:T(8,128)(2,1)S(1)} %copy-done, bf16[12,256,256]{2,1,0:T(8,128)(2,1)S(1)} %copy-done.1, ...), custom_call_target="tpu_custom_call", output_to_operand_aliasing={{0}: (5, {})} | custom-call | tf_op jit(solution)/shard_map/pallas_call | solution.py:604
  7.6 0.0 collective-permute-done.1.halo_ref
  7.6 2.7 %shard_map.75 = (f32[91,128,128]{2,1,0:T(8,128)S(1)}, bf16[11,128,128]{2,1,0:T(8,128)(2,1)S(1)}) custom-call(s32[178]{0:T(256)S(4)} %get-tuple-element.19.meta_ref, bf16[11,128,128]{2,1,0:T(8,128)(2,1)S(1)} %collective-permute-done.1.halo_ref, bf16[72,128,128]{2,1,0:T(8,128)(2,1)S(1)} %bitcast.5, ...), custom_call_target="tpu_custom_call", output_to_operand_aliasing={{0}: (6, {})} | custom-call | tf_op jit(solution)/shard_map/pallas_call | solution.py:614
  10.4 0.1 collective-permute-start.4
  10.4 3.5 %collective-permute-start = (bf16[7,128,128]{2,1,0:T(8,128)(2,1)S(1)}, bf16[7,128,128]{2,1,0:T(8,128)(2,1)S(1)}, u32[]{:S(2)}, u32[]{:S(2)}) collective-permute-start(bf16[7,128,128]{2,1,0:T(8,128)(2,1)S(1)} %get-tuple-element.21), channel_id=1, source_target_pairs={{1,2},{3,4},{5,6},{7,8},{9,10},{11,12},{13,14},{2,1},{4,3},{6,5},{... | collective-permute-start | bytes 688136 | tf_op jit(solution)/shard_map/ppermute | solution.py:572
  14.0 1.3 %shard_map.76 = (f32[91,128,128]{2,1,0:T(8,128)S(1)}, s32[1]{0:T(128)S(4)}) custom-call(s32[178]{0:T(256)S(4)} %get-tuple-element.19.meta_ref, bf16[72,128,128]{2,1,0:T(8,128)(2,1)S(1)} %bitcast.6, bf16[12,4,128,256]{3,2,1,0:T(8,128)(2,1)S(1)} %copy-done, bf16[12,256,256]{2,1,0:T(8,128)(2,1)S(1)} %copy-done.1, ...), custom_call_target="tpu_custom_call", output_to_operand_aliasing={{0}: (5, {})} | custom-call | tf_op jit(solution)/shard_map/pallas_call | solution.py:624
  15.3 0.0 collective-permute-done.2.halo_ref
  15.3 0.7 %shard_map.77 = (bf16[13,256,256]{2,1,0:T(8,128)(2,1)S(1)}, bf16[4,128,128]{2,1,0:T(8,128)(2,1)S(1)}) custom-call(s32[178]{0:T(256)S(4)} %get-tuple-element.19.meta_ref, s32[1]{0:T(128)S(4)} %get-tuple-element.25.done_ref, bf16[11,128,128]{2,1,0:T(8,128)(2,1)S(1)} %collective-permute-done.2.halo_ref, bf16[12,4,128,256]{3,2,1,0:T(8,128)(2,1)S(1)} %copy-done, ...), custom_call_target="tpu_custom_call" | custom-call | tf_op jit(solution)/shard_map/pallas_call | solution.py:634
  16.1 3.6 %collective-permute-start.3 = (bf16[4,128,128]{2,1,0:T(8,128)(2,1)S(1)}, bf16[4,128,128]{2,1,0:T(8,128)(2,1)S(1)}, u32[]{:S(2)}, u32[]{:S(2)}) collective-permute-start(bf16[4,128,128]{2,1,0:T(8,128)(2,1)S(1)} %get-tuple-element.27), channel_id=1, source_target_pairs={{1,2},{3,4},{5,6},{7,8},{9,10},{11,12},{13,14},{2,1},{4,3},{6,5},{... | collective-permute-start | bytes 393224 | tf_op jit(solution)/shard_map/ppermute | solution.py:572
  19.7 0.0 collective-permute-done.4.first_ref
  19.7 2.1 %shard_map.78 = (f32[91,128,128]{2,1,0:T(8,128)S(1)}, f32[72,128,128]{2,1,0:T(8,128)}) custom-call(s32[178]{0:T(256)S(4)} %get-tuple-element.19.meta_ref, bf16[11,128,128]{2,1,0:T(8,128)(2,1)S(1)} %collective-permute-done.4.first_ref, bf16[72,128,128]{2,1,0:T(8,128)(2,1)S(1)} %bitcast.7, ...), custom_call_target="tpu_custom_call", output_to_operand_aliasing={{0}: (7, {})} | custom-call | tf_op jit(solution)/shard_map/pallas_call | solution.py:644
  21.8 0.0 collective-permute-done.early_ref
  21.8 1.1 %collective-permute-done.3.late_ref = bf16[4,128,128]{2,1,0:T(8,128)(2,1)S(1)} collective-permute-done((bf16[4,128,128]{2,1,0:T(8,128)(2,1)S(1)}, bf16[4,128,128]{2,1,0:T(8,128)(2,1)S(1)}, u32[]{:S(2)}, u32[]{:S(2)}) %collective-permute-start.3) | collective-permute-done | bytes 131104 | tf_op jit(solution)/shard_map/ppermute | solution.py:572
  22.9 0.9 %shard_map.79 = f32[72,128,128]{2,1,0:T(8,128)} custom-call(s32[178]{0:T(256)S(4)} %get-tuple-element.19.meta_ref, bf16[7,128,128]{2,1,0:T(8,128)(2,1)S(1)} %collective-permute-done.early_ref, bf16[4,128,128]{2,1,0:T(8,128)(2,1)S(1)} %collective-permute-done.3.late_ref, ...), custom_call_target="tpu_custom_call", output_to_operand_aliasing={{}: (4, {})} | custom-call | tf_op jit(solution)/shard_map/pallas_call | solution.py:654
Async XLA Ops:
  0.0 6.3 %copy-start = (bf16[12,4,128,256]{3,2,1,0:T(8,128)(2,1)S(1)}, bf16[12,4,128,256]{3,2,1,0:T(8,128)(2,1)}, u32[]{:S(2)}) copy-start(bf16[12,4,128,256]{3,2,1,0:T(8,128)(2,1)} %ao_ref.9) | copy-start | bytes 9437188
  0.0 6.3 %copy-start.1 = (bf16[12,256,256]{2,1,0:T(8,128)(2,1)S(1)}, bf16[12,256,256]{2,1,0:T(8,128)(2,1)}, u32[]{:S(2)}) copy-start(bf16[12,256,256]{2,1,0:T(8,128)(2,1)} %kernel_ref.9) | copy-start | bytes 4718596
  0.0 6.4 %copy-start.2 = (bf16[8,9,128,128]{3,2,1,0:T(8,128)(2,1)S(1)}, bf16[8,9,128,128]{3,2,1,0:T(8,128)(2,1)}, u32[]{:S(2)}) copy-start(bf16[8,9,128,128]{3,2,1,0:T(8,128)(2,1)} %param.7) | copy-start | bytes 7077892
  0.0 6.4 %copy-start.3 = (f32[12,256]{1,0:T(8,128)S(1)}, f32[12,256]{1,0:T(8,128)}, u32[]{:S(2)}) copy-start(f32[12,256]{1,0:T(8,128)} %weights_ref.9) | copy-start | bytes 36868
  1.5 6.2 %collective-permute-start.1 = (bf16[11,128,128]{2,1,0:T(8,128)(2,1)S(1)}, bf16[11,128,128]{2,1,0:T(8,128)(2,1)S(1)}, u32[]{:S(2)}, u32[]{:S(2)}) collective-permute-start(bf16[11,128,128]{2,1,0:T(8,128)(2,1)S(1)} %get-tuple-element.22), channel_id=1, source_target_pairs={{0,1},{2,3},{4,5},{6,7},{8,9},{10,11},{12,13},{14,15},{1,0},{3,2},... | collective-permute-start | bytes 1081352 | tf_op jit(solution)/shard_map/ppermute | solution.py:566
  1.6 13.7 %collective-permute-start.2 = (bf16[11,128,128]{2,1,0:T(8,128)(2,1)S(1)}, bf16[11,128,128]{2,1,0:T(8,128)(2,1)S(1)}, u32[]{:S(2)}, u32[]{:S(2)}) collective-permute-start(bf16[11,128,128]{2,1,0:T(8,128)(2,1)S(1)} %get-tuple-element.26), channel_id=1, source_target_pairs={{1,2},{3,4},{5,6},{7,8},{9,10},{11,12},{13,14},{2,1},{4,3},{6,5},{... | collective-permute-start | bytes 1081352 | tf_op jit(solution)/shard_map/ppermute | solution.py:572
  10.4 9.3 %collective-permute-start.4 = (bf16[11,128,128]{2,1,0:T(8,128)(2,1)S(1)}, bf16[11,128,128]{2,1,0:T(8,128)(2,1)S(1)}, u32[]{:S(2)}, u32[]{:S(2)}) collective-permute-start(bf16[11,128,128]{2,1,0:T(8,128)(2,1)S(1)} %get-tuple-element.28), channel_id=1, source_target_pairs={{0,1},{2,3},{4,5},{6,7},{8,9},{10,11},{12,13},{14,15},{1,0},{3,2},... | collective-permute-start | bytes 1081352 | tf_op jit(solution)/shard_map/ppermute | solution.py:566
  10.4 11.4 %collective-permute-start = (bf16[7,128,128]{2,1,0:T(8,128)(2,1)S(1)}, bf16[7,128,128]{2,1,0:T(8,128)(2,1)S(1)}, u32[]{:S(2)}, u32[]{:S(2)}) collective-permute-start(bf16[7,128,128]{2,1,0:T(8,128)(2,1)S(1)} %get-tuple-element.21), channel_id=1, source_target_pairs={{1,2},{3,4},{5,6},{7,8},{9,10},{11,12},{13,14},{2,1},{4,3},{6,5},{... | collective-permute-start | bytes 688136 | tf_op jit(solution)/shard_map/ppermute | solution.py:572
  16.1 6.8 %collective-permute-start.3 = (bf16[4,128,128]{2,1,0:T(8,128)(2,1)S(1)}, bf16[4,128,128]{2,1,0:T(8,128)(2,1)S(1)}, u32[]{:S(2)}, u32[]{:S(2)}) collective-permute-start(bf16[4,128,128]{2,1,0:T(8,128)(2,1)S(1)} %get-tuple-element.27), channel_id=1, source_target_pairs={{1,2},{3,4},{5,6},{7,8},{9,10},{11,12},{13,14},{2,1},{4,3},{6,5},{... | collective-permute-start | bytes 393224 | tf_op jit(solution)/shard_map/ppermute | solution.py:572

commit v6 on v5

--- a/solution.py
+++ b/solution.py
@@ -528,20 +528,17 @@
     copy.wait()
 
 
-def finish_kernel(geo, meta_ref, early_ref, late_ref, acc_ref, out_in, out_ref, total, sems):
+def join_kernel(geo, packs, meta_ref, got_ref, acc_ref, out_in, out_ref, total, sems):
     def add(up, down):
         copies = []
-        for packs, ref in ((geo.early_packs, early_ref), (geo.late_packs, late_ref)):
-            for start, place, count in packs[0 if up else 1]:
-                spot = pl.ds(len(copies) * geo.band, count)
-                total[spot] = acc_ref[pl.ds(start, count)] + ref[pl.ds(place, count)].astype(
-                    jnp.float32
-                )
-                copy = pltpu.make_async_copy(
-                    total.at[spot], out_ref.at[pl.ds(start, count)], sems.at[len(copies)]
-                )
-                copy.start()
-                copies.append(copy)
+        for start, place, count in packs[0 if up else 1]:
+            spot = pl.ds(place, count)
+            total[spot] = acc_ref[pl.ds(start, count)] + got_ref[spot].astype(jnp.float32)
+            copy = pltpu.make_async_copy(
+                total.at[spot], out_ref.at[pl.ds(start, count)], sems.at[len(copies)]
+            )
+            copy.start()
+            copies.append(copy)
         for copy in copies:
             copy.wait()
 
@@ -650,15 +647,15 @@
         {7: 0},
     )(meta, first, *panel, h, acc)
 
-    parts = 2 * geo.reach
-    out = call(
-        functools.partial(finish_kernel, geo),
-        whole,
-        [SMEM_SPEC] + [VMEM_SPEC] * 3 + [ANY_SPEC],
-        ANY_SPEC,
-        [pltpu.VMEM((parts * band, nb, nb), jnp.float32), dma((parts,))],
-        {4: 0},
-    )(meta, early, late, acc, out)
+    for packs, got in ((geo.early_packs, early), (geo.late_packs, late)):
+        out = call(
+            functools.partial(join_kernel, geo, packs),
+            whole,
+            [SMEM_SPEC] + [VMEM_SPEC] * 2 + [ANY_SPEC],
+            ANY_SPEC,
+            [pltpu.VMEM(got.shape, jnp.float32), dma((geo.reach,))],
+            {3: 0},
+        )(meta, got, acc, out)
     return out.reshape(rows, band, nb, nb)
 
 

time: 24.2 us -> 24 us (level)
  the two profiles are of different devices: /device:TPU:1 before, /device:TPU:6 now
where the time goes in v6:
time: 24 us; the launch traced here: 23.9 us
  Pallas kernels  11.4 us (48%)
  starting transfers between devices  8.01 us (33%)
  waiting for transfers between devices  4.28 us (18%)
    ppermute x3, starting transfers between devices, to_second(): got = lax.ppermute(x, 'blk', pairs + [(j, i) for i, j in pairs])  6.46 us
    ppermute x3, waiting for transfers between devices, to_second(): got = lax.ppermute(x, 'blk', pairs + [(j, i) for i, j in pairs])  4.28 us
    pallas_call x1, Pallas kernels, local(): call(functools.partial(inner_kernel, geo), (acc_type, whole), [SMEM_SPEC]...  2.13 us
    pallas_call x1, Pallas kernels, local(): call(functools.partial(near_kernel, geo), (acc_type, pack(geo.halo)), [SM...  2.12 us
    pallas_call x1, Pallas kernels, local(): call(functools.partial(early_kernel, geo), (acc_type, pack(geo.early)), [...  1.85 us
    ppermute x2, starting transfers between devices, to_first(): got = lax.ppermute(x, 'blk', pairs + [(j, i) for i, j in pairs])  1.54 us
    pallas_call x2, Pallas kernels, local(): call(functools.partial(join_kernel, geo, packs), whole, [SMEM_SPEC] + [VM...  1.54 us
    pallas_call x1, Pallas kernels, local(): call(functools.partial(pack_kernel, geo), (pack(geo.halo),) * 2 + (pltpu....  1.42 us
  transfers between devices with their start and end apart: 5, of which 2 were waited for; matrix products, arithmetic and copies ran while one was open for 0% of the time, Pallas kernels for 39%

profile of v6, /device:TPU:6, one launch (start us, length us, event | category | flops | bytes accessed | tf_op | source)
XLA Modules:
  0.0 23.9 jit_solution(14534925980361681872)
XLA Ops:
  0.0 0.0 copy-start
  0.0 0.0 copy-start.1
  0.0 0.0 copy-start.2
  0.0 0.0 copy-start.3
  0.0 1.4 %shard_map.73 = (bf16[11,128,128]{2,1,0:T(8,128)(2,1)S(1)}, bf16[11,128,128]{2,1,0:T(8,128)(2,1)S(1)}, s32[178]{0:T(256)S(4)}, f32[91,128,128]{2,1,0:T(8,128)S(1)}) custom-call(bf16[72,128,128]{2,1,0:T(8,128)(2,1)} %bitcast.3, s32[12]{0:T(128)} %centre_in.1, s32[4,12]{1,0:T(4,128)} %bitcast.8, s32[12]{0:T(128)} %counts_in.1), custom_call_target="tpu_custom_call" | custom-call | flops 10000000000 | bytes 100000000 | tf_op jit(solution)/shard_map/pallas_call | solution.py:584
  1.5 0.1 collective-permute-start
  1.5 2.6 %collective-permute-start.1 = (bf16[11,128,128]{2,1,0:T(8,128)(2,1)S(1)}, bf16[11,128,128]{2,1,0:T(8,128)(2,1)S(1)}, u32[]{:S(2)}, u32[]{:S(2)}) collective-permute-start(bf16[11,128,128]{2,1,0:T(8,128)(2,1)S(1)} %get-tuple-element.25), channel_id=1, source_target_pairs={{1,2},{3,4},{5,6},{7,8},{9,10},{11,12},{13,14},{2,1},{4,3},{6,5},{... | collective-permute-start | bytes 1081352 | tf_op jit(solution)/shard_map/ppermute | solution.py:569
  4.2 0.0 copy-done
  4.2 0.0 copy-done.1
  4.2 0.0 copy-done.2
  4.2 0.0 copy-done.3
  4.2 1.8 %shard_map.74 = (f32[91,128,128]{2,1,0:T(8,128)S(1)}, bf16[7,128,128]{2,1,0:T(8,128)(2,1)S(1)}) custom-call(s32[178]{0:T(256)S(4)} %get-tuple-element.19.meta_ref, bf16[72,128,128]{2,1,0:T(8,128)(2,1)S(1)} %bitcast.4, bf16[12,4,128,256]{3,2,1,0:T(8,128)(2,1)S(1)} %copy-done, bf16[12,256,256]{2,1,0:T(8,128)(2,1)S(1)} %copy-done.1, ...), custom_call_target="tpu_custom_call", output_to_operand_aliasing={{0}: (5, {})} | custom-call | tf_op jit(solution)/shard_map/pallas_call | solution.py:601
  6.1 0.0 collective-permute-done.halo_ref
  6.1 2.1 %shard_map.75 = (f32[91,128,128]{2,1,0:T(8,128)S(1)}, bf16[11,128,128]{2,1,0:T(8,128)(2,1)S(1)}) custom-call(s32[178]{0:T(256)S(4)} %get-tuple-element.19.meta_ref, bf16[11,128,128]{2,1,0:T(8,128)(2,1)S(1)} %collective-permute-done.halo_ref, bf16[72,128,128]{2,1,0:T(8,128)(2,1)S(1)} %bitcast.5, ...), custom_call_target="tpu_custom_call", output_to_operand_aliasing={{0}: (6, {})} | custom-call | tf_op jit(solution)/shard_map/pallas_call | solution.py:611
  8.2 1.5 %collective-permute-start.3 = (bf16[11,128,128]{2,1,0:T(8,128)(2,1)S(1)}, bf16[11,128,128]{2,1,0:T(8,128)(2,1)S(1)}, u32[]{:S(2)}, u32[]{:S(2)}) collective-permute-start(bf16[11,128,128]{2,1,0:T(8,128)(2,1)S(1)} %get-tuple-element.27), channel_id=1, source_target_pairs={{0,1},{2,3},{4,5},{6,7},{8,9},{10,11},{12,13},{14,15},{1,0},{3,2},... | collective-permute-start | bytes 1081352 | tf_op jit(solution)/shard_map/ppermute | solution.py:563
  9.7 1.9 %collective-permute-start.4 = (bf16[7,128,128]{2,1,0:T(8,128)(2,1)S(1)}, bf16[7,128,128]{2,1,0:T(8,128)(2,1)S(1)}, u32[]{:S(2)}, u32[]{:S(2)}) collective-permute-start(bf16[7,128,128]{2,1,0:T(8,128)(2,1)S(1)} %get-tuple-element.31), channel_id=1, source_target_pairs={{1,2},{3,4},{5,6},{7,8},{9,10},{11,12},{13,14},{2,1},{4,3},{6,5},{... | collective-permute-start | bytes 688136 | tf_op jit(solution)/shard_map/ppermute | solution.py:569
  11.6 1.3 %shard_map.76 = (f32[91,128,128]{2,1,0:T(8,128)S(1)}, s32[1]{0:T(128)S(4)}) custom-call(s32[178]{0:T(256)S(4)} %get-tuple-element.19.meta_ref, bf16[72,128,128]{2,1,0:T(8,128)(2,1)S(1)} %bitcast.6, bf16[12,4,128,256]{3,2,1,0:T(8,128)(2,1)S(1)} %copy-done, bf16[12,256,256]{2,1,0:T(8,128)(2,1)S(1)} %copy-done.1, ...), custom_call_target="tpu_custom_call", output_to_operand_aliasing={{0}: (5, {})} | custom-call | tf_op jit(solution)/shard_map/pallas_call | solution.py:621
  12.9 1.5 %collective-permute-done.1.halo_ref = bf16[11,128,128]{2,1,0:T(8,128)(2,1)S(1)} collective-permute-done((bf16[11,128,128]{2,1,0:T(8,128)(2,1)S(1)}, bf16[11,128,128]{2,1,0:T(8,128)(2,1)S(1)}, u32[]{:S(2)}, u32[]{:S(2)}) %collective-permute-start.1) | collective-permute-done | bytes 360480 | tf_op jit(solution)/shard_map/ppermute | solution.py:569
  14.4 1.0 %shard_map.77 = (bf16[13,256,256]{2,1,0:T(8,128)(2,1)S(1)}, bf16[4,128,128]{2,1,0:T(8,128)(2,1)S(1)}) custom-call(s32[178]{0:T(256)S(4)} %get-tuple-element.19.meta_ref, s32[1]{0:T(128)S(4)} %get-tuple-element.24.done_ref, bf16[11,128,128]{2,1,0:T(8,128)(2,1)S(1)} %collective-permute-done.1.halo_ref, bf16[12,4,128,256]{3,2,1,0:T(8,128)(2,1)S(1)} %copy-done, ...), custom_call_target="tpu_custom_call" | custom-call | tf_op jit(solution)/shard_map/pallas_call | solution.py:631
  15.4 1.9 %collective-permute-start.2 = (bf16[4,128,128]{2,1,0:T(8,128)(2,1)S(1)}, bf16[4,128,128]{2,1,0:T(8,128)(2,1)S(1)}, u32[]{:S(2)}, u32[]{:S(2)}) collective-permute-start(bf16[4,128,128]{2,1,0:T(8,128)(2,1)S(1)} %get-tuple-element.26), channel_id=1, source_target_pairs={{1,2},{3,4},{5,6},{7,8},{9,10},{11,12},{13,14},{2,1},{4,3},{6,5},{... | collective-permute-start | bytes 393224 | tf_op jit(solution)/shard_map/ppermute | solution.py:569
  17.4 0.0 collective-permute-done.3.first_ref
  17.4 2.1 %shard_map.78 = (f32[91,128,128]{2,1,0:T(8,128)S(1)}, f32[72,128,128]{2,1,0:T(8,128)}) custom-call(s32[178]{0:T(256)S(4)} %get-tuple-element.19.meta_ref, bf16[11,128,128]{2,1,0:T(8,128)(2,1)S(1)} %collective-permute-done.3.first_ref, bf16[72,128,128]{2,1,0:T(8,128)(2,1)S(1)} %bitcast.7, ...), custom_call_target="tpu_custom_call", output_to_operand_aliasing={{0}: (7, {})} | custom-call | tf_op jit(solution)/shard_map/pallas_call | solution.py:641
  19.5 0.0 collective-permute-done.4.got_ref
  19.5 0.8 %shard_map.79.out_in = f32[72,128,128]{2,1,0:T(8,128)} custom-call(s32[178]{0:T(256)S(4)} %get-tuple-element.19.meta_ref, bf16[7,128,128]{2,1,0:T(8,128)(2,1)S(1)} %collective-permute-done.4.got_ref, f32[91,128,128]{2,1,0:T(8,128)S(1)} %get-tuple-element.30.acc_ref, f32[72,128,128]{2,1,0:T(8,128)} %get-tuple-element.32.out_in), custom_call_target="tpu_custom_call", output_to_operand_aliasing={{}: (3, {})} | custom-call | tf_op jit(solution)/shard_map/pallas_call | solution.py:651
  20.4 2.8 %collective-permute-done.2.got_ref = bf16[4,128,128]{2,1,0:T(8,128)(2,1)S(1)} collective-permute-done((bf16[4,128,128]{2,1,0:T(8,128)(2,1)S(1)}, bf16[4,128,128]{2,1,0:T(8,128)(2,1)S(1)}, u32[]{:S(2)}, u32[]{:S(2)}) %collective-permute-start.2) | collective-permute-done | bytes 131104 | tf_op jit(solution)/shard_map/ppermute | solution.py:569
  23.1 0.7 %shard_map.80 = f32[72,128,128]{2,1,0:T(8,128)} custom-call(s32[178]{0:T(256)S(4)} %get-tuple-element.19.meta_ref, bf16[4,128,128]{2,1,0:T(8,128)(2,1)S(1)} %collective-permute-done.2.got_ref, f32[91,128,128]{2,1,0:T(8,128)S(1)} %get-tuple-element.30.acc_ref, f32[72,128,128]{2,1,0:T(8,128)} %shard_map.79.out_in), custom_call_target="tpu_custom_call", output_to_operand_aliasing={{}: (3, {})} | custom-call | tf_op jit(solution)/shard_map/pallas_call | solution.py:651
Async XLA Ops:
  0.0 4.2 %copy-start = (bf16[12,4,128,256]{3,2,1,0:T(8,128)(2,1)S(1)}, bf16[12,4,128,256]{3,2,1,0:T(8,128)(2,1)}, u32[]{:S(2)}) copy-start(bf16[12,4,128,256]{3,2,1,0:T(8,128)(2,1)} %ao_ref.9) | copy-start | bytes 9437188
  0.0 4.2 %copy-start.1 = (bf16[12,256,256]{2,1,0:T(8,128)(2,1)S(1)}, bf16[12,256,256]{2,1,0:T(8,128)(2,1)}, u32[]{:S(2)}) copy-start(bf16[12,256,256]{2,1,0:T(8,128)(2,1)} %kernel_ref.9) | copy-start | bytes 4718596
  0.0 4.2 %copy-start.2 = (bf16[8,9,128,128]{3,2,1,0:T(8,128)(2,1)S(1)}, bf16[8,9,128,128]{3,2,1,0:T(8,128)(2,1)}, u32[]{:S(2)}) copy-start(bf16[8,9,128,128]{3,2,1,0:T(8,128)(2,1)} %param.7) | copy-start | bytes 7077892
  0.0 4.2 %copy-start.3 = (f32[12,256]{1,0:T(8,128)S(1)}, f32[12,256]{1,0:T(8,128)}, u32[]{:S(2)}) copy-start(f32[12,256]{1,0:T(8,128)} %weights_ref.9) | copy-start | bytes 36868
  1.5 4.6 %collective-permute-start = (bf16[11,128,128]{2,1,0:T(8,128)(2,1)S(1)}, bf16[11,128,128]{2,1,0:T(8,128)(2,1)S(1)}, u32[]{:S(2)}, u32[]{:S(2)}) collective-permute-start(bf16[11,128,128]{2,1,0:T(8,128)(2,1)S(1)} %get-tuple-element.20), channel_id=1, source_target_pairs={{0,1},{2,3},{4,5},{6,7},{8,9},{10,11},{12,13},{14,15},{1,0},{3,2},... | collective-permute-start | bytes 1081352 | tf_op jit(solution)/shard_map/ppermute | solution.py:563
  1.5 12.9 %collective-permute-start.1 = (bf16[11,128,128]{2,1,0:T(8,128)(2,1)S(1)}, bf16[11,128,128]{2,1,0:T(8,128)(2,1)S(1)}, u32[]{:S(2)}, u32[]{:S(2)}) collective-permute-start(bf16[11,128,128]{2,1,0:T(8,128)(2,1)S(1)} %get-tuple-element.25), channel_id=1, source_target_pairs={{1,2},{3,4},{5,6},{7,8},{9,10},{11,12},{13,14},{2,1},{4,3},{6,5},{... | collective-permute-start | bytes 1081352 | tf_op jit(solution)/shard_map/ppermute | solution.py:569
  8.2 9.2 %collective-permute-start.3 = (bf16[11,128,128]{2,1,0:T(8,128)(2,1)S(1)}, bf16[11,128,128]{2,1,0:T(8,128)(2,1)S(1)}, u32[]{:S(2)}, u32[]{:S(2)}) collective-permute-start(bf16[11,128,128]{2,1,0:T(8,128)(2,1)S(1)} %get-tuple-element.27), channel_id=1, source_target_pairs={{0,1},{2,3},{4,5},{6,7},{8,9},{10,11},{12,13},{14,15},{1,0},{3,2},... | collective-permute-start | bytes 1081352 | tf_op jit(solution)/shard_map/ppermute | solution.py:563
  9.7 9.8 %collective-permute-start.4 = (bf16[7,128,128]{2,1,0:T(8,128)(2,1)S(1)}, bf16[7,128,128]{2,1,0:T(8,128)(2,1)S(1)}, u32[]{:S(2)}, u32[]{:S(2)}) collective-permute-start(bf16[7,128,128]{2,1,0:T(8,128)(2,1)S(1)} %get-tuple-element.31), channel_id=1, source_target_pairs={{1,2},{3,4},{5,6},{7,8},{9,10},{11,12},{13,14},{2,1},{4,3},{6,5},{... | collective-permute-start | bytes 688136 | tf_op jit(solution)/shard_map/ppermute | solution.py:569
  15.4 7.7 %collective-permute-start.2 = (bf16[4,128,128]{2,1,0:T(8,128)(2,1)S(1)}, bf16[4,128,128]{2,1,0:T(8,128)(2,1)S(1)}, u32[]{:S(2)}, u32[]{:S(2)}) collective-permute-start(bf16[4,128,128]{2,1,0:T(8,128)(2,1)S(1)} %get-tuple-element.26), channel_id=1, source_target_pairs={{1,2},{3,4},{5,6},{7,8},{9,10},{11,12},{13,14},{2,1},{4,3},{6,5},{... | collective-permute-start | bytes 393224 | tf_op jit(solution)/shard_map/ppermute | solution.py:569

commit v7 on v5

--- a/solution.py
+++ b/solution.py
@@ -218,23 +218,20 @@
     for which, width, bounds in zip(
         (INNER_MANY, INNER_FEW), (geo.slots, 2), inner_share(geo, meta_ref)
     ):
-        each_group(
-            geo,
-            meta_ref,
-            which,
-            lambda chosen, width=width: add_whole(geo, chosen, width, *refs),
-            begin=bounds[stage],
-            end=bounds[stage + 1],
-        )
-
-
-def each_group(geo, meta_ref, which, body, size=GROUP, begin=0, end=None):
+        work = lambda chosen, width=width: add_whole(geo, chosen, width, *refs)
+        begin, end = bounds[stage], bounds[stage + 1]
+        pairs = (end - begin) // 2
+        each_group(geo, meta_ref, which, work, size=2 * GROUP, end=pairs, skip=begin * GROUP)
+        each_group(geo, meta_ref, which, work, begin=begin + 2 * pairs, end=end)
+
+
+def each_group(geo, meta_ref, which, body, size=GROUP, begin=0, end=None, skip=0):
     length = meta_ref[geo.lengths_at + which]
 
     def step(i, carry):
         chosen = []
         for n in range(size):
-            place = i * size + n
+            place = skip + i * size + n
             there = place < length
             b = meta_ref[which * geo.list_size + jnp.minimum(place, length)]
             chosen.append((jnp.where(there, b, 0), there))

time: 24.2 us -> 24.6 us (1.017)
  Pallas kernels: 10.5 us -> 11.1 us
    pallas_call x1, Pallas kernels: 1.3 us -> 1.72 us  [local(): call(functools.partial(waiting_kernel, geo), (acc_type, pltpu.SMEM((1,),...]
  transfers between devices with their start and end apart: 5 -> 5, of which waited for: 1 -> 1; matrix products, arithmetic and copies ran while one was open for 0% -> 0% of each run, Pallas kernels for 34% -> 36%
where the time goes in v7:
time: 24.6 us; the launch traced here: 24.4 us
  starting transfers between devices  11.9 us (48%)
  Pallas kernels  11.1 us (45%)
  waiting for transfers between devices  0.96 us (4%)
  between operations  0.32 us (1%)
    ppermute x3, starting transfers between devices, to_second(): got = lax.ppermute(x, 'blk', pairs + [(j, i) for i, j in pairs])  11.8 us
    pallas_call x1, Pallas kernels, local(): call(functools.partial(near_kernel, geo), (acc_type, pack(geo.halo)), [SM...  2.76 us
    pallas_call x1, Pallas kernels, local(): call(functools.partial(inner_kernel, geo), (acc_type, whole), [SMEM_SPEC]...  2.15 us
    pallas_call x1, Pallas kernels, local(): call(functools.partial(waiting_kernel, geo), (acc_type, pltpu.SMEM((1,),...  1.72 us
    pallas_call x1, Pallas kernels, local(): call(functools.partial(pack_kernel, geo), (pack(geo.halo),) * 2 + (pltpu....  1.43 us
    pallas_call x1, Pallas kernels, local(): call(functools.partial(early_kernel, geo), (acc_type, pack(geo.early)), [...  1.23 us
    ppermute x3, waiting for transfers between devices, to_second(): got = lax.ppermute(x, 'blk', pairs + [(j, i) for i, j in pairs])  0.95 us
    pallas_call x1, Pallas kernels, local(): call(functools.partial(late_kernel, geo), (h_type, pack(geo.late)), [SMEM...  0.93 us
  transfers between devices with their start and end apart: 5, of which 1 were waited for; matrix products, arithmetic and copies ran while one was open for 0% of the time, Pallas kernels for 36%

profile of v7, /device:TPU:1, one launch (start us, length us, event | category | flops | bytes accessed | tf_op | source)
XLA Modules:
  0.0 24.4 jit_solution(11845364226937677073)
XLA Ops:
  0.0 0.0 copy-start
  0.0 0.0 copy-start.1
  0.0 0.0 copy-start.2
  0.0 0.0 copy-start.3
  0.0 1.4 %shard_map.73 = (bf16[11,128,128]{2,1,0:T(8,128)(2,1)S(1)}, bf16[11,128,128]{2,1,0:T(8,128)(2,1)S(1)}, s32[178]{0:T(256)S(4)}, f32[91,128,128]{2,1,0:T(8,128)S(1)}) custom-call(bf16[72,128,128]{2,1,0:T(8,128)(2,1)} %bitcast.3, s32[12]{0:T(128)} %centre_in.1, s32[4,12]{1,0:T(4,128)} %bitcast.8, s32[12]{0:T(128)} %counts_in.1), custom_call_target="tpu_custom_call" | custom-call | flops 10000000000 | bytes 100000000 | tf_op jit(solution)/shard_map/pallas_call | solution.py:584
  1.5 0.1 collective-permute-start.1
  1.6 4.8 %collective-permute-start.2 = (bf16[11,128,128]{2,1,0:T(8,128)(2,1)S(1)}, bf16[11,128,128]{2,1,0:T(8,128)(2,1)S(1)}, u32[]{:S(2)}, u32[]{:S(2)}) collective-permute-start(bf16[11,128,128]{2,1,0:T(8,128)(2,1)S(1)} %get-tuple-element.26), channel_id=1, source_target_pairs={{1,2},{3,4},{5,6},{7,8},{9,10},{11,12},{13,14},{2,1},{4,3},{6,5},{... | collective-permute-start | bytes 1081352 | tf_op jit(solution)/shard_map/ppermute | solution.py:569
  6.3 0.0 copy-done
  6.3 0.0 copy-done.1
  6.4 0.0 copy-done.2
  6.4 0.0 copy-done.3
  6.4 1.2 %shard_map.74 = (f32[91,128,128]{2,1,0:T(8,128)S(1)}, bf16[7,128,128]{2,1,0:T(8,128)(2,1)S(1)}) custom-call(s32[178]{0:T(256)S(4)} %get-tuple-element.19.meta_ref, bf16[72,128,128]{2,1,0:T(8,128)(2,1)S(1)} %bitcast.4, bf16[12,4,128,256]{3,2,1,0:T(8,128)(2,1)S(1)} %copy-done, bf16[12,256,256]{2,1,0:T(8,128)(2,1)S(1)} %copy-done.1, ...), custom_call_target="tpu_custom_call", output_to_operand_aliasing={{0}: (5, {})} | custom-call | tf_op jit(solution)/shard_map/pallas_call | solution.py:601
  7.6 0.0 collective-permute-done.1.halo_ref
  7.6 2.8 %shard_map.75 = (f32[91,128,128]{2,1,0:T(8,128)S(1)}, bf16[11,128,128]{2,1,0:T(8,128)(2,1)S(1)}) custom-call(s32[178]{0:T(256)S(4)} %get-tuple-element.19.meta_ref, bf16[11,128,128]{2,1,0:T(8,128)(2,1)S(1)} %collective-permute-done.1.halo_ref, bf16[72,128,128]{2,1,0:T(8,128)(2,1)S(1)} %bitcast.5, ...), custom_call_target="tpu_custom_call", output_to_operand_aliasing={{0}: (6, {})} | custom-call | tf_op jit(solution)/shard_map/pallas_call | solution.py:611
  10.4 0.1 collective-permute-start.4
  10.5 3.5 %collective-permute-start = (bf16[7,128,128]{2,1,0:T(8,128)(2,1)S(1)}, bf16[7,128,128]{2,1,0:T(8,128)(2,1)S(1)}, u32[]{:S(2)}, u32[]{:S(2)}) collective-permute-start(bf16[7,128,128]{2,1,0:T(8,128)(2,1)S(1)} %get-tuple-element.21), channel_id=1, source_target_pairs={{1,2},{3,4},{5,6},{7,8},{9,10},{11,12},{13,14},{2,1},{4,3},{6,5},{... | collective-permute-start | bytes 688136 | tf_op jit(solution)/shard_map/ppermute | solution.py:569
  14.0 1.7 %shard_map.76 = (f32[91,128,128]{2,1,0:T(8,128)S(1)}, s32[1]{0:T(128)S(4)}) custom-call(s32[178]{0:T(256)S(4)} %get-tuple-element.19.meta_ref, bf16[72,128,128]{2,1,0:T(8,128)(2,1)S(1)} %bitcast.6, bf16[12,4,128,256]{3,2,1,0:T(8,128)(2,1)S(1)} %copy-done, bf16[12,256,256]{2,1,0:T(8,128)(2,1)S(1)} %copy-done.1, ...), custom_call_target="tpu_custom_call", output_to_operand_aliasing={{0}: (5, {})} | custom-call | tf_op jit(solution)/shard_map/pallas_call | solution.py:621
  15.7 0.0 collective-permute-done.2.halo_ref
  15.7 0.9 %shard_map.77 = (bf16[13,256,256]{2,1,0:T(8,128)(2,1)S(1)}, bf16[4,128,128]{2,1,0:T(8,128)(2,1)S(1)}) custom-call(s32[178]{0:T(256)S(4)} %get-tuple-element.19.meta_ref, s32[1]{0:T(128)S(4)} %get-tuple-element.25.done_ref, bf16[11,128,128]{2,1,0:T(8,128)(2,1)S(1)} %collective-permute-done.2.halo_ref, bf16[12,4,128,256]{3,2,1,0:T(8,128)(2,1)S(1)} %copy-done, ...), custom_call_target="tpu_custom_call" | custom-call | tf_op jit(solution)/shard_map/pallas_call | solution.py:631
  16.7 3.5 %collective-permute-start.3 = (bf16[4,128,128]{2,1,0:T(8,128)(2,1)S(1)}, bf16[4,128,128]{2,1,0:T(8,128)(2,1)S(1)}, u32[]{:S(2)}, u32[]{:S(2)}) collective-permute-start(bf16[4,128,128]{2,1,0:T(8,128)(2,1)S(1)} %get-tuple-element.27), channel_id=1, source_target_pairs={{1,2},{3,4},{5,6},{7,8},{9,10},{11,12},{13,14},{2,1},{4,3},{6,5},{... | collective-permute-start | bytes 393224 | tf_op jit(solution)/shard_map/ppermute | solution.py:569
  20.2 0.0 collective-permute-done.4.first_ref
  20.2 2.1 %shard_map.78 = (f32[91,128,128]{2,1,0:T(8,128)S(1)}, f32[72,128,128]{2,1,0:T(8,128)}) custom-call(s32[178]{0:T(256)S(4)} %get-tuple-element.19.meta_ref, bf16[11,128,128]{2,1,0:T(8,128)(2,1)S(1)} %collective-permute-done.4.first_ref, bf16[72,128,128]{2,1,0:T(8,128)(2,1)S(1)} %bitcast.7, ...), custom_call_target="tpu_custom_call", output_to_operand_aliasing={{0}: (7, {})} | custom-call | tf_op jit(solution)/shard_map/pallas_call | solution.py:641
  22.3 0.0 collective-permute-done.early_ref
  22.3 0.9 %collective-permute-done.3.late_ref = bf16[4,128,128]{2,1,0:T(8,128)(2,1)S(1)} collective-permute-done((bf16[4,128,128]{2,1,0:T(8,128)(2,1)S(1)}, bf16[4,128,128]{2,1,0:T(8,128)(2,1)S(1)}, u32[]{:S(2)}, u32[]{:S(2)}) %collective-permute-start.3) | collective-permute-done | bytes 131104 | tf_op jit(solution)/shard_map/ppermute | solution.py:569
  23.3 0.9 %shard_map.79 = f32[72,128,128]{2,1,0:T(8,128)} custom-call(s32[178]{0:T(256)S(4)} %get-tuple-element.19.meta_ref, bf16[7,128,128]{2,1,0:T(8,128)(2,1)S(1)} %collective-permute-done.early_ref, bf16[4,128,128]{2,1,0:T(8,128)(2,1)S(1)} %collective-permute-done.3.late_ref, ...), custom_call_target="tpu_custom_call", output_to_operand_aliasing={{}: (4, {})} | custom-call | tf_op jit(solution)/shard_map/pallas_call | solution.py:651
Async XLA Ops:
  0.0 6.3 %copy-start = (bf16[12,4,128,256]{3,2,1,0:T(8,128)(2,1)S(1)}, bf16[12,4,128,256]{3,2,1,0:T(8,128)(2,1)}, u32[]{:S(2)}) copy-start(bf16[12,4,128,256]{3,2,1,0:T(8,128)(2,1)} %ao_ref.9) | copy-start | bytes 9437188
  0.0 6.3 %copy-start.1 = (bf16[12,256,256]{2,1,0:T(8,128)(2,1)S(1)}, bf16[12,256,256]{2,1,0:T(8,128)(2,1)}, u32[]{:S(2)}) copy-start(bf16[12,256,256]{2,1,0:T(8,128)(2,1)} %kernel_ref.9) | copy-start | bytes 4718596
  0.0 6.4 %copy-start.2 = (bf16[8,9,128,128]{3,2,1,0:T(8,128)(2,1)S(1)}, bf16[8,9,128,128]{3,2,1,0:T(8,128)(2,1)}, u32[]{:S(2)}) copy-start(bf16[8,9,128,128]{3,2,1,0:T(8,128)(2,1)} %param.7) | copy-start | bytes 7077892
  0.0 6.4 %copy-start.3 = (f32[12,256]{1,0:T(8,128)S(1)}, f32[12,256]{1,0:T(8,128)}, u32[]{:S(2)}) copy-start(f32[12,256]{1,0:T(8,128)} %weights_ref.9) | copy-start | bytes 36868
  1.5 6.2 %collective-permute-start.1 = (bf16[11,128,128]{2,1,0:T(8,128)(2,1)S(1)}, bf16[11,128,128]{2,1,0:T(8,128)(2,1)S(1)}, u32[]{:S(2)}, u32[]{:S(2)}) collective-permute-start(bf16[11,128,128]{2,1,0:T(8,128)(2,1)S(1)} %get-tuple-element.22), channel_id=1, source_target_pairs={{0,1},{2,3},{4,5},{6,7},{8,9},{10,11},{12,13},{14,15},{1,0},{3,2},... | collective-permute-start | bytes 1081352 | tf_op jit(solution)/shard_map/ppermute | solution.py:563
  1.6 14.2 %collective-permute-start.2 = (bf16[11,128,128]{2,1,0:T(8,128)(2,1)S(1)}, bf16[11,128,128]{2,1,0:T(8,128)(2,1)S(1)}, u32[]{:S(2)}, u32[]{:S(2)}) collective-permute-start(bf16[11,128,128]{2,1,0:T(8,128)(2,1)S(1)} %get-tuple-element.26), channel_id=1, source_target_pairs={{1,2},{3,4},{5,6},{7,8},{9,10},{11,12},{13,14},{2,1},{4,3},{6,5},{... | collective-permute-start | bytes 1081352 | tf_op jit(solution)/shard_map/ppermute | solution.py:569
  10.4 9.8 %collective-permute-start.4 = (bf16[11,128,128]{2,1,0:T(8,128)(2,1)S(1)}, bf16[11,128,128]{2,1,0:T(8,128)(2,1)S(1)}, u32[]{:S(2)}, u32[]{:S(2)}) collective-permute-start(bf16[11,128,128]{2,1,0:T(8,128)(2,1)S(1)} %get-tuple-element.28), channel_id=1, source_target_pairs={{0,1},{2,3},{4,5},{6,7},{8,9},{10,11},{12,13},{14,15},{1,0},{3,2},... | collective-permute-start | bytes 1081352 | tf_op jit(solution)/shard_map/ppermute | solution.py:563
  10.5 11.9 %collective-permute-start = (bf16[7,128,128]{2,1,0:T(8,128)(2,1)S(1)}, bf16[7,128,128]{2,1,0:T(8,128)(2,1)S(1)}, u32[]{:S(2)}, u32[]{:S(2)}) collective-permute-start(bf16[7,128,128]{2,1,0:T(8,128)(2,1)S(1)} %get-tuple-element.21), channel_id=1, source_target_pairs={{1,2},{3,4},{5,6},{7,8},{9,10},{11,12},{13,14},{2,1},{4,3},{6,5},{... | collective-permute-start | bytes 688136 | tf_op jit(solution)/shard_map/ppermute | solution.py:569
  16.7 6.6 %collective-permute-start.3 = (bf16[4,128,128]{2,1,0:T(8,128)(2,1)S(1)}, bf16[4,128,128]{2,1,0:T(8,128)(2,1)S(1)}, u32[]{:S(2)}, u32[]{:S(2)}) collective-permute-start(bf16[4,128,128]{2,1,0:T(8,128)(2,1)S(1)} %get-tuple-element.27), channel_id=1, source_target_pairs={{1,2},{3,4},{5,6},{7,8},{9,10},{11,12},{13,14},{2,1},{4,3},{6,5},{... | collective-permute-start | bytes 393224 | tf_op jit(solution)/shard_map/ppermute | solution.py:569

commit v8 on v7

--- a/solution.py
+++ b/solution.py
@@ -194,51 +194,54 @@
         copy.wait()
 
 
-def group_count(geo, meta_ref, which):
-    return (meta_ref[geo.lengths_at + which] + GROUP - 1) // GROUP
+def listed(geo, meta_ref, which, skip=0):
+    return lambda place: meta_ref[which * geo.list_size + skip + place]
+
+
+def length_of(geo, meta_ref, which):
+    return meta_ref[geo.lengths_at + which]
+
+
+def groups_in(length):
+    return (length + GROUP - 1) // GROUP
 
 
 def inner_share(geo, meta_ref):
-    before = BUDGET
-    for which in (CROSS_MANY, CROSS_FEW, NEAR_MANY, NEAR_FEW):
-        before = before - COST[which % 2] * group_count(geo, meta_ref, which)
-    waiting = jnp.where((lax.axis_index("blk") + 1) // 2 % 2 == 1, WAIT, 0)
-    share = []
-    for which in (INNER_MANY, INNER_FEW):
-        cost, count = COST[which % 2], group_count(geo, meta_ref, which)
-        first = jnp.minimum(jnp.maximum(before, 0) // cost, count)
-        second = jnp.minimum(jnp.maximum(waiting, 0) // cost, count - first)
-        before = before - cost * first
-        waiting = waiting - cost * second
-        share.append((0, first, first + second, count))
-    return share
-
-
-def inner_part(geo, meta_ref, stage, refs):
-    for which, width, bounds in zip(
-        (INNER_MANY, INNER_FEW), (geo.slots, 2), inner_share(geo, meta_ref)
-    ):
-        work = lambda chosen, width=width: add_whole(geo, chosen, width, *refs)
-        begin, end = bounds[stage], bounds[stage + 1]
-        pairs = (end - begin) // 2
-        each_group(geo, meta_ref, which, work, size=2 * GROUP, end=pairs, skip=begin * GROUP)
-        each_group(geo, meta_ref, which, work, begin=begin + 2 * pairs, end=end)
-
-
-def each_group(geo, meta_ref, which, body, size=GROUP, begin=0, end=None, skip=0):
-    length = meta_ref[geo.lengths_at + which]
-
+    room = BUDGET
+    for which in (CROSS_MANY, CROSS_FEW):
+        room = room - COST[which % 2] * groups_in(length_of(geo, meta_ref, which))
+    room = room - COST[1] * groups_in(length_of(geo, meta_ref, NEAR_FEW))
+    taken = []
+    for near, inner in ((NEAR_MANY, INNER_MANY), (NEAR_FEW, INNER_FEW)):
+        cost = COST[near % 2]
+        near = length_of(geo, meta_ref, near)
+        whole = near + length_of(geo, meta_ref, inner)
+        groups = jnp.maximum(groups_in(near), jnp.maximum(room, 0) // cost)
+        together = jnp.minimum(groups * GROUP, whole)
+        room = room - cost * groups_in(together)
+        taken.append(together - near)
+        room = room + COST[1] * groups_in(length_of(geo, meta_ref, NEAR_FEW))
+    waiting = jnp.where((lax.axis_index("blk") + 1) // 2 % 2 == 1, WAIT // COST[0] * GROUP, 0)
+    rest = length_of(geo, meta_ref, INNER_MANY) - taken[0]
+    return taken[0], taken[1], jnp.minimum(waiting, rest)
+
+
+def each_group(length, get, body, size=GROUP):
     def step(i, carry):
         chosen = []
         for n in range(size):
-            place = skip + i * size + n
+            place = i * size + n
             there = place < length
-            b = meta_ref[which * geo.list_size + jnp.minimum(place, length)]
+            b = get(jnp.where(there, place, 0))
             chosen.append((jnp.where(there, b, 0), there))
         body(chosen)
         return carry
 
-    lax.fori_loop(begin, (length + size - 1) // size if end is None else end, step, 0)
+    lax.fori_loop(0, (length + size - 1) // size, step, 0)
+
+
+def each_listed(geo, meta_ref, which, body, size=GROUP):
+    each_group(length_of(geo, meta_ref, which), listed(geo, meta_ref, which), body, size)
 
 
 class Slots:
@@ -439,7 +442,7 @@
         acc_ref[where] = jnp.zeros_like(acc_ref[where])
     refs = (meta_ref, tiles_ref, ao_ref, kernel_ref, weights_ref, acc_ref)
     for which, width in ((CROSS_MANY, geo.slots), (CROSS_FEW, 2)):
-        each_group(
+        each_listed(
             geo, meta_ref, which, lambda chosen, width=width: add_own(geo, chosen, width, *refs)
         )
     early_out[...] = acc_ref[pl.ds(geo.early_at, geo.early)].astype(early_out.dtype)
@@ -449,18 +452,33 @@
     geo, meta_ref, halo_ref, tiles_ref, ao_ref, kernel_ref, weights_ref, acc_in, acc_ref, first_out
 ):
     refs = (meta_ref, tiles_ref, ao_ref, kernel_ref, weights_ref, acc_ref, halo_ref)
-    for which, width in ((NEAR_MANY, geo.slots), (NEAR_FEW, 2)):
+    many, few, _ = inner_share(geo, meta_ref)
+    for near, inner, taken, width in (
+        (NEAR_MANY, INNER_MANY, many, geo.slots),
+        (NEAR_FEW, INNER_FEW, few, 2),
+    ):
+        length = length_of(geo, meta_ref, near)
+        begin = jnp.int32(inner * geo.list_size) - length
+
+        def get(place, length=length, begin=begin, near=near):
+            return meta_ref[jnp.where(place < length, near * geo.list_size, begin) + place]
+
         each_group(
-            geo, meta_ref, which, lambda chosen, width=width: add_whole(geo, chosen, width, *refs)
+            length + taken, get, lambda chosen, width=width: add_whole(geo, chosen, width, *refs)
         )
     first_out[...] = acc_ref[pl.ds(geo.first_at, geo.halo)].astype(first_out.dtype)
-    inner_part(geo, meta_ref, 0, refs[:-1])
 
 
 def waiting_kernel(
     geo, meta_ref, tiles_ref, ao_ref, kernel_ref, weights_ref, acc_in, acc_ref, done_ref
 ):
-    inner_part(geo, meta_ref, 1, (meta_ref, tiles_ref, ao_ref, kernel_ref, weights_ref, acc_ref))
+    refs = (meta_ref, tiles_ref, ao_ref, kernel_ref, weights_ref, acc_ref)
+    many, _, waiting = inner_share(geo, meta_ref)
+    each_group(
+        waiting,
+        listed(geo, meta_ref, INNER_MANY, many),
+        lambda chosen: add_whole(geo, chosen, geo.slots, *refs),
+    )
     done_ref[0] = 1
 
 
@@ -475,9 +493,7 @@
             geo, chosen, meta_ref, halo_ref, ao_ref, kernel_ref, weights_ref, h_ref, total_ref
         )
 
-    groups = (meta_ref[geo.lengths_at + CROSS] + 1) // LATE_GROUP
-    each_group(geo, meta_ref, CROSS, work, size=LATE_GROUP, end=groups)
-    each_group(geo, meta_ref, CROSS, work, size=LATE_GROUP // 2, begin=2 * groups)
+    each_listed(geo, meta_ref, CROSS, work, LATE_GROUP)
     for i in range(geo.reach):
         for j in range(geo.reach):
             late_out[i * geo.reach + j] = total_ref[
@@ -491,7 +507,13 @@
 ):
     odd = meta_ref[geo.odd_at] == 1
     refs = (meta_ref, tiles_ref, ao_ref, kernel_ref, weights_ref, acc_ref)
-    inner_part(geo, meta_ref, 2, refs)
+    many, few, waiting = inner_share(geo, meta_ref)
+    for which, done, width in ((INNER_MANY, many + waiting, geo.slots), (INNER_FEW, few, 2)):
+        each_group(
+            length_of(geo, meta_ref, which) - done,
+            listed(geo, meta_ref, which, done),
+            lambda chosen, width=width: add_whole(geo, chosen, width, *refs),
+        )
 
     def add_near(up, down):
         for start, place, count in geo.packs[0 if up else 1]:
@@ -502,7 +524,7 @@
     copy = pltpu.make_async_copy(acc_ref.at[done], out_ref.at[done], sems.at[0])
     copy.start()
     for which, width in ((CROSS_MANY, geo.slots), (CROSS_FEW, 2)):
-        each_group(
+        each_listed(
             geo,
             meta_ref,
             which,

time: 24.6 us -> 24.7 us (level); the launches traced: 24.4 us -> 24.9 us
  Pallas kernels: 11.1 us -> 11.8 us
  starting transfers between devices: 11.9 us -> 12.6 us
  waiting for transfers between devices: 0.96 us -> 0.27 us
    pallas_call x1, Pallas kernels: 2.15 us -> 3.96 us  [local(): call(functools.partial(inner_kernel, geo), (acc_type, whole), [SMEM_SPEC]...]
    pallas_call x1, Pallas kernels: 1.72 us -> 0.06 us  [local(): call(functools.partial(waiting_kernel, geo), (acc_type, pltpu.SMEM((1,),...]
    ppermute x3, starting transfers between devices: 11.8 us -> 12.5 us  [to_second(): got = lax.ppermute(x, 'blk', pairs + [(j, i) for i, j in pairs])]
    ppermute x3, waiting for transfers between devices: 0.95 us -> 0.27 us  [to_second(): got = lax.ppermute(x, 'blk', pairs + [(j, i) for i, j in pairs])]
    pallas_call x1, Pallas kernels: 2.76 us -> 3.18 us  [local(): call(functools.partial(near_kernel, geo), (acc_type, pack(geo.halo)), [SM...]
  transfers between devices with their start and end apart: 5 -> 5, of which waited for: 1 -> 1; matrix products, arithmetic and copies ran while one was open for 0% -> 0% of each run, Pallas kernels for 36% -> 38%
where the time goes in v8:
time: 24.7 us; the launch traced here: 24.9 us
  starting transfers between devices  12.6 us (51%)
  Pallas kernels  11.8 us (48%)
  waiting for transfers between devices  0.27 us (1%)
    ppermute x3, starting transfers between devices, to_second(): got = lax.ppermute(x, 'blk', pairs + [(j, i) for i, j in pairs])  12.5 us
    pallas_call x1, Pallas kernels, local(): call(functools.partial(inner_kernel, geo), (acc_type, whole), [SMEM_SPEC]...  3.96 us
    pallas_call x1, Pallas kernels, local(): call(functools.partial(near_kernel, geo), (acc_type, pack(geo.halo)), [SM...  3.18 us
    pallas_call x1, Pallas kernels, local(): call(functools.partial(pack_kernel, geo), (pack(geo.halo),) * 2 + (pltpu....  1.43 us
    pallas_call x1, Pallas kernels, local(): call(functools.partial(early_kernel, geo), (acc_type, pack(geo.early)), [...  1.24 us
    pallas_call x1, Pallas kernels, local(): call(functools.partial(late_kernel, geo), (h_type, pack(geo.late)), [SMEM...  1.02 us
    pallas_call x1, Pallas kernels, local(): call(functools.partial(finish_kernel, geo), whole, [SMEM_SPEC] + [VMEM_SP...  0.92 us
  transfers between devices with their start and end apart: 5, of which 1 were waited for; matrix products, arithmetic and copies ran while one was open for 0% of the time, Pallas kernels for 38%

profile of v8, /device:TPU:1, one launch (start us, length us, event | category | flops | bytes accessed | tf_op | source)
XLA Modules:
  0.0 24.9 jit_solution(10687010364926055152)
XLA Ops:
  0.0 0.0 copy-start
  0.0 0.0 copy-start.1
  0.0 0.0 copy-start.2
  0.0 0.0 copy-start.3
  0.0 1.4 %shard_map.73 = (bf16[11,128,128]{2,1,0:T(8,128)(2,1)S(1)}, bf16[11,128,128]{2,1,0:T(8,128)(2,1)S(1)}, s32[178]{0:T(256)S(4)}, f32[91,128,128]{2,1,0:T(8,128)S(1)}) custom-call(bf16[72,128,128]{2,1,0:T(8,128)(2,1)} %bitcast.3, s32[12]{0:T(128)} %centre_in.1, s32[4,12]{1,0:T(4,128)} %bitcast.8, s32[12]{0:T(128)} %counts_in.1), custom_call_target="tpu_custom_call" | custom-call | flops 10000000000 | bytes 100000000 | tf_op jit(solution)/shard_map/pallas_call | solution.py:606
  1.5 0.1 collective-permute-start.1
  1.6 4.8 %collective-permute-start.2 = (bf16[11,128,128]{2,1,0:T(8,128)(2,1)S(1)}, bf16[11,128,128]{2,1,0:T(8,128)(2,1)S(1)}, u32[]{:S(2)}, u32[]{:S(2)}) collective-permute-start(bf16[11,128,128]{2,1,0:T(8,128)(2,1)S(1)} %get-tuple-element.26), channel_id=1, source_target_pairs={{1,2},{3,4},{5,6},{7,8},{9,10},{11,12},{13,14},{2,1},{4,3},{6,5},{... | collective-permute-start | bytes 1081352 | tf_op jit(solution)/shard_map/ppermute | solution.py:591
  6.3 0.0 copy-done
  6.3 0.0 copy-done.1
  6.4 0.0 copy-done.2
  6.4 0.0 copy-done.3
  6.4 1.2 %shard_map.74 = (f32[91,128,128]{2,1,0:T(8,128)S(1)}, bf16[7,128,128]{2,1,0:T(8,128)(2,1)S(1)}) custom-call(s32[178]{0:T(256)S(4)} %get-tuple-element.19.meta_ref, bf16[72,128,128]{2,1,0:T(8,128)(2,1)S(1)} %bitcast.4, bf16[12,4,128,256]{3,2,1,0:T(8,128)(2,1)S(1)} %copy-done, bf16[12,256,256]{2,1,0:T(8,128)(2,1)S(1)} %copy-done.1, ...), custom_call_target="tpu_custom_call", output_to_operand_aliasing={{0}: (5, {})} | custom-call | tf_op jit(solution)/shard_map/pallas_call | solution.py:623
  7.6 0.0 collective-permute-done.1.halo_ref
  7.6 3.2 %shard_map.75 = (f32[91,128,128]{2,1,0:T(8,128)S(1)}, bf16[11,128,128]{2,1,0:T(8,128)(2,1)S(1)}) custom-call(s32[178]{0:T(256)S(4)} %get-tuple-element.19.meta_ref, bf16[11,128,128]{2,1,0:T(8,128)(2,1)S(1)} %collective-permute-done.1.halo_ref, bf16[72,128,128]{2,1,0:T(8,128)(2,1)S(1)} %bitcast.5, ...), custom_call_target="tpu_custom_call", output_to_operand_aliasing={{0}: (6, {})} | custom-call | tf_op jit(solution)/shard_map/pallas_call | solution.py:633
  10.8 0.1 collective-permute-start.4
  10.9 3.3 %collective-permute-start = (bf16[7,128,128]{2,1,0:T(8,128)(2,1)S(1)}, bf16[7,128,128]{2,1,0:T(8,128)(2,1)S(1)}, u32[]{:S(2)}, u32[]{:S(2)}) collective-permute-start(bf16[7,128,128]{2,1,0:T(8,128)(2,1)S(1)} %get-tuple-element.21), channel_id=1, source_target_pairs={{1,2},{3,4},{5,6},{7,8},{9,10},{11,12},{13,14},{2,1},{4,3},{6,5},{... | collective-permute-start | bytes 688136 | tf_op jit(solution)/shard_map/ppermute | solution.py:591
  14.2 0.1 shard_map.76
  14.3 0.3 %collective-permute-done.2.halo_ref = bf16[11,128,128]{2,1,0:T(8,128)(2,1)S(1)} collective-permute-done((bf16[11,128,128]{2,1,0:T(8,128)(2,1)S(1)}, bf16[11,128,128]{2,1,0:T(8,128)(2,1)S(1)}, u32[]{:S(2)}, u32[]{:S(2)}) %collective-permute-start.2) | collective-permute-done | bytes 360480 | tf_op jit(solution)/shard_map/ppermute | solution.py:591
  14.6 1.0 %shard_map.77 = (bf16[13,256,256]{2,1,0:T(8,128)(2,1)S(1)}, bf16[4,128,128]{2,1,0:T(8,128)(2,1)S(1)}) custom-call(s32[178]{0:T(256)S(4)} %get-tuple-element.19.meta_ref, s32[1]{0:T(128)S(4)} %get-tuple-element.25.done_ref, bf16[11,128,128]{2,1,0:T(8,128)(2,1)S(1)} %collective-permute-done.2.halo_ref, bf16[12,4,128,256]{3,2,1,0:T(8,128)(2,1)S(1)} %copy-done, ...), custom_call_target="tpu_custom_call" | custom-call | tf_op jit(solution)/shard_map/pallas_call | solution.py:653
  15.6 4.4 %collective-permute-start.3 = (bf16[4,128,128]{2,1,0:T(8,128)(2,1)S(1)}, bf16[4,128,128]{2,1,0:T(8,128)(2,1)S(1)}, u32[]{:S(2)}, u32[]{:S(2)}) collective-permute-start(bf16[4,128,128]{2,1,0:T(8,128)(2,1)S(1)} %get-tuple-element.27), channel_id=1, source_target_pairs={{1,2},{3,4},{5,6},{7,8},{9,10},{11,12},{13,14},{2,1},{4,3},{6,5},{... | collective-permute-start | bytes 393224 | tf_op jit(solution)/shard_map/ppermute | solution.py:591
  20.0 0.0 collective-permute-done.4.first_ref
  20.0 4.0 %shard_map.78 = (f32[91,128,128]{2,1,0:T(8,128)S(1)}, f32[72,128,128]{2,1,0:T(8,128)}) custom-call(s32[178]{0:T(256)S(4)} %get-tuple-element.19.meta_ref, bf16[11,128,128]{2,1,0:T(8,128)(2,1)S(1)} %collective-permute-done.4.first_ref, bf16[72,128,128]{2,1,0:T(8,128)(2,1)S(1)} %bitcast.7, ...), custom_call_target="tpu_custom_call", output_to_operand_aliasing={{0}: (7, {})} | custom-call | tf_op jit(solution)/shard_map/pallas_call | solution.py:663
  24.0 0.0 collective-permute-done.early_ref
  24.0 0.0 collective-permute-done.3.late_ref
  24.0 0.9 %shard_map.79 = f32[72,128,128]{2,1,0:T(8,128)} custom-call(s32[178]{0:T(256)S(4)} %get-tuple-element.19.meta_ref, bf16[7,128,128]{2,1,0:T(8,128)(2,1)S(1)} %collective-permute-done.early_ref, bf16[4,128,128]{2,1,0:T(8,128)(2,1)S(1)} %collective-permute-done.3.late_ref, ...), custom_call_target="tpu_custom_call", output_to_operand_aliasing={{}: (4, {})} | custom-call | tf_op jit(solution)/shard_map/pallas_call | solution.py:673
Async XLA Ops:
  0.0 6.3 %copy-start = (bf16[12,4,128,256]{3,2,1,0:T(8,128)(2,1)S(1)}, bf16[12,4,128,256]{3,2,1,0:T(8,128)(2,1)}, u32[]{:S(2)}) copy-start(bf16[12,4,128,256]{3,2,1,0:T(8,128)(2,1)} %ao_ref.9) | copy-start | bytes 9437188
  0.0 6.3 %copy-start.1 = (bf16[12,256,256]{2,1,0:T(8,128)(2,1)S(1)}, bf16[12,256,256]{2,1,0:T(8,128)(2,1)}, u32[]{:S(2)}) copy-start(bf16[12,256,256]{2,1,0:T(8,128)(2,1)} %kernel_ref.9) | copy-start | bytes 4718596
  0.0 6.4 %copy-start.2 = (bf16[8,9,128,128]{3,2,1,0:T(8,128)(2,1)S(1)}, bf16[8,9,128,128]{3,2,1,0:T(8,128)(2,1)}, u32[]{:S(2)}) copy-start(bf16[8,9,128,128]{3,2,1,0:T(8,128)(2,1)} %param.7) | copy-start | bytes 7077892
  0.0 6.4 %copy-start.3 = (f32[12,256]{1,0:T(8,128)S(1)}, f32[12,256]{1,0:T(8,128)}, u32[]{:S(2)}) copy-start(f32[12,256]{1,0:T(8,128)} %weights_ref.9) | copy-start | bytes 36868
  1.5 6.2 %collective-permute-start.1 = (bf16[11,128,128]{2,1,0:T(8,128)(2,1)S(1)}, bf16[11,128,128]{2,1,0:T(8,128)(2,1)S(1)}, u32[]{:S(2)}, u32[]{:S(2)}) collective-permute-start(bf16[11,128,128]{2,1,0:T(8,128)(2,1)S(1)} %get-tuple-element.22), channel_id=1, source_target_pairs={{0,1},{2,3},{4,5},{6,7},{8,9},{10,11},{12,13},{14,15},{1,0},{3,2},... | collective-permute-start | bytes 1081352 | tf_op jit(solution)/shard_map/ppermute | solution.py:585
  1.6 13.0 %collective-permute-start.2 = (bf16[11,128,128]{2,1,0:T(8,128)(2,1)S(1)}, bf16[11,128,128]{2,1,0:T(8,128)(2,1)S(1)}, u32[]{:S(2)}, u32[]{:S(2)}) collective-permute-start(bf16[11,128,128]{2,1,0:T(8,128)(2,1)S(1)} %get-tuple-element.26), channel_id=1, source_target_pairs={{1,2},{3,4},{5,6},{7,8},{9,10},{11,12},{13,14},{2,1},{4,3},{6,5},{... | collective-permute-start | bytes 1081352 | tf_op jit(solution)/shard_map/ppermute | solution.py:591
  10.8 9.2 %collective-permute-start.4 = (bf16[11,128,128]{2,1,0:T(8,128)(2,1)S(1)}, bf16[11,128,128]{2,1,0:T(8,128)(2,1)S(1)}, u32[]{:S(2)}, u32[]{:S(2)}) collective-permute-start(bf16[11,128,128]{2,1,0:T(8,128)(2,1)S(1)} %get-tuple-element.28), channel_id=1, source_target_pairs={{0,1},{2,3},{4,5},{6,7},{8,9},{10,11},{12,13},{14,15},{1,0},{3,2},... | collective-permute-start | bytes 1081352 | tf_op jit(solution)/shard_map/ppermute | solution.py:585
  10.9 13.1 %collective-permute-start = (bf16[7,128,128]{2,1,0:T(8,128)(2,1)S(1)}, bf16[7,128,128]{2,1,0:T(8,128)(2,1)S(1)}, u32[]{:S(2)}, u32[]{:S(2)}) collective-permute-start(bf16[7,128,128]{2,1,0:T(8,128)(2,1)S(1)} %get-tuple-element.21), channel_id=1, source_target_pairs={{1,2},{3,4},{5,6},{7,8},{9,10},{11,12},{13,14},{2,1},{4,3},{6,5},{... | collective-permute-start | bytes 688136 | tf_op jit(solution)/shard_map/ppermute | solution.py:591
  15.6 8.4 %collective-permute-start.3 = (bf16[4,128,128]{2,1,0:T(8,128)(2,1)S(1)}, bf16[4,128,128]{2,1,0:T(8,128)(2,1)S(1)}, u32[]{:S(2)}, u32[]{:S(2)}) collective-permute-start(bf16[4,128,128]{2,1,0:T(8,128)(2,1)S(1)} %get-tuple-element.27), channel_id=1, source_target_pairs={{1,2},{3,4},{5,6},{7,8},{9,10},{11,12},{13,14},{2,1},{4,3},{6,5},{... | collective-permute-start | bytes 393224 | tf_op jit(solution)/shard_map/ppermute | solution.py:591

commit v9 on v5

--- a/solution.py
+++ b/solution.py
@@ -198,11 +198,15 @@
     return (meta_ref[geo.lengths_at + which] + GROUP - 1) // GROUP
 
 
+def waits():
+    return (lax.axis_index("blk") + 1) // 2 % 2 == 1
+
+
 def inner_share(geo, meta_ref):
     before = BUDGET
     for which in (CROSS_MANY, CROSS_FEW, NEAR_MANY, NEAR_FEW):
         before = before - COST[which % 2] * group_count(geo, meta_ref, which)
-    waiting = jnp.where((lax.axis_index("blk") + 1) // 2 % 2 == 1, WAIT, 0)
+    waiting = jnp.where(waits(), WAIT, 0)
     share = []
     for which in (INNER_MANY, INNER_FEW):
         cost, count = COST[which % 2], group_count(geo, meta_ref, which)
@@ -528,10 +532,10 @@
     copy.wait()
 
 
-def finish_kernel(geo, meta_ref, early_ref, late_ref, acc_ref, out_in, out_ref, total, sems):
+def finish_cross(geo, odd, parts, acc_ref, out_ref, total, sems):
     def add(up, down):
         copies = []
-        for packs, ref in ((geo.early_packs, early_ref), (geo.late_packs, late_ref)):
+        for packs, ref in parts:
             for start, place, count in packs[0 if up else 1]:
                 spot = pl.ds(len(copies) * geo.band, count)
                 total[spot] = acc_ref[pl.ds(start, count)] + ref[pl.ds(place, count)].astype(
@@ -545,7 +549,28 @@
         for copy in copies:
             copy.wait()
 
-    by_parity(meta_ref[geo.odd_at] == 1, add, False, True)
+    by_parity(odd, add, False, True)
+
+
+def early_join_kernel(geo, meta_ref, early_ref, acc_ref, out_in, out_ref, total, sems):
+    @pl.when(waits())
+    def _():
+        odd = meta_ref[geo.odd_at] == 1
+        finish_cross(geo, odd, ((geo.early_packs, early_ref),), acc_ref, out_ref, total, sems)
+
+
+def finish_kernel(geo, meta_ref, late_ref, early_ref, acc_ref, out_in, out_ref, total, sems):
+    odd = meta_ref[geo.odd_at] == 1
+    late = (geo.late_packs, late_ref)
+
+    @pl.when(waits())
+    def _():
+        finish_cross(geo, odd, (late,), acc_ref, out_ref, total, sems)
+
+    @pl.when(jnp.logical_not(waits()))
+    def _():
+        parts = ((geo.early_packs, early_ref), late)
+        finish_cross(geo, odd, parts, acc_ref, out_ref, total, sems)
 
 
 def call(kernel, out_shape, in_specs, out_specs, scratch, aliases=None, cost=None):
@@ -650,15 +675,18 @@
         {7: 0},
     )(meta, first, *panel, h, acc)
 
-    parts = 2 * geo.reach
-    out = call(
-        functools.partial(finish_kernel, geo),
-        whole,
-        [SMEM_SPEC] + [VMEM_SPEC] * 3 + [ANY_SPEC],
-        ANY_SPEC,
-        [pltpu.VMEM((parts * band, nb, nb), jnp.float32), dma((parts,))],
-        {4: 0},
-    )(meta, early, late, acc, out)
+    for kernel_of, got, parts in (
+        (early_join_kernel, (early,), geo.reach),
+        (finish_kernel, (late, early), 2 * geo.reach),
+    ):
+        out = call(
+            functools.partial(kernel_of, geo),
+            whole,
+            [SMEM_SPEC] + [VMEM_SPEC] * (len(got) + 1) + [ANY_SPEC],
+            ANY_SPEC,
+            [pltpu.VMEM((parts * band, nb, nb), jnp.float32), dma((parts,))],
+            {len(got) + 2: 0},
+        )(meta, *got, acc, out)
     return out.reshape(rows, band, nb, nb)
 
 

time: 24.2 us -> 24 us (level)
  waiting for transfers between devices: 1.07 us -> 0.32 us
  starting transfers between devices: 12.1 us -> 12.7 us
    ppermute x3, waiting for transfers between devices: 1.07 us -> 0.31 us  [to_second(): got = lax.ppermute(x, 'blk', pairs + [(j, i) for i, j in pairs])]
    pallas_call x1 -> x2, Pallas kernels: 0.9 us -> 1.58 us  [local(): call(functools.partial(kernel_of, geo), whole, [SMEM_SPEC] + [VMEM_SPEC]...]
    ppermute x3, starting transfers between devices: 11.9 us -> 12.5 us  [to_second(): got = lax.ppermute(x, 'blk', pairs + [(j, i) for i, j in pairs])]
    pallas_call x1, Pallas kernels: 1.3 us -> 0.7 us  [local(): call(functools.partial(waiting_kernel, geo), (acc_type, pltpu.SMEM((1,),...]
  transfers between devices with their start and end apart: 5 -> 5, of which waited for: 1 -> 1; matrix products, arithmetic and copies ran while one was open for 0% -> 0% of each run, Pallas kernels for 34% -> 35%
where the time goes in v9:
time: 24 us; the launch traced here: 23.7 us
  starting transfers between devices  12.7 us (53%)
  Pallas kernels  10.5 us (44%)
  waiting for transfers between devices  0.32 us (1%)
    ppermute x3, starting transfers between devices, to_second(): got = lax.ppermute(x, 'blk', pairs + [(j, i) for i, j in pairs])  12.5 us
    pallas_call x1, Pallas kernels, local(): call(functools.partial(near_kernel, geo), (acc_type, pack(geo.halo)), [SM...  2.72 us
    pallas_call x1, Pallas kernels, local(): call(functools.partial(inner_kernel, geo), (acc_type, whole), [SMEM_SPEC]...  2.12 us
    pallas_call x2, Pallas kernels, local(): call(functools.partial(kernel_of, geo), whole, [SMEM_SPEC] + [VMEM_SPEC]...  1.58 us
    pallas_call x1, Pallas kernels, local(): call(functools.partial(pack_kernel, geo), (pack(geo.halo),) * 2 + (pltpu....  1.43 us
    pallas_call x1, Pallas kernels, local(): call(functools.partial(early_kernel, geo), (acc_type, pack(geo.early)), [...  1.24 us
    pallas_call x1, Pallas kernels, local(): call(functools.partial(late_kernel, geo), (h_type, pack(geo.late)), [SMEM...  0.75 us
    pallas_call x1, Pallas kernels, local(): call(functools.partial(waiting_kernel, geo), (acc_type, pltpu.SMEM((1,),...  0.7 us
  transfers between devices with their start and end apart: 5, of which 1 were waited for; matrix products, arithmetic and copies ran while one was open for 0% of the time, Pallas kernels for 35%

profile of v9, /device:TPU:1, one launch (start us, length us, event | category | flops | bytes accessed | tf_op | source)
XLA Modules:
  0.0 23.7 jit_solution(6186934027889609053)
XLA Ops:
  0.0 0.0 copy-start
  0.0 0.0 copy-start.1
  0.0 0.0 copy-start.2
  0.0 0.0 copy-start.3
  0.0 1.4 %shard_map.73 = (bf16[11,128,128]{2,1,0:T(8,128)(2,1)S(1)}, bf16[11,128,128]{2,1,0:T(8,128)(2,1)S(1)}, s32[178]{0:T(256)S(4)}, f32[91,128,128]{2,1,0:T(8,128)S(1)}) custom-call(bf16[72,128,128]{2,1,0:T(8,128)(2,1)} %bitcast.3, s32[12]{0:T(128)} %centre_in.1, s32[4,12]{1,0:T(4,128)} %bitcast.8, s32[12]{0:T(128)} %counts_in.1), custom_call_target="tpu_custom_call" | custom-call | flops 10000000000 | bytes 100000000 | tf_op jit(solution)/shard_map/pallas_call | solution.py:612
  1.5 0.1 collective-permute-start
  1.6 4.8 %collective-permute-start.1 = (bf16[11,128,128]{2,1,0:T(8,128)(2,1)S(1)}, bf16[11,128,128]{2,1,0:T(8,128)(2,1)S(1)}, u32[]{:S(2)}, u32[]{:S(2)}) collective-permute-start(bf16[11,128,128]{2,1,0:T(8,128)(2,1)S(1)} %get-tuple-element.25), channel_id=1, source_target_pairs={{1,2},{3,4},{5,6},{7,8},{9,10},{11,12},{13,14},{2,1},{4,3},{6,5},{... | collective-permute-start | bytes 1081352 | tf_op jit(solution)/shard_map/ppermute | solution.py:597
  6.3 0.0 copy-done
  6.3 0.0 copy-done.1
  6.4 0.0 copy-done.2
  6.4 0.0 copy-done.3
  6.4 1.2 %shard_map.74 = (f32[91,128,128]{2,1,0:T(8,128)S(1)}, bf16[7,128,128]{2,1,0:T(8,128)(2,1)S(1)}) custom-call(s32[178]{0:T(256)S(4)} %get-tuple-element.19.meta_ref, bf16[72,128,128]{2,1,0:T(8,128)(2,1)S(1)} %bitcast.4, bf16[12,4,128,256]{3,2,1,0:T(8,128)(2,1)S(1)} %copy-done, bf16[12,256,256]{2,1,0:T(8,128)(2,1)S(1)} %copy-done.1, ...), custom_call_target="tpu_custom_call", output_to_operand_aliasing={{0}: (5, {})} | custom-call | tf_op jit(solution)/shard_map/pallas_call | solution.py:629
  7.6 0.0 collective-permute-done.halo_ref
  7.6 2.7 %shard_map.75 = (f32[91,128,128]{2,1,0:T(8,128)S(1)}, bf16[11,128,128]{2,1,0:T(8,128)(2,1)S(1)}) custom-call(s32[178]{0:T(256)S(4)} %get-tuple-element.19.meta_ref, bf16[11,128,128]{2,1,0:T(8,128)(2,1)S(1)} %collective-permute-done.halo_ref, bf16[72,128,128]{2,1,0:T(8,128)(2,1)S(1)} %bitcast.5, ...), custom_call_target="tpu_custom_call", output_to_operand_aliasing={{0}: (6, {})} | custom-call | tf_op jit(solution)/shard_map/pallas_call | solution.py:639
  10.4 0.1 collective-permute-start.4
  10.4 3.8 %collective-permute-start.3 = (bf16[7,128,128]{2,1,0:T(8,128)(2,1)S(1)}, bf16[7,128,128]{2,1,0:T(8,128)(2,1)S(1)}, u32[]{:S(2)}, u32[]{:S(2)}) collective-permute-start(bf16[7,128,128]{2,1,0:T(8,128)(2,1)S(1)} %get-tuple-element.27), channel_id=1, source_target_pairs={{1,2},{3,4},{5,6},{7,8},{9,10},{11,12},{13,14},{2,1},{4,3},{6,5},{... | collective-permute-start | bytes 688136 | tf_op jit(solution)/shard_map/ppermute | solution.py:597
  14.2 0.7 %shard_map.76 = (f32[91,128,128]{2,1,0:T(8,128)S(1)}, s32[1]{0:T(128)S(4)}) custom-call(s32[178]{0:T(256)S(4)} %get-tuple-element.19.meta_ref, bf16[72,128,128]{2,1,0:T(8,128)(2,1)S(1)} %bitcast.6, bf16[12,4,128,256]{3,2,1,0:T(8,128)(2,1)S(1)} %copy-done, bf16[12,256,256]{2,1,0:T(8,128)(2,1)S(1)} %copy-done.1, ...), custom_call_target="tpu_custom_call", output_to_operand_aliasing={{0}: (5, {})} | custom-call | tf_op jit(solution)/shard_map/pallas_call | solution.py:649
  14.9 0.0 collective-permute-done.1.halo_ref
  14.9 0.7 %shard_map.77 = (bf16[13,256,256]{2,1,0:T(8,128)(2,1)S(1)}, bf16[4,128,128]{2,1,0:T(8,128)(2,1)S(1)}) custom-call(s32[178]{0:T(256)S(4)} %get-tuple-element.19.meta_ref, s32[1]{0:T(128)S(4)} %get-tuple-element.24.done_ref, bf16[11,128,128]{2,1,0:T(8,128)(2,1)S(1)} %collective-permute-done.1.halo_ref, bf16[12,4,128,256]{3,2,1,0:T(8,128)(2,1)S(1)} %copy-done, ...), custom_call_target="tpu_custom_call" | custom-call | tf_op jit(solution)/shard_map/pallas_call | solution.py:659
  15.7 4.0 %collective-permute-start.2 = (bf16[4,128,128]{2,1,0:T(8,128)(2,1)S(1)}, bf16[4,128,128]{2,1,0:T(8,128)(2,1)S(1)}, u32[]{:S(2)}, u32[]{:S(2)}) collective-permute-start(bf16[4,128,128]{2,1,0:T(8,128)(2,1)S(1)} %get-tuple-element.26), channel_id=1, source_target_pairs={{1,2},{3,4},{5,6},{7,8},{9,10},{11,12},{13,14},{2,1},{4,3},{6,5},{... | collective-permute-start | bytes 393224 | tf_op jit(solution)/shard_map/ppermute | solution.py:597
  19.7 0.0 collective-permute-done.4.first_ref
  19.7 2.1 %shard_map.78 = (f32[91,128,128]{2,1,0:T(8,128)S(1)}, f32[72,128,128]{2,1,0:T(8,128)}) custom-call(s32[178]{0:T(256)S(4)} %get-tuple-element.19.meta_ref, bf16[11,128,128]{2,1,0:T(8,128)(2,1)S(1)} %collective-permute-done.4.first_ref, bf16[72,128,128]{2,1,0:T(8,128)(2,1)S(1)} %bitcast.7, ...), custom_call_target="tpu_custom_call", output_to_operand_aliasing={{0}: (7, {})} | custom-call | tf_op jit(solution)/shard_map/pallas_call | solution.py:669
  21.8 0.0 collective-permute-done.3.early_ref
  21.8 0.8 %shard_map.79.out_in = f32[72,128,128]{2,1,0:T(8,128)} custom-call(s32[178]{0:T(256)S(4)} %get-tuple-element.19.meta_ref, bf16[7,128,128]{2,1,0:T(8,128)(2,1)S(1)} %collective-permute-done.3.early_ref, f32[91,128,128]{2,1,0:T(8,128)S(1)} %get-tuple-element.31.acc_ref, f32[72,128,128]{2,1,0:T(8,128)} %get-tuple-element.32.out_in), custom_call_target="tpu_custom_call", output_to_operand_aliasing={{}: (3, {})} | custom-call | tf_op jit(solution)/shard_map/pallas_call | solution.py:682
  22.7 0.3 %collective-permute-done.2.late_ref = bf16[4,128,128]{2,1,0:T(8,128)(2,1)S(1)} collective-permute-done((bf16[4,128,128]{2,1,0:T(8,128)(2,1)S(1)}, bf16[4,128,128]{2,1,0:T(8,128)(2,1)S(1)}, u32[]{:S(2)}, u32[]{:S(2)}) %collective-permute-start.2) | collective-permute-done | bytes 131104 | tf_op jit(solution)/shard_map/ppermute | solution.py:597
  23.0 0.7 %shard_map.80 = f32[72,128,128]{2,1,0:T(8,128)} custom-call(s32[178]{0:T(256)S(4)} %get-tuple-element.19.meta_ref, bf16[4,128,128]{2,1,0:T(8,128)(2,1)S(1)} %collective-permute-done.2.late_ref, bf16[7,128,128]{2,1,0:T(8,128)(2,1)S(1)} %collective-permute-done.3.early_ref, ...), custom_call_target="tpu_custom_call", output_to_operand_aliasing={{}: (4, {})} | custom-call | tf_op jit(solution)/shard_map/pallas_call | solution.py:682
Async XLA Ops:
  0.0 6.3 %copy-start = (bf16[12,4,128,256]{3,2,1,0:T(8,128)(2,1)S(1)}, bf16[12,4,128,256]{3,2,1,0:T(8,128)(2,1)}, u32[]{:S(2)}) copy-start(bf16[12,4,128,256]{3,2,1,0:T(8,128)(2,1)} %ao_ref.9) | copy-start | bytes 9437188
  0.0 6.3 %copy-start.1 = (bf16[12,256,256]{2,1,0:T(8,128)(2,1)S(1)}, bf16[12,256,256]{2,1,0:T(8,128)(2,1)}, u32[]{:S(2)}) copy-start(bf16[12,256,256]{2,1,0:T(8,128)(2,1)} %kernel_ref.9) | copy-start | bytes 4718596
  0.0 6.4 %copy-start.2 = (bf16[8,9,128,128]{3,2,1,0:T(8,128)(2,1)S(1)}, bf16[8,9,128,128]{3,2,1,0:T(8,128)(2,1)}, u32[]{:S(2)}) copy-start(bf16[8,9,128,128]{3,2,1,0:T(8,128)(2,1)} %param.7) | copy-start | bytes 7077892
  0.0 6.4 %copy-start.3 = (f32[12,256]{1,0:T(8,128)S(1)}, f32[12,256]{1,0:T(8,128)}, u32[]{:S(2)}) copy-start(f32[12,256]{1,0:T(8,128)} %weights_ref.9) | copy-start | bytes 36868
  1.5 6.2 %collective-permute-start = (bf16[11,128,128]{2,1,0:T(8,128)(2,1)S(1)}, bf16[11,128,128]{2,1,0:T(8,128)(2,1)S(1)}, u32[]{:S(2)}, u32[]{:S(2)}) collective-permute-start(bf16[11,128,128]{2,1,0:T(8,128)(2,1)S(1)} %get-tuple-element.20), channel_id=1, source_target_pairs={{0,1},{2,3},{4,5},{6,7},{8,9},{10,11},{12,13},{14,15},{1,0},{3,2},... | collective-permute-start | bytes 1081352 | tf_op jit(solution)/shard_map/ppermute | solution.py:591
  1.6 13.4 %collective-permute-start.1 = (bf16[11,128,128]{2,1,0:T(8,128)(2,1)S(1)}, bf16[11,128,128]{2,1,0:T(8,128)(2,1)S(1)}, u32[]{:S(2)}, u32[]{:S(2)}) collective-permute-start(bf16[11,128,128]{2,1,0:T(8,128)(2,1)S(1)} %get-tuple-element.25), channel_id=1, source_target_pairs={{1,2},{3,4},{5,6},{7,8},{9,10},{11,12},{13,14},{2,1},{4,3},{6,5},{... | collective-permute-start | bytes 1081352 | tf_op jit(solution)/shard_map/ppermute | solution.py:597
  10.4 9.3 %collective-permute-start.4 = (bf16[11,128,128]{2,1,0:T(8,128)(2,1)S(1)}, bf16[11,128,128]{2,1,0:T(8,128)(2,1)S(1)}, u32[]{:S(2)}, u32[]{:S(2)}) collective-permute-start(bf16[11,128,128]{2,1,0:T(8,128)(2,1)S(1)} %get-tuple-element.28), channel_id=1, source_target_pairs={{0,1},{2,3},{4,5},{6,7},{8,9},{10,11},{12,13},{14,15},{1,0},{3,2},... | collective-permute-start | bytes 1081352 | tf_op jit(solution)/shard_map/ppermute | solution.py:591
  10.4 11.4 %collective-permute-start.3 = (bf16[7,128,128]{2,1,0:T(8,128)(2,1)S(1)}, bf16[7,128,128]{2,1,0:T(8,128)(2,1)S(1)}, u32[]{:S(2)}, u32[]{:S(2)}) collective-permute-start(bf16[7,128,128]{2,1,0:T(8,128)(2,1)S(1)} %get-tuple-element.27), channel_id=1, source_target_pairs={{1,2},{3,4},{5,6},{7,8},{9,10},{11,12},{13,14},{2,1},{4,3},{6,5},{... | collective-permute-start | bytes 688136 | tf_op jit(solution)/shard_map/ppermute | solution.py:597
  15.7 7.3 %collective-permute-start.2 = (bf16[4,128,128]{2,1,0:T(8,128)(2,1)S(1)}, bf16[4,128,128]{2,1,0:T(8,128)(2,1)S(1)}, u32[]{:S(2)}, u32[]{:S(2)}) collective-permute-start(bf16[4,128,128]{2,1,0:T(8,128)(2,1)S(1)} %get-tuple-element.26), channel_id=1, source_target_pairs={{1,2},{3,4},{5,6},{7,8},{9,10},{11,12},{13,14},{2,1},{4,3},{6,5},{... | collective-permute-start | bytes 393224 | tf_op jit(solution)/shard_map/ppermute | solution.py:597

commit v10 on v9

--- a/solution.py
+++ b/solution.py
@@ -552,8 +552,13 @@
     by_parity(odd, add, False, True)
 
 
+def has_time(geo, meta_ref):
+    left = [bounds[3] - bounds[2] for bounds in inner_share(geo, meta_ref)]
+    return waits() & (left[0] + left[1] == 0)
+
+
 def early_join_kernel(geo, meta_ref, early_ref, acc_ref, out_in, out_ref, total, sems):
-    @pl.when(waits())
+    @pl.when(has_time(geo, meta_ref))
     def _():
         odd = meta_ref[geo.odd_at] == 1
         finish_cross(geo, odd, ((geo.early_packs, early_ref),), acc_ref, out_ref, total, sems)
@@ -562,12 +567,13 @@
 def finish_kernel(geo, meta_ref, late_ref, early_ref, acc_ref, out_in, out_ref, total, sems):
     odd = meta_ref[geo.odd_at] == 1
     late = (geo.late_packs, late_ref)
-
-    @pl.when(waits())
+    joined = has_time(geo, meta_ref)
+
+    @pl.when(joined)
     def _():
         finish_cross(geo, odd, (late,), acc_ref, out_ref, total, sems)
 
-    @pl.when(jnp.logical_not(waits()))
+    @pl.when(jnp.logical_not(joined))
     def _():
         parts = ((geo.early_packs, early_ref), late)
         finish_cross(geo, odd, parts, acc_ref, out_ref, total, sems)

time: 24 us -> 24 us (level)
  Pallas kernels: 10.5 us -> 11.2 us
  starting transfers between devices: 12.7 us -> 12.1 us
    ppermute x3, starting transfers between devices: 12.5 us -> 11.9 us  [to_second(): got = lax.ppermute(x, 'blk', pairs + [(j, i) for i, j in pairs])]
    pallas_call x1, Pallas kernels: 0.7 us -> 1.3 us  [local(): call(functools.partial(waiting_kernel, geo), (acc_type, pltpu.SMEM((1,),...]
  transfers between devices with their start and end apart: 5 -> 5, of which waited for: 1 -> 1; matrix products, arithmetic and copies ran while one was open for 0% -> 0% of each run, Pallas kernels for 35% -> 38%
where the time goes in v10:
time: 24 us; the launch traced here: 23.7 us
  starting transfers between devices  12.1 us (50%)
  Pallas kernels  11.2 us (47%)
  waiting for transfers between devices  0.26 us (1%)
    ppermute x3, starting transfers between devices, to_second(): got = lax.ppermute(x, 'blk', pairs + [(j, i) for i, j in pairs])  11.9 us
    pallas_call x1, Pallas kernels, local(): call(functools.partial(near_kernel, geo), (acc_type, pack(geo.halo)), [SM...  2.73 us
    pallas_call x1, Pallas kernels, local(): call(functools.partial(inner_kernel, geo), (acc_type, whole), [SMEM_SPEC]...  2.12 us
    pallas_call x2, Pallas kernels, local(): call(functools.partial(kernel_of, geo), whole, [SMEM_SPEC] + [VMEM_SPEC]...  1.63 us
    pallas_call x1, Pallas kernels, local(): call(functools.partial(pack_kernel, geo), (pack(geo.halo),) * 2 + (pltpu....  1.43 us
    pallas_call x1, Pallas kernels, local(): call(functools.partial(waiting_kernel, geo), (acc_type, pltpu.SMEM((1,),...  1.3 us
    pallas_call x1, Pallas kernels, local(): call(functools.partial(early_kernel, geo), (acc_type, pack(geo.early)), [...  1.24 us
    pallas_call x1, Pallas kernels, local(): call(functools.partial(late_kernel, geo), (h_type, pack(geo.late)), [SMEM...  0.75 us
  transfers between devices with their start and end apart: 5, of which 1 were waited for; matrix products, arithmetic and copies ran while one was open for 0% of the time, Pallas kernels for 38%

profile of v10, /device:TPU:1, one launch (start us, length us, event | category | flops | bytes accessed | tf_op | source)
XLA Modules:
  0.0 23.7 jit_solution(5422632477350032997)
XLA Ops:
  0.0 0.0 copy-start
  0.0 0.0 copy-start.1
  0.0 0.0 copy-start.2
  0.0 0.0 copy-start.3
  0.0 1.4 %shard_map.73 = (bf16[11,128,128]{2,1,0:T(8,128)(2,1)S(1)}, bf16[11,128,128]{2,1,0:T(8,128)(2,1)S(1)}, s32[178]{0:T(256)S(4)}, f32[91,128,128]{2,1,0:T(8,128)S(1)}) custom-call(bf16[72,128,128]{2,1,0:T(8,128)(2,1)} %bitcast.3, s32[12]{0:T(128)} %centre_in.1, s32[4,12]{1,0:T(4,128)} %bitcast.8, s32[12]{0:T(128)} %counts_in.1), custom_call_target="tpu_custom_call" | custom-call | flops 10000000000 | bytes 100000000 | tf_op jit(solution)/shard_map/pallas_call | solution.py:618
  1.5 0.1 collective-permute-start
  1.6 4.8 %collective-permute-start.1 = (bf16[11,128,128]{2,1,0:T(8,128)(2,1)S(1)}, bf16[11,128,128]{2,1,0:T(8,128)(2,1)S(1)}, u32[]{:S(2)}, u32[]{:S(2)}) collective-permute-start(bf16[11,128,128]{2,1,0:T(8,128)(2,1)S(1)} %get-tuple-element.25), channel_id=1, source_target_pairs={{1,2},{3,4},{5,6},{7,8},{9,10},{11,12},{13,14},{2,1},{4,3},{6,5},{... | collective-permute-start | bytes 1081352 | tf_op jit(solution)/shard_map/ppermute | solution.py:603
  6.3 0.0 copy-done
  6.3 0.0 copy-done.1
  6.4 0.0 copy-done.2
  6.4 0.0 copy-done.3
  6.4 1.2 %shard_map.74 = (f32[91,128,128]{2,1,0:T(8,128)S(1)}, bf16[7,128,128]{2,1,0:T(8,128)(2,1)S(1)}) custom-call(s32[178]{0:T(256)S(4)} %get-tuple-element.19.meta_ref, bf16[72,128,128]{2,1,0:T(8,128)(2,1)S(1)} %bitcast.4, bf16[12,4,128,256]{3,2,1,0:T(8,128)(2,1)S(1)} %copy-done, bf16[12,256,256]{2,1,0:T(8,128)(2,1)S(1)} %copy-done.1, ...), custom_call_target="tpu_custom_call", output_to_operand_aliasing={{0}: (5, {})} | custom-call | tf_op jit(solution)/shard_map/pallas_call | solution.py:635
  7.6 0.0 collective-permute-done.halo_ref
  7.6 2.7 %shard_map.75 = (f32[91,128,128]{2,1,0:T(8,128)S(1)}, bf16[11,128,128]{2,1,0:T(8,128)(2,1)S(1)}) custom-call(s32[178]{0:T(256)S(4)} %get-tuple-element.19.meta_ref, bf16[11,128,128]{2,1,0:T(8,128)(2,1)S(1)} %collective-permute-done.halo_ref, bf16[72,128,128]{2,1,0:T(8,128)(2,1)S(1)} %bitcast.5, ...), custom_call_target="tpu_custom_call", output_to_operand_aliasing={{0}: (6, {})} | custom-call | tf_op jit(solution)/shard_map/pallas_call | solution.py:645
  10.4 0.1 collective-permute-start.4
  10.5 3.7 %collective-permute-start.3 = (bf16[7,128,128]{2,1,0:T(8,128)(2,1)S(1)}, bf16[7,128,128]{2,1,0:T(8,128)(2,1)S(1)}, u32[]{:S(2)}, u32[]{:S(2)}) collective-permute-start(bf16[7,128,128]{2,1,0:T(8,128)(2,1)S(1)} %get-tuple-element.27), channel_id=1, source_target_pairs={{1,2},{3,4},{5,6},{7,8},{9,10},{11,12},{13,14},{2,1},{4,3},{6,5},{... | collective-permute-start | bytes 688136 | tf_op jit(solution)/shard_map/ppermute | solution.py:603
  14.2 1.3 %shard_map.76 = (f32[91,128,128]{2,1,0:T(8,128)S(1)}, s32[1]{0:T(128)S(4)}) custom-call(s32[178]{0:T(256)S(4)} %get-tuple-element.19.meta_ref, bf16[72,128,128]{2,1,0:T(8,128)(2,1)S(1)} %bitcast.6, bf16[12,4,128,256]{3,2,1,0:T(8,128)(2,1)S(1)} %copy-done, bf16[12,256,256]{2,1,0:T(8,128)(2,1)S(1)} %copy-done.1, ...), custom_call_target="tpu_custom_call", output_to_operand_aliasing={{0}: (5, {})} | custom-call | tf_op jit(solution)/shard_map/pallas_call | solution.py:655
  15.5 0.0 collective-permute-done.1.halo_ref
  15.5 0.7 %shard_map.77 = (bf16[13,256,256]{2,1,0:T(8,128)(2,1)S(1)}, bf16[4,128,128]{2,1,0:T(8,128)(2,1)S(1)}) custom-call(s32[178]{0:T(256)S(4)} %get-tuple-element.19.meta_ref, s32[1]{0:T(128)S(4)} %get-tuple-element.24.done_ref, bf16[11,128,128]{2,1,0:T(8,128)(2,1)S(1)} %collective-permute-done.1.halo_ref, bf16[12,4,128,256]{3,2,1,0:T(8,128)(2,1)S(1)} %copy-done, ...), custom_call_target="tpu_custom_call" | custom-call | tf_op jit(solution)/shard_map/pallas_call | solution.py:665
  16.3 3.4 %collective-permute-start.2 = (bf16[4,128,128]{2,1,0:T(8,128)(2,1)S(1)}, bf16[4,128,128]{2,1,0:T(8,128)(2,1)S(1)}, u32[]{:S(2)}, u32[]{:S(2)}) collective-permute-start(bf16[4,128,128]{2,1,0:T(8,128)(2,1)S(1)} %get-tuple-element.26), channel_id=1, source_target_pairs={{1,2},{3,4},{5,6},{7,8},{9,10},{11,12},{13,14},{2,1},{4,3},{6,5},{... | collective-permute-start | bytes 393224 | tf_op jit(solution)/shard_map/ppermute | solution.py:603
  19.7 0.0 collective-permute-done.4.first_ref
  19.7 2.1 %shard_map.78 = (f32[91,128,128]{2,1,0:T(8,128)S(1)}, f32[72,128,128]{2,1,0:T(8,128)}) custom-call(s32[178]{0:T(256)S(4)} %get-tuple-element.19.meta_ref, bf16[11,128,128]{2,1,0:T(8,128)(2,1)S(1)} %collective-permute-done.4.first_ref, bf16[72,128,128]{2,1,0:T(8,128)(2,1)S(1)} %bitcast.7, ...), custom_call_target="tpu_custom_call", output_to_operand_aliasing={{0}: (7, {})} | custom-call | tf_op jit(solution)/shard_map/pallas_call | solution.py:675
  21.8 0.0 collective-permute-done.3.early_ref
  21.8 0.9 %shard_map.79.out_in = f32[72,128,128]{2,1,0:T(8,128)} custom-call(s32[178]{0:T(256)S(4)} %get-tuple-element.19.meta_ref, bf16[7,128,128]{2,1,0:T(8,128)(2,1)S(1)} %collective-permute-done.3.early_ref, f32[91,128,128]{2,1,0:T(8,128)S(1)} %get-tuple-element.31.acc_ref, f32[72,128,128]{2,1,0:T(8,128)} %get-tuple-element.32.out_in), custom_call_target="tpu_custom_call", output_to_operand_aliasing={{}: (3, {})} | custom-call | tf_op jit(solution)/shard_map/pallas_call | solution.py:688
  22.7 0.3 %collective-permute-done.2.late_ref = bf16[4,128,128]{2,1,0:T(8,128)(2,1)S(1)} collective-permute-done((bf16[4,128,128]{2,1,0:T(8,128)(2,1)S(1)}, bf16[4,128,128]{2,1,0:T(8,128)(2,1)S(1)}, u32[]{:S(2)}, u32[]{:S(2)}) %collective-permute-start.2) | collective-permute-done | bytes 131104 | tf_op jit(solution)/shard_map/ppermute | solution.py:603
  23.0 0.7 %shard_map.80 = f32[72,128,128]{2,1,0:T(8,128)} custom-call(s32[178]{0:T(256)S(4)} %get-tuple-element.19.meta_ref, bf16[4,128,128]{2,1,0:T(8,128)(2,1)S(1)} %collective-permute-done.2.late_ref, bf16[7,128,128]{2,1,0:T(8,128)(2,1)S(1)} %collective-permute-done.3.early_ref, ...), custom_call_target="tpu_custom_call", output_to_operand_aliasing={{}: (4, {})} | custom-call | tf_op jit(solution)/shard_map/pallas_call | solution.py:688
Async XLA Ops:
  0.0 6.3 %copy-start = (bf16[12,4,128,256]{3,2,1,0:T(8,128)(2,1)S(1)}, bf16[12,4,128,256]{3,2,1,0:T(8,128)(2,1)}, u32[]{:S(2)}) copy-start(bf16[12,4,128,256]{3,2,1,0:T(8,128)(2,1)} %ao_ref.9) | copy-start | bytes 9437188
  0.0 6.3 %copy-start.1 = (bf16[12,256,256]{2,1,0:T(8,128)(2,1)S(1)}, bf16[12,256,256]{2,1,0:T(8,128)(2,1)}, u32[]{:S(2)}) copy-start(bf16[12,256,256]{2,1,0:T(8,128)(2,1)} %kernel_ref.9) | copy-start | bytes 4718596
  0.0 6.4 %copy-start.2 = (bf16[8,9,128,128]{3,2,1,0:T(8,128)(2,1)S(1)}, bf16[8,9,128,128]{3,2,1,0:T(8,128)(2,1)}, u32[]{:S(2)}) copy-start(bf16[8,9,128,128]{3,2,1,0:T(8,128)(2,1)} %param.7) | copy-start | bytes 7077892
  0.0 6.4 %copy-start.3 = (f32[12,256]{1,0:T(8,128)S(1)}, f32[12,256]{1,0:T(8,128)}, u32[]{:S(2)}) copy-start(f32[12,256]{1,0:T(8,128)} %weights_ref.9) | copy-start | bytes 36868
  1.5 6.2 %collective-permute-start = (bf16[11,128,128]{2,1,0:T(8,128)(2,1)S(1)}, bf16[11,128,128]{2,1,0:T(8,128)(2,1)S(1)}, u32[]{:S(2)}, u32[]{:S(2)}) collective-permute-start(bf16[11,128,128]{2,1,0:T(8,128)(2,1)S(1)} %get-tuple-element.20), channel_id=1, source_target_pairs={{0,1},{2,3},{4,5},{6,7},{8,9},{10,11},{12,13},{14,15},{1,0},{3,2},... | collective-permute-start | bytes 1081352 | tf_op jit(solution)/shard_map/ppermute | solution.py:597
  1.6 13.9 %collective-permute-start.1 = (bf16[11,128,128]{2,1,0:T(8,128)(2,1)S(1)}, bf16[11,128,128]{2,1,0:T(8,128)(2,1)S(1)}, u32[]{:S(2)}, u32[]{:S(2)}) collective-permute-start(bf16[11,128,128]{2,1,0:T(8,128)(2,1)S(1)} %get-tuple-element.25), channel_id=1, source_target_pairs={{1,2},{3,4},{5,6},{7,8},{9,10},{11,12},{13,14},{2,1},{4,3},{6,5},{... | collective-permute-start | bytes 1081352 | tf_op jit(solution)/shard_map/ppermute | solution.py:603
  10.4 9.3 %collective-permute-start.4 = (bf16[11,128,128]{2,1,0:T(8,128)(2,1)S(1)}, bf16[11,128,128]{2,1,0:T(8,128)(2,1)S(1)}, u32[]{:S(2)}, u32[]{:S(2)}) collective-permute-start(bf16[11,128,128]{2,1,0:T(8,128)(2,1)S(1)} %get-tuple-element.28), channel_id=1, source_target_pairs={{0,1},{2,3},{4,5},{6,7},{8,9},{10,11},{12,13},{14,15},{1,0},{3,2},... | collective-permute-start | bytes 1081352 | tf_op jit(solution)/shard_map/ppermute | solution.py:597
  10.5 11.4 %collective-permute-start.3 = (bf16[7,128,128]{2,1,0:T(8,128)(2,1)S(1)}, bf16[7,128,128]{2,1,0:T(8,128)(2,1)S(1)}, u32[]{:S(2)}, u32[]{:S(2)}) collective-permute-start(bf16[7,128,128]{2,1,0:T(8,128)(2,1)S(1)} %get-tuple-element.27), channel_id=1, source_target_pairs={{1,2},{3,4},{5,6},{7,8},{9,10},{11,12},{13,14},{2,1},{4,3},{6,5},{... | collective-permute-start | bytes 688136 | tf_op jit(solution)/shard_map/ppermute | solution.py:603
  16.3 6.7 %collective-permute-start.2 = (bf16[4,128,128]{2,1,0:T(8,128)(2,1)S(1)}, bf16[4,128,128]{2,1,0:T(8,128)(2,1)S(1)}, u32[]{:S(2)}, u32[]{:S(2)}) collective-permute-start(bf16[4,128,128]{2,1,0:T(8,128)(2,1)S(1)} %get-tuple-element.26), channel_id=1, source_target_pairs={{1,2},{3,4},{5,6},{7,8},{9,10},{11,12},{13,14},{2,1},{4,3},{6,5},{... | collective-permute-start | bytes 393224 | tf_op jit(solution)/shard_map/ppermute | solution.py:603

commit v11 on v6

--- a/solution.py
+++ b/solution.py
@@ -490,7 +490,7 @@
 
 def inner_kernel(
     geo, meta_ref, first_ref, tiles_ref, ao_ref, kernel_ref, weights_ref, h_ref, acc_in,
-    acc_ref, out_ref, sems,
+    acc_ref, out_ref, early_ref, late_ref, sems,
 ):
     odd = meta_ref[geo.odd_at] == 1
     refs = (meta_ref, tiles_ref, ao_ref, kernel_ref, weights_ref, acc_ref)
@@ -515,6 +515,10 @@
         )
 
     def write_quiet(up, down):
+        side = 1 if up else 0
+        for packs, ref in ((geo.early_packs, early_ref), (geo.late_packs, late_ref)):
+            for start, place, count in packs[side]:
+                ref[pl.ds(place, count)] = acc_ref[pl.ds(start, count)]
         run_copies(
             [
                 pltpu.make_async_copy(
@@ -528,21 +532,15 @@
     copy.wait()
 
 
-def join_kernel(geo, packs, meta_ref, got_ref, acc_ref, out_in, out_ref, total, sems):
-    def add(up, down):
-        copies = []
-        for start, place, count in packs[0 if up else 1]:
-            spot = pl.ds(place, count)
-            total[spot] = acc_ref[pl.ds(start, count)] + got_ref[spot].astype(jnp.float32)
-            copy = pltpu.make_async_copy(
-                total.at[spot], out_ref.at[pl.ds(start, count)], sems.at[len(copies)]
-            )
-            copy.start()
-            copies.append(copy)
-        for copy in copies:
-            copy.wait()
-
-    by_parity(meta_ref[geo.odd_at] == 1, add, False, True)
+def finish_cross(odd, packs, got, own, out):
+    total = own + got.astype(jnp.float32)
+    by_size = lambda pack: sorted(pack, key=lambda segment: segment[2])
+    for upper, lower in zip(*(by_size(pack) for pack in packs)):
+        start = jnp.where(odd, upper[0], lower[0])
+        place = jnp.where(odd, upper[1], lower[1])
+        part = lax.dynamic_slice_in_dim(total, place, upper[2])
+        out = lax.dynamic_update_slice_in_dim(out, part, start, axis=0)
+    return out
 
 
 def call(kernel, out_shape, in_specs, out_specs, scratch, aliases=None, cost=None):
@@ -564,10 +562,10 @@
     return pltpu.with_memory_space_constraint(got, pltpu.VMEM)
 
 
-def to_second(x, size):
+def to_second(x, size, for_kernel=True):
     pairs = [(i, i + 1) for i in range(1, size - 1, 2)]
     got = lax.ppermute(x, "blk", pairs + [(j, i) for i, j in pairs])
-    return pltpu.with_memory_space_constraint(got, pltpu.VMEM)
+    return pltpu.with_memory_space_constraint(got, pltpu.VMEM) if for_kernel else got
 
 
 def local(density, ao_values, kernel, grid_weights, centre, sig_offsets, counts):
@@ -606,7 +604,7 @@
         [],
         {5: 0},
     )(meta, *panel, acc)
-    early = to_second(early, size)
+    early = to_second(early, size, False)
 
     acc, first = call(
         functools.partial(near_kernel, geo),
@@ -635,27 +633,22 @@
         (VMEM_SPEC,) * 2,
         [pltpu.VMEM((geo.reach * nb, geo.reach * nb), jnp.float32)],
     )(meta, done, cross_halo, *panel[1:])
-    late = to_second(late, size)
+    late = to_second(late, size, False)
 
     whole = jax.ShapeDtypeStruct((geo.own, nb, nb), jnp.float32)
-    acc, out = call(
+    sums = [jax.ShapeDtypeStruct((count, nb, nb), jnp.float32) for count in (geo.early, geo.late)]
+    _, out, *own = call(
         functools.partial(inner_kernel, geo),
-        (acc_type, whole),
+        (acc_type, whole, *sums),
         [SMEM_SPEC] + [VMEM_SPEC] * 7,
-        (VMEM_SPEC, ANY_SPEC),
+        (VMEM_SPEC, ANY_SPEC, VMEM_SPEC, VMEM_SPEC),
         [dma((1 + max(len(runs) for runs in geo.quiet),))],
         {7: 0},
     )(meta, first, *panel, h, acc)
 
-    for packs, got in ((geo.early_packs, early), (geo.late_packs, late)):
-        out = call(
-            functools.partial(join_kernel, geo, packs),
-            whole,
-            [SMEM_SPEC] + [VMEM_SPEC] * 2 + [ANY_SPEC],
-            ANY_SPEC,
-            [pltpu.VMEM(got.shape, jnp.float32), dma((geo.reach,))],
-            {3: 0},
-        )(meta, got, acc, out)
+    odd = lax.axis_index("blk") % 2 == 1
+    out = finish_cross(odd, geo.early_packs, early, own[0], out)
+    out = finish_cross(odd, geo.late_packs, late, own[1], out)
     return out.reshape(rows, band, nb, nb)
 
 

time: 24 us -> 42.5 us (1.77)
  the two profiles are of different devices: /device:TPU:6 before, /device:TPU:15 now
where the time goes in v11:
time: 42.5 us; the launch traced here: 41.7 us
  local copies, waits for them, and re-layouts  16.3 us (38%)
  Pallas kernels  13.8 us (32%)
  starting transfers between devices  10.4 us (24%)
  other arithmetic  1.01 us (2%)
    unnamed x20, local copies, waits for them, and re-layouts  13.6 us
    ppermute x3, starting transfers between devices, to_second(): got = lax.ppermute(x, 'blk', pairs + [(j, i) for i, j in pairs])  9.63 us
    pallas_call x1, Pallas kernels, local(): call(functools.partial(inner_kernel, geo), (acc_type, whole, *sums), [SME...  5.22 us
    pallas_call x1, Pallas kernels, local(): call(functools.partial(near_kernel, geo), (acc_type, pack(geo.halo)), [SM...  2.83 us
    dynamic_update_slice x4, local copies, waits for them, and re-layouts, finish_cross(): out = lax.dynamic_update_slice_in_dim(out, part, start, axis=0)  2.76 us
    pallas_call x1, Pallas kernels, local(): call(functools.partial(early_kernel, geo), (acc_type, pack(geo.early)), [...  2.54 us
    pallas_call x1, Pallas kernels, local(): call(functools.partial(pack_kernel, geo), (pack(geo.halo),) * 2 + (pltpu....  2.16 us
    pallas_call x1, Pallas kernels, local(): call(functools.partial(late_kernel, geo), (h_type, pack(geo.late)), [SMEM...  1.04 us
  transfers between devices with their start and end apart: 5, of which 0 were waited for; matrix products, arithmetic and copies ran while one was open for 6% of the time, Pallas kernels for 28%

profile of v11, /device:TPU:15, one launch (start us, length us, event | category | flops | bytes accessed | tf_op | source)
XLA Modules:
  0.0 41.7 jit_solution(12766317718809177802)
XLA Ops:
  0.0 0.0 copy-start.9
  0.0 2.2 %shard_map.73 = (bf16[11,128,128]{2,1,0:T(8,128)(2,1)S(1)}, bf16[11,128,128]{2,1,0:T(8,128)(2,1)}, s32[178]{0:T(256)S(4)}, f32[91,128,128]{2,1,0:T(8,128)S(1)}) custom-call(bf16[72,128,128]{2,1,0:T(8,128)(2,1)} %bitcast.3, s32[12]{0:T(128)} %centre_in.1, s32[4,12]{1,0:T(4,128)} %bitcast.8, s32[12]{0:T(128)} %counts_in.1), custom_call_target="tpu_custom_call" | custom-call | flops 10000000000 | bytes 100000000 | tf_op jit(solution)/shard_map/pallas_call | solution.py:582
  2.2 0.7 %collective-permute-start = (bf16[11,128,128]{2,1,0:T(8,128)(2,1)S(1)}, bf16[11,128,128]{2,1,0:T(8,128)(2,1)S(1)}, u32[]{:S(2)}, u32[]{:S(2)}) collective-permute-start(bf16[11,128,128]{2,1,0:T(8,128)(2,1)S(1)} %get-tuple-element.21), channel_id=1, source_target_pairs={{0,1},{2,3},{4,5},{6,7},{8,9},{10,11},{12,13},{14,15},{1,0},{3,2},... | collective-permute-start | bytes 1081352 | tf_op jit(solution)/shard_map/ppermute | solution.py:561
  2.9 3.2 %collective-permute-start.2 = (bf16[11,128,128]{2,1,0:T(8,128)(2,1)}, bf16[11,128,128]{2,1,0:T(8,128)(2,1)S(1)}, u32[]{:S(2)}, u32[]{:S(2)}) collective-permute-start(bf16[11,128,128]{2,1,0:T(8,128)(2,1)} %get-tuple-element.27), channel_id=1, source_target_pairs={{1,2},{3,4},{5,6},{7,8},{9,10},{11,12},{13,14},{2,1},{4,3},{6,5},{... | collective-permute-start | bytes 1081352 | tf_op jit(solution)/shard_map/ppermute | solution.py:567
  6.1 0.0 copy-done.4
  6.1 0.0 copy-done.5
  6.1 0.0 copy-done.7
  6.1 0.0 copy-done.9
  6.2 2.5 %shard_map.74 = (f32[91,128,128]{2,1,0:T(8,128)S(1)}, bf16[7,128,128]{2,1,0:T(8,128)(2,1)}) custom-call(s32[178]{0:T(256)S(4)} %get-tuple-element.20.meta_ref, bf16[72,128,128]{2,1,0:T(8,128)(2,1)S(1)} %bitcast.4, bf16[12,4,128,256]{3,2,1,0:T(8,128)(2,1)S(1)} %copy-done.4, bf16[12,256,256]{2,1,0:T(8,128)(2,1)S(1)} %copy-done.5, ...), custom_call_target="tpu_custom_call", output_to_operand_aliasing={{0}: (5, {})} | custom-call | tf_op jit(solution)/shard_map/pallas_call | solution.py:599
  8.7 0.0 collective-permute-done.halo_ref
  8.7 2.8 %shard_map.75 = (f32[91,128,128]{2,1,0:T(8,128)S(1)}, bf16[11,128,128]{2,1,0:T(8,128)(2,1)}) custom-call(s32[178]{0:T(256)S(4)} %get-tuple-element.20.meta_ref, bf16[11,128,128]{2,1,0:T(8,128)(2,1)S(1)} %collective-permute-done.halo_ref, bf16[72,128,128]{2,1,0:T(8,128)(2,1)S(1)} %bitcast.5, ...), custom_call_target="tpu_custom_call", output_to_operand_aliasing={{0}: (6, {})} | custom-call | tf_op jit(solution)/shard_map/pallas_call | solution.py:609
  11.5 2.6 %copy-done = f32[91,128,128]{2,1,0:T(8,128)} copy-done((f32[91,128,128]{2,1,0:T(8,128)}, f32[91,128,128]{2,1,0:T(8,128)S(1)}, u32[]{:S(2)}) %copy-start) | copy-done | bytes 5963800
  14.1 0.0 collective-permute-start.1
  14.1 3.9 %collective-permute-start.3 = (bf16[7,128,128]{2,1,0:T(8,128)(2,1)}, bf16[7,128,128]{2,1,0:T(8,128)(2,1)}, u32[]{:S(2)}, u32[]{:S(2)}) collective-permute-start(bf16[7,128,128]{2,1,0:T(8,128)(2,1)} %get-tuple-element.32), channel_id=1, source_target_pairs={{1,2},{3,4},{5,6},{7,8},{9,10},{11,12},{13,14},{2,1},{4,3},{6,5},{... | collective-permute-start | bytes 688136 | tf_op jit(solution)/shard_map/ppermute | solution.py:567
  18.0 0.0 copy-start.1
  18.0 2.7 %copy-done.1 = f32[91,128,128]{2,1,0:T(8,128)S(1)} copy-done((f32[91,128,128]{2,1,0:T(8,128)S(1)}, f32[91,128,128]{2,1,0:T(8,128)}, u32[]{:S(2)}) %copy-start.1) | copy-done | bytes 5963800
  20.7 1.4 %copy-done.6 = bf16[12,256,256]{2,1,0:T(8,128)(2,1)S(1)} copy-done((bf16[12,256,256]{2,1,0:T(8,128)(2,1)S(1)}, bf16[12,256,256]{2,1,0:T(8,128)(2,1)}, u32[]{:S(2)}) %copy-start.6) | copy-done | bytes 1572888
  22.1 1.7 %copy-done.8 = bf16[8,9,128,128]{3,2,1,0:T(8,128)(2,1)S(1)} copy-done((bf16[8,9,128,128]{3,2,1,0:T(8,128)(2,1)S(1)}, bf16[8,9,128,128]{3,2,1,0:T(8,128)(2,1)}, u32[]{:S(2)}) %copy-start.8) | copy-done | bytes 2359320
  23.8 2.6 %copy-done.2 = f32[91,128,128]{2,1,0:T(8,128)} copy-done((f32[91,128,128]{2,1,0:T(8,128)}, f32[91,128,128]{2,1,0:T(8,128)S(1)}, u32[]{:S(2)}) %copy-start.2) | copy-done | bytes 5963800
  26.3 0.0 collective-permute-done.2.halo_ref
  26.3 1.0 %shard_map.77 = (bf16[13,256,256]{2,1,0:T(8,128)(2,1)S(1)}, bf16[4,128,128]{2,1,0:T(8,128)(2,1)S(1)}) custom-call(s32[178]{0:T(256)S(4)} %get-tuple-element.20.meta_ref, s32[1]{0:T(128)S(4)} %get-tuple-element.26.done_ref, bf16[11,128,128]{2,1,0:T(8,128)(2,1)S(1)} %collective-permute-done.2.halo_ref, bf16[12,4,128,256]{3,2,1,0:T(8,128)(2,1)S(1)} %copy-done.4, ...), custom_call_target="tpu_custom_call" | custom-call | tf_op jit(solution)/shard_map/pallas_call | solution.py:629
  27.4 2.6 %collective-permute-start.4 = (bf16[4,128,128]{2,1,0:T(8,128)(2,1)S(1)}, bf16[4,128,128]{2,1,0:T(8,128)(2,1)S(1)}, u32[]{:S(2)}, u32[]{:S(2)}) collective-permute-start(bf16[4,128,128]{2,1,0:T(8,128)(2,1)S(1)} %get-tuple-element.34), channel_id=1, source_target_pairs={{1,2},{3,4},{5,6},{7,8},{9,10},{11,12},{13,14},{2,1},{4,3},{6,5},{... | collective-permute-start | bytes 393224 | tf_op jit(solution)/shard_map/ppermute | solution.py:567
  30.0 0.0 collective-permute-done.1.first_ref
  30.0 2.7 %copy-done.3 = f32[91,128,128]{2,1,0:T(8,128)S(1)} copy-done((f32[91,128,128]{2,1,0:T(8,128)S(1)}, f32[91,128,128]{2,1,0:T(8,128)}, u32[]{:S(2)}) %copy-start.3) | copy-done | bytes 5963800
  32.7 5.2 %shard_map.78 = (f32[91,128,128]{2,1,0:T(8,128)S(1)}, f32[72,128,128]{2,1,0:T(8,128)}, f32[7,128,128]{2,1,0:T(8,128)S(1)}, f32[4,128,128]{2,1,0:T(8,128)S(1)}) custom-call(s32[178]{0:T(256)S(4)} %get-tuple-element.20.meta_ref, bf16[11,128,128]{2,1,0:T(8,128)(2,1)} %collective-permute-done.1.first_ref, ...), custom_call_target="tpu_custom_call", output_to_operand_aliasing={{0}: (7, {})} | custom-call | tf_op jit(solution)/shard_map/pallas_call | solution.py:640
  37.9 0.0 collective-permute-done.3
  37.9 1.0 %convert_add_fusion = f32[7,128,128]{2,1,0:T(8,128)S(1)} fusion(f32[7,128,128]{2,1,0:T(8,128)S(1)} %get-tuple-element.31, bf16[7,128,128]{2,1,0:T(8,128)(2,1)} %collective-permute-done.3), kind=kLoop, calls=%fused_computation | loop fusion | flops 229376 | bytes 1146880 | tf_op jit(solution)/shard_map/add | solution.py:536
  38.9 0.7 %dynamic-slice_dynamic-update-slice_fusion.1 = f32[72,128,128]{2,1,0:T(8,128)} fusion(f32[72,128,128]{2,1,0:T(8,128)} %get-tuple-element.30, s32[]{:T(128)S(6)} %select_n.38, f32[7,128,128]{2,1,0:T(8,128)S(1)} %convert_add_fusion, s32[]{:T(128)S(6)} %select_n.37), kind=kLoop, calls=%fused_computation.3 | loop fusion | bytes 393224 | tf_op jit(solution)/shard_map/dynamic_update_slice | solution.py:542
  39.6 0.7 %dynamic-slice_dynamic-update-slice_fusion = f32[72,128,128]{2,1,0:T(8,128)} fusion(f32[72,128,128]{2,1,0:T(8,128)} %dynamic-slice_dynamic-update-slice_fusion.1, s32[]{:T(128)S(6)} %select_n.40, f32[7,128,128]{2,1,0:T(8,128)S(1)} %convert_add_fusion, s32[]{:T(128)S(6)} %select_n.39), kind=kLoop, calls=%fused_computation.2 | loop fusion | bytes 524296 | tf_op jit(solution)/shard_map/dynamic_update_slice | solution.py:542
  40.3 0.0 collective-permute-done.4
  40.3 0.7 %slice_dynamic-update-slice_fusion.1 = f32[72,128,128]{2,1,0:T(8,128)} fusion(f32[72,128,128]{2,1,0:T(8,128)} %dynamic-slice_dynamic-update-slice_fusion, s32[]{:T(128)S(6)} %select_n.41, f32[4,128,128]{2,1,0:T(8,128)S(1)} %convert_add_fusion.1), kind=kLoop, calls=%fused_computation.5 | loop fusion | bytes 262148 | tf_op jit(solution)/shard_map/dynamic_update_slice | solution.py:542
  41.0 0.7 %slice_dynamic-update-slice_fusion = f32[72,128,128]{2,1,0:T(8,128)} fusion(f32[72,128,128]{2,1,0:T(8,128)} %slice_dynamic-update-slice_fusion.1, s32[]{:T(128)S(6)} %select_n.42, f32[4,128,128]{2,1,0:T(8,128)S(1)} %convert_add_fusion.1), kind=kLoop, calls=%fused_computation.4 | loop fusion | bytes 262148 | tf_op jit(solution)/shard_map/dynamic_update_slice | solution.py:542
  (10 shorter events, 0.0 us)
Async XLA Ops:
  0.0 6.1 %copy-start.4 = (bf16[12,4,128,256]{3,2,1,0:T(8,128)(2,1)S(1)}, bf16[12,4,128,256]{3,2,1,0:T(8,128)(2,1)}, u32[]{:S(2)}) copy-start(bf16[12,4,128,256]{3,2,1,0:T(8,128)(2,1)} %ao_ref.9) | copy-start | bytes 9437188
  0.0 6.1 %copy-start.5 = (bf16[12,256,256]{2,1,0:T(8,128)(2,1)S(1)}, bf16[12,256,256]{2,1,0:T(8,128)(2,1)}, u32[]{:S(2)}) copy-start(bf16[12,256,256]{2,1,0:T(8,128)(2,1)} %kernel_ref.9) | copy-start | bytes 4718596
  0.0 6.1 %copy-start.7 = (bf16[8,9,128,128]{3,2,1,0:T(8,128)(2,1)S(1)}, bf16[8,9,128,128]{3,2,1,0:T(8,128)(2,1)}, u32[]{:S(2)}) copy-start(bf16[8,9,128,128]{3,2,1,0:T(8,128)(2,1)} %param.7) | copy-start | bytes 7077892
  0.0 6.1 %copy-start.9 = (f32[12,256]{1,0:T(8,128)S(1)}, f32[12,256]{1,0:T(8,128)}, u32[]{:S(2)}) copy-start(f32[12,256]{1,0:T(8,128)} %weights_ref.9) | copy-start | bytes 36868
  2.2 6.5 %collective-permute-start = (bf16[11,128,128]{2,1,0:T(8,128)(2,1)S(1)}, bf16[11,128,128]{2,1,0:T(8,128)(2,1)S(1)}, u32[]{:S(2)}, u32[]{:S(2)}) collective-permute-start(bf16[11,128,128]{2,1,0:T(8,128)(2,1)S(1)} %get-tuple-element.21), channel_id=1, source_target_pairs={{0,1},{2,3},{4,5},{6,7},{8,9},{10,11},{12,13},{14,15},{1,0},{3,2},... | collective-permute-start | bytes 1081352 | tf_op jit(solution)/shard_map/ppermute | solution.py:561
  2.9 23.4 %collective-permute-start.2 = (bf16[11,128,128]{2,1,0:T(8,128)(2,1)}, bf16[11,128,128]{2,1,0:T(8,128)(2,1)S(1)}, u32[]{:S(2)}, u32[]{:S(2)}) collective-permute-start(bf16[11,128,128]{2,1,0:T(8,128)(2,1)} %get-tuple-element.27), channel_id=1, source_target_pairs={{1,2},{3,4},{5,6},{7,8},{9,10},{11,12},{13,14},{2,1},{4,3},{6,5},{... | collective-permute-start | bytes 1081352 | tf_op jit(solution)/shard_map/ppermute | solution.py:567
  11.5 2.6 %copy-start = (f32[91,128,128]{2,1,0:T(8,128)}, f32[91,128,128]{2,1,0:T(8,128)S(1)}, u32[]{:S(2)}) copy-start(f32[91,128,128]{2,1,0:T(8,128)S(1)} %get-tuple-element.25.acc_in) | copy-start | bytes 17891332
  14.1 15.9 %collective-permute-start.1 = (bf16[11,128,128]{2,1,0:T(8,128)(2,1)}, bf16[11,128,128]{2,1,0:T(8,128)(2,1)}, u32[]{:S(2)}, u32[]{:S(2)}) collective-permute-start(bf16[11,128,128]{2,1,0:T(8,128)(2,1)} %get-tuple-element.24), channel_id=1, source_target_pairs={{0,1},{2,3},{4,5},{6,7},{8,9},{10,11},{12,13},{14,15},{1,0},{3,2},... | collective-permute-start | bytes 1081352 | tf_op jit(solution)/shard_map/ppermute | solution.py:561
  14.1 23.8 %collective-permute-start.3 = (bf16[7,128,128]{2,1,0:T(8,128)(2,1)}, bf16[7,128,128]{2,1,0:T(8,128)(2,1)}, u32[]{:S(2)}, u32[]{:S(2)}) collective-permute-start(bf16[7,128,128]{2,1,0:T(8,128)(2,1)} %get-tuple-element.32), channel_id=1, source_target_pairs={{1,2},{3,4},{5,6},{7,8},{9,10},{11,12},{13,14},{2,1},{4,3},{6,5},{... | collective-permute-start | bytes 688136 | tf_op jit(solution)/shard_map/ppermute | solution.py:567
  18.0 2.7 %copy-start.1 = (f32[91,128,128]{2,1,0:T(8,128)S(1)}, f32[91,128,128]{2,1,0:T(8,128)}, u32[]{:S(2)}) copy-start(f32[91,128,128]{2,1,0:T(8,128)} %copy-done) | copy-start | bytes 17891332
  20.7 1.4 %copy-start.6 = (bf16[12,256,256]{2,1,0:T(8,128)(2,1)S(1)}, bf16[12,256,256]{2,1,0:T(8,128)(2,1)}, u32[]{:S(2)}) copy-start(bf16[12,256,256]{2,1,0:T(8,128)(2,1)} %kernel_ref.9) | copy-start | bytes 4718596
  22.1 1.7 %copy-start.8 = (bf16[8,9,128,128]{3,2,1,0:T(8,128)(2,1)S(1)}, bf16[8,9,128,128]{3,2,1,0:T(8,128)(2,1)}, u32[]{:S(2)}) copy-start(bf16[8,9,128,128]{3,2,1,0:T(8,128)(2,1)} %param.7) | copy-start | bytes 7077892
  23.8 2.6 %copy-start.2 = (f32[91,128,128]{2,1,0:T(8,128)}, f32[91,128,128]{2,1,0:T(8,128)S(1)}, u32[]{:S(2)}) copy-start(f32[91,128,128]{2,1,0:T(8,128)S(1)} %get-tuple-element.29.acc_in) | copy-start | bytes 17891332
  27.4 12.9 %collective-permute-start.4 = (bf16[4,128,128]{2,1,0:T(8,128)(2,1)S(1)}, bf16[4,128,128]{2,1,0:T(8,128)(2,1)S(1)}, u32[]{:S(2)}, u32[]{:S(2)}) collective-permute-start(bf16[4,128,128]{2,1,0:T(8,128)(2,1)S(1)} %get-tuple-element.34), channel_id=1, source_target_pairs={{1,2},{3,4},{5,6},{7,8},{9,10},{11,12},{13,14},{2,1},{4,3},{6,5},{... | collective-permute-start | bytes 393224 | tf_op jit(solution)/shard_map/ppermute | solution.py:567
  30.0 2.7 %copy-start.3 = (f32[91,128,128]{2,1,0:T(8,128)S(1)}, f32[91,128,128]{2,1,0:T(8,128)}, u32[]{:S(2)}) copy-start(f32[91,128,128]{2,1,0:T(8,128)} %copy-done.2) | copy-start | bytes 17891332

commit v12 on v5

--- a/solution.py
+++ b/solution.py
@@ -163,20 +163,19 @@
     index = lax.axis_index("blk")
     odd = index % 2 == 1
 
-    def copies(up, down):
-        return [
-            pltpu.make_async_copy(
-                density_ref.at[pl.ds(start, count)], ref.at[pl.ds(place, count)], sems.at[side, i]
+    by_size = lambda pack: sorted(pack, key=lambda segment: segment[2])
+    copies = []
+    for side, (ref, upper) in enumerate(((cross_ref, odd), (near_ref, jnp.logical_not(odd)))):
+        for i, (up, down) in enumerate(zip(*(by_size(pack) for pack in geo.packs))):
+            start = jnp.where(upper, up[0], down[0])
+            place = jnp.where(upper, up[1], down[1])
+            copies.append(
+                pltpu.make_async_copy(
+                    density_ref.at[pl.ds(start, up[2])], ref.at[pl.ds(place, up[2])], sems.at[side, i]
+                )
             )
-            for side, (pack, ref) in enumerate(zip(geo.packs, (up, down)))
-            for i, (start, place, count) in enumerate(pack)
-        ]
-
-    def start(up, down):
-        for copy in copies(up, down):
-            copy.start()
-
-    by_parity(odd, start, near_ref, cross_ref)
+    for copy in copies:
+        copy.start()
     scalars = [
         pltpu.make_async_copy(*pair, sems.at[2, i])
         for i, pair in enumerate(
@@ -190,7 +189,7 @@
     for copy in scalars:
         copy.wait()
     build_lists(geo, index, centre_ref, offsets_ref, counts_ref, meta_ref)
-    for copy in copies(near_ref, cross_ref):
+    for copy in copies:
         copy.wait()
 
 

time: 24.2 us -> 24.3 us (level)
  starting transfers between devices: 12.1 us -> 12.9 us
  Pallas kernels: 10.5 us -> 9.99 us
    ppermute x3, starting transfers between devices: 11.9 us -> 12.7 us  [to_second(): got = lax.ppermute(x, 'blk', pairs + [(j, i) for i, j in pairs])]
    pallas_call x1, Pallas kernels: 1.3 us -> 0.7 us  [local(): call(functools.partial(waiting_kernel, geo), (acc_type, pltpu.SMEM((1,),...]
  transfers between devices with their start and end apart: 5 -> 5, of which waited for: 1 -> 1; matrix products, arithmetic and copies ran while one was open for 0% -> 0% of each run, Pallas kernels for 34% -> 31%
where the time goes in v12:
time: 24.3 us; the launch traced here: 24.1 us
  starting transfers between devices  12.9 us (53%)
  Pallas kernels  9.99 us (41%)
  waiting for transfers between devices  1.03 us (4%)
    ppermute x3, starting transfers between devices, to_second(): got = lax.ppermute(x, 'blk', pairs + [(j, i) for i, j in pairs])  12.7 us
    pallas_call x1, Pallas kernels, local(): call(functools.partial(near_kernel, geo), (acc_type, pack(geo.halo)), [SM...  2.73 us
    pallas_call x1, Pallas kernels, local(): call(functools.partial(inner_kernel, geo), (acc_type, whole), [SMEM_SPEC]...  2.12 us
    pallas_call x1, Pallas kernels, local(): call(functools.partial(pack_kernel, geo), (pack(geo.halo),) * 2 + (pltpu....  1.56 us
    pallas_call x1, Pallas kernels, local(): call(functools.partial(early_kernel, geo), (acc_type, pack(geo.early)), [...  1.24 us
    ppermute x3, waiting for transfers between devices, to_second(): got = lax.ppermute(x, 'blk', pairs + [(j, i) for i, j in pairs])  1.02 us
    pallas_call x1, Pallas kernels, local(): call(functools.partial(finish_kernel, geo), whole, [SMEM_SPEC] + [VMEM_SP...  0.9 us
    pallas_call x1, Pallas kernels, local(): call(functools.partial(late_kernel, geo), (h_type, pack(geo.late)), [SMEM...  0.75 us
  transfers between devices with their start and end apart: 5, of which 1 were waited for; matrix products, arithmetic and copies ran while one was open for 0% of the time, Pallas kernels for 31%

profile of v12, /device:TPU:1, one launch (start us, length us, event | category | flops | bytes accessed | tf_op | source)
XLA Modules:
  0.0 24.1 jit_solution(7719345291883999804)
XLA Ops:
  0.0 0.0 copy-start
  0.0 0.0 copy-start.1
  0.0 0.0 copy-start.2
  0.0 0.0 copy-start.3
  0.0 1.6 %shard_map.73 = (bf16[11,128,128]{2,1,0:T(8,128)(2,1)S(1)}, bf16[11,128,128]{2,1,0:T(8,128)(2,1)S(1)}, s32[178]{0:T(256)S(4)}, f32[91,128,128]{2,1,0:T(8,128)S(1)}) custom-call(bf16[72,128,128]{2,1,0:T(8,128)(2,1)} %bitcast.3, s32[12]{0:T(128)} %centre_in.1, s32[4,12]{1,0:T(4,128)} %bitcast.8, s32[12]{0:T(128)} %counts_in.1), custom_call_target="tpu_custom_call" | custom-call | flops 10000000000 | bytes 100000000 | tf_op jit(solution)/shard_map/pallas_call | solution.py:586
  1.6 0.1 collective-permute-start.1
  1.7 4.6 %collective-permute-start.2 = (bf16[11,128,128]{2,1,0:T(8,128)(2,1)S(1)}, bf16[11,128,128]{2,1,0:T(8,128)(2,1)S(1)}, u32[]{:S(2)}, u32[]{:S(2)}) collective-permute-start(bf16[11,128,128]{2,1,0:T(8,128)(2,1)S(1)} %get-tuple-element.26), channel_id=1, source_target_pairs={{1,2},{3,4},{5,6},{7,8},{9,10},{11,12},{13,14},{2,1},{4,3},{6,5},{... | collective-permute-start | bytes 1081352 | tf_op jit(solution)/shard_map/ppermute | solution.py:571
  6.3 0.0 copy-done
  6.3 0.0 copy-done.1
  6.4 0.0 copy-done.2
  6.4 0.0 copy-done.3
  6.4 1.2 %shard_map.74 = (f32[91,128,128]{2,1,0:T(8,128)S(1)}, bf16[7,128,128]{2,1,0:T(8,128)(2,1)S(1)}) custom-call(s32[178]{0:T(256)S(4)} %get-tuple-element.19.meta_ref, bf16[72,128,128]{2,1,0:T(8,128)(2,1)S(1)} %bitcast.4, bf16[12,4,128,256]{3,2,1,0:T(8,128)(2,1)S(1)} %copy-done, bf16[12,256,256]{2,1,0:T(8,128)(2,1)S(1)} %copy-done.1, ...), custom_call_target="tpu_custom_call", output_to_operand_aliasing={{0}: (5, {})} | custom-call | tf_op jit(solution)/shard_map/pallas_call | solution.py:603
  7.6 0.0 collective-permute-done.1.halo_ref
  7.6 2.7 %shard_map.75 = (f32[91,128,128]{2,1,0:T(8,128)S(1)}, bf16[11,128,128]{2,1,0:T(8,128)(2,1)S(1)}) custom-call(s32[178]{0:T(256)S(4)} %get-tuple-element.19.meta_ref, bf16[11,128,128]{2,1,0:T(8,128)(2,1)S(1)} %collective-permute-done.1.halo_ref, bf16[72,128,128]{2,1,0:T(8,128)(2,1)S(1)} %bitcast.5, ...), custom_call_target="tpu_custom_call", output_to_operand_aliasing={{0}: (6, {})} | custom-call | tf_op jit(solution)/shard_map/pallas_call | solution.py:613
  10.4 0.1 collective-permute-start.4
  10.4 3.5 %collective-permute-start = (bf16[7,128,128]{2,1,0:T(8,128)(2,1)S(1)}, bf16[7,128,128]{2,1,0:T(8,128)(2,1)S(1)}, u32[]{:S(2)}, u32[]{:S(2)}) collective-permute-start(bf16[7,128,128]{2,1,0:T(8,128)(2,1)S(1)} %get-tuple-element.21), channel_id=1, source_target_pairs={{1,2},{3,4},{5,6},{7,8},{9,10},{11,12},{13,14},{2,1},{4,3},{6,5},{... | collective-permute-start | bytes 688136 | tf_op jit(solution)/shard_map/ppermute | solution.py:571
  14.0 0.7 %shard_map.76 = (f32[91,128,128]{2,1,0:T(8,128)S(1)}, s32[1]{0:T(128)S(4)}) custom-call(s32[178]{0:T(256)S(4)} %get-tuple-element.19.meta_ref, bf16[72,128,128]{2,1,0:T(8,128)(2,1)S(1)} %bitcast.6, bf16[12,4,128,256]{3,2,1,0:T(8,128)(2,1)S(1)} %copy-done, bf16[12,256,256]{2,1,0:T(8,128)(2,1)S(1)} %copy-done.1, ...), custom_call_target="tpu_custom_call", output_to_operand_aliasing={{0}: (5, {})} | custom-call | tf_op jit(solution)/shard_map/pallas_call | solution.py:623
  14.7 0.0 collective-permute-done.2.halo_ref
  14.7 0.8 %shard_map.77 = (bf16[13,256,256]{2,1,0:T(8,128)(2,1)S(1)}, bf16[4,128,128]{2,1,0:T(8,128)(2,1)S(1)}) custom-call(s32[178]{0:T(256)S(4)} %get-tuple-element.19.meta_ref, s32[1]{0:T(128)S(4)} %get-tuple-element.25.done_ref, bf16[11,128,128]{2,1,0:T(8,128)(2,1)S(1)} %collective-permute-done.2.halo_ref, bf16[12,4,128,256]{3,2,1,0:T(8,128)(2,1)S(1)} %copy-done, ...), custom_call_target="tpu_custom_call" | custom-call | tf_op jit(solution)/shard_map/pallas_call | solution.py:633
  15.4 4.5 %collective-permute-start.3 = (bf16[4,128,128]{2,1,0:T(8,128)(2,1)S(1)}, bf16[4,128,128]{2,1,0:T(8,128)(2,1)S(1)}, u32[]{:S(2)}, u32[]{:S(2)}) collective-permute-start(bf16[4,128,128]{2,1,0:T(8,128)(2,1)S(1)} %get-tuple-element.27), channel_id=1, source_target_pairs={{1,2},{3,4},{5,6},{7,8},{9,10},{11,12},{13,14},{2,1},{4,3},{6,5},{... | collective-permute-start | bytes 393224 | tf_op jit(solution)/shard_map/ppermute | solution.py:571
  20.0 0.0 collective-permute-done.4.first_ref
  20.0 2.1 %shard_map.78 = (f32[91,128,128]{2,1,0:T(8,128)S(1)}, f32[72,128,128]{2,1,0:T(8,128)}) custom-call(s32[178]{0:T(256)S(4)} %get-tuple-element.19.meta_ref, bf16[11,128,128]{2,1,0:T(8,128)(2,1)S(1)} %collective-permute-done.4.first_ref, bf16[72,128,128]{2,1,0:T(8,128)(2,1)S(1)} %bitcast.7, ...), custom_call_target="tpu_custom_call", output_to_operand_aliasing={{0}: (7, {})} | custom-call | tf_op jit(solution)/shard_map/pallas_call | solution.py:643
  22.1 0.0 collective-permute-done.early_ref
  22.1 1.0 %collective-permute-done.3.late_ref = bf16[4,128,128]{2,1,0:T(8,128)(2,1)S(1)} collective-permute-done((bf16[4,128,128]{2,1,0:T(8,128)(2,1)S(1)}, bf16[4,128,128]{2,1,0:T(8,128)(2,1)S(1)}, u32[]{:S(2)}, u32[]{:S(2)}) %collective-permute-start.3) | collective-permute-done | bytes 131104 | tf_op jit(solution)/shard_map/ppermute | solution.py:571
  23.2 0.9 %shard_map.79 = f32[72,128,128]{2,1,0:T(8,128)} custom-call(s32[178]{0:T(256)S(4)} %get-tuple-element.19.meta_ref, bf16[7,128,128]{2,1,0:T(8,128)(2,1)S(1)} %collective-permute-done.early_ref, bf16[4,128,128]{2,1,0:T(8,128)(2,1)S(1)} %collective-permute-done.3.late_ref, ...), custom_call_target="tpu_custom_call", output_to_operand_aliasing={{}: (4, {})} | custom-call | tf_op jit(solution)/shard_map/pallas_call | solution.py:653
Async XLA Ops:
  0.0 6.3 %copy-start = (bf16[12,4,128,256]{3,2,1,0:T(8,128)(2,1)S(1)}, bf16[12,4,128,256]{3,2,1,0:T(8,128)(2,1)}, u32[]{:S(2)}) copy-start(bf16[12,4,128,256]{3,2,1,0:T(8,128)(2,1)} %ao_ref.9) | copy-start | bytes 9437188
  0.0 6.3 %copy-start.1 = (bf16[12,256,256]{2,1,0:T(8,128)(2,1)S(1)}, bf16[12,256,256]{2,1,0:T(8,128)(2,1)}, u32[]{:S(2)}) copy-start(bf16[12,256,256]{2,1,0:T(8,128)(2,1)} %kernel_ref.9) | copy-start | bytes 4718596
  0.0 6.4 %copy-start.2 = (bf16[8,9,128,128]{3,2,1,0:T(8,128)(2,1)S(1)}, bf16[8,9,128,128]{3,2,1,0:T(8,128)(2,1)}, u32[]{:S(2)}) copy-start(bf16[8,9,128,128]{3,2,1,0:T(8,128)(2,1)} %param.7) | copy-start | bytes 7077892
  0.0 6.4 %copy-start.3 = (f32[12,256]{1,0:T(8,128)S(1)}, f32[12,256]{1,0:T(8,128)}, u32[]{:S(2)}) copy-start(f32[12,256]{1,0:T(8,128)} %weights_ref.9) | copy-start | bytes 36868
  1.6 6.0 %collective-permute-start.1 = (bf16[11,128,128]{2,1,0:T(8,128)(2,1)S(1)}, bf16[11,128,128]{2,1,0:T(8,128)(2,1)S(1)}, u32[]{:S(2)}, u32[]{:S(2)}) collective-permute-start(bf16[11,128,128]{2,1,0:T(8,128)(2,1)S(1)} %get-tuple-element.22), channel_id=1, source_target_pairs={{0,1},{2,3},{4,5},{6,7},{8,9},{10,11},{12,13},{14,15},{1,0},{3,2},... | collective-permute-start | bytes 1081352 | tf_op jit(solution)/shard_map/ppermute | solution.py:565
  1.7 13.0 %collective-permute-start.2 = (bf16[11,128,128]{2,1,0:T(8,128)(2,1)S(1)}, bf16[11,128,128]{2,1,0:T(8,128)(2,1)S(1)}, u32[]{:S(2)}, u32[]{:S(2)}) collective-permute-start(bf16[11,128,128]{2,1,0:T(8,128)(2,1)S(1)} %get-tuple-element.26), channel_id=1, source_target_pairs={{1,2},{3,4},{5,6},{7,8},{9,10},{11,12},{13,14},{2,1},{4,3},{6,5},{... | collective-permute-start | bytes 1081352 | tf_op jit(solution)/shard_map/ppermute | solution.py:571
  10.4 9.6 %collective-permute-start.4 = (bf16[11,128,128]{2,1,0:T(8,128)(2,1)S(1)}, bf16[11,128,128]{2,1,0:T(8,128)(2,1)S(1)}, u32[]{:S(2)}, u32[]{:S(2)}) collective-permute-start(bf16[11,128,128]{2,1,0:T(8,128)(2,1)S(1)} %get-tuple-element.28), channel_id=1, source_target_pairs={{0,1},{2,3},{4,5},{6,7},{8,9},{10,11},{12,13},{14,15},{1,0},{3,2},... | collective-permute-start | bytes 1081352 | tf_op jit(solution)/shard_map/ppermute | solution.py:565
  10.4 11.7 %collective-permute-start = (bf16[7,128,128]{2,1,0:T(8,128)(2,1)S(1)}, bf16[7,128,128]{2,1,0:T(8,128)(2,1)S(1)}, u32[]{:S(2)}, u32[]{:S(2)}) collective-permute-start(bf16[7,128,128]{2,1,0:T(8,128)(2,1)S(1)} %get-tuple-element.21), channel_id=1, source_target_pairs={{1,2},{3,4},{5,6},{7,8},{9,10},{11,12},{13,14},{2,1},{4,3},{6,5},{... | collective-permute-start | bytes 688136 | tf_op jit(solution)/shard_map/ppermute | solution.py:571
  15.4 7.7 %collective-permute-start.3 = (bf16[4,128,128]{2,1,0:T(8,128)(2,1)S(1)}, bf16[4,128,128]{2,1,0:T(8,128)(2,1)S(1)}, u32[]{:S(2)}, u32[]{:S(2)}) collective-permute-start(bf16[4,128,128]{2,1,0:T(8,128)(2,1)S(1)} %get-tuple-element.27), channel_id=1, source_target_pairs={{1,2},{3,4},{5,6},{7,8},{9,10},{11,12},{13,14},{2,1},{4,3},{6,5},{... | collective-permute-start | bytes 393224 | tf_op jit(solution)/shard_map/ppermute | solution.py:571

commit v13 on v10

--- a/solution.py
+++ b/solution.py
@@ -163,20 +163,19 @@
     index = lax.axis_index("blk")
     odd = index % 2 == 1
 
-    def copies(up, down):
-        return [
-            pltpu.make_async_copy(
-                density_ref.at[pl.ds(start, count)], ref.at[pl.ds(place, count)], sems.at[side, i]
+    by_size = lambda pack: sorted(pack, key=lambda segment: segment[2])
+    copies = []
+    for side, (ref, upper) in enumerate(((cross_ref, odd), (near_ref, jnp.logical_not(odd)))):
+        for i, (up, down) in enumerate(zip(*(by_size(pack) for pack in geo.packs))):
+            start = jnp.where(upper, up[0], down[0])
+            place = jnp.where(upper, up[1], down[1])
+            copies.append(
+                pltpu.make_async_copy(
+                    density_ref.at[pl.ds(start, up[2])], ref.at[pl.ds(place, up[2])], sems.at[side, i]
+                )
             )
-            for side, (pack, ref) in enumerate(zip(geo.packs, (up, down)))
-            for i, (start, place, count) in enumerate(pack)
-        ]
-
-    def start(up, down):
-        for copy in copies(up, down):
-            copy.start()
-
-    by_parity(odd, start, near_ref, cross_ref)
+    for copy in copies:
+        copy.start()
     scalars = [
         pltpu.make_async_copy(*pair, sems.at[2, i])
         for i, pair in enumerate(
@@ -190,7 +189,7 @@
     for copy in scalars:
         copy.wait()
     build_lists(geo, index, centre_ref, offsets_ref, counts_ref, meta_ref)
-    for copy in copies(near_ref, cross_ref):
+    for copy in copies:
         copy.wait()
 
 

time: 24 us -> 24.1 us (level)
    pallas_call x1, Pallas kernels: 1.24 us -> 2.25 us  [local(): call(functools.partial(early_kernel, geo), (acc_type, pack(geo.early)), [...]
    pallas_call x1, Pallas kernels: 2.73 us -> 1.72 us  [local(): call(functools.partial(near_kernel, geo), (acc_type, pack(geo.halo)), [SM...]
    pallas_call x1, Pallas kernels: 1.3 us -> 0.7 us  [local(): call(functools.partial(waiting_kernel, geo), (acc_type, pltpu.SMEM((1,),...]
    pallas_call x1, Pallas kernels: 0.75 us -> 1.04 us  [local(): call(functools.partial(late_kernel, geo), (h_type, pack(geo.late)), [SMEM...]
  transfers between devices with their start and end apart: 5 -> 5, of which waited for: 1 -> 1; matrix products, arithmetic and copies ran while one was open for 0% -> 0% of each run, Pallas kernels for 38% -> 37%
where the time goes in v13:
time: 24.1 us; the launch traced here: 23.7 us
  starting transfers between devices  12.3 us (51%)
  Pallas kernels  11.1 us (46%)
    ppermute x3, starting transfers between devices, to_second(): got = lax.ppermute(x, 'blk', pairs + [(j, i) for i, j in pairs])  12.1 us
    pallas_call x1, Pallas kernels, local(): call(functools.partial(early_kernel, geo), (acc_type, pack(geo.early)), [...  2.25 us
    pallas_call x1, Pallas kernels, local(): call(functools.partial(inner_kernel, geo), (acc_type, whole), [SMEM_SPEC]...  2.19 us
    pallas_call x1, Pallas kernels, local(): call(functools.partial(near_kernel, geo), (acc_type, pack(geo.halo)), [SM...  1.72 us
    pallas_call x2, Pallas kernels, local(): call(functools.partial(kernel_of, geo), whole, [SMEM_SPEC] + [VMEM_SPEC]...  1.63 us
    pallas_call x1, Pallas kernels, local(): call(functools.partial(pack_kernel, geo), (pack(geo.halo),) * 2 + (pltpu....  1.56 us
    pallas_call x1, Pallas kernels, local(): call(functools.partial(late_kernel, geo), (h_type, pack(geo.late)), [SMEM...  1.04 us
    pallas_call x1, Pallas kernels, local(): call(functools.partial(waiting_kernel, geo), (acc_type, pltpu.SMEM((1,),...  0.7 us
  transfers between devices with their start and end apart: 5, of which 1 were waited for; matrix products, arithmetic and copies ran while one was open for 0% of the time, Pallas kernels for 37%

profile of v13, /device:TPU:1, one launch (start us, length us, event | category | flops | bytes accessed | tf_op | source)
XLA Modules:
  0.0 23.7 jit_solution(7805986590265642267)
XLA Ops:
  0.0 0.0 copy-start
  0.0 0.0 copy-start.1
  0.0 0.0 copy-start.2
  0.0 0.0 copy-start.3
  0.0 1.6 %shard_map.73 = (bf16[11,128,128]{2,1,0:T(8,128)(2,1)S(1)}, bf16[11,128,128]{2,1,0:T(8,128)(2,1)S(1)}, s32[178]{0:T(256)S(4)}, f32[91,128,128]{2,1,0:T(8,128)S(1)}) custom-call(bf16[72,128,128]{2,1,0:T(8,128)(2,1)} %bitcast.3, s32[12]{0:T(128)} %centre_in.1, s32[4,12]{1,0:T(4,128)} %bitcast.8, s32[12]{0:T(128)} %counts_in.1), custom_call_target="tpu_custom_call" | custom-call | flops 10000000000 | bytes 100000000 | tf_op jit(solution)/shard_map/pallas_call | solution.py:617
  1.6 0.1 collective-permute-start
  1.7 4.6 %collective-permute-start.1 = (bf16[11,128,128]{2,1,0:T(8,128)(2,1)S(1)}, bf16[11,128,128]{2,1,0:T(8,128)(2,1)S(1)}, u32[]{:S(2)}, u32[]{:S(2)}) collective-permute-start(bf16[11,128,128]{2,1,0:T(8,128)(2,1)S(1)} %get-tuple-element.25), channel_id=1, source_target_pairs={{1,2},{3,4},{5,6},{7,8},{9,10},{11,12},{13,14},{2,1},{4,3},{6,5},{... | collective-permute-start | bytes 1081352 | tf_op jit(solution)/shard_map/ppermute | solution.py:602
  6.3 0.0 copy-done
  6.3 0.0 copy-done.1
  6.4 0.0 copy-done.2
  6.4 0.0 copy-done.3
  6.4 2.2 %shard_map.74 = (f32[91,128,128]{2,1,0:T(8,128)S(1)}, bf16[7,128,128]{2,1,0:T(8,128)(2,1)S(1)}) custom-call(s32[178]{0:T(256)S(4)} %get-tuple-element.19.meta_ref, bf16[72,128,128]{2,1,0:T(8,128)(2,1)S(1)} %bitcast.4, bf16[12,4,128,256]{3,2,1,0:T(8,128)(2,1)S(1)} %copy-done, bf16[12,256,256]{2,1,0:T(8,128)(2,1)S(1)} %copy-done.1, ...), custom_call_target="tpu_custom_call", output_to_operand_aliasing={{0}: (5, {})} | custom-call | tf_op jit(solution)/shard_map/pallas_call | solution.py:634
  8.6 0.0 collective-permute-done.halo_ref
  8.6 1.7 %shard_map.75 = (f32[91,128,128]{2,1,0:T(8,128)S(1)}, bf16[11,128,128]{2,1,0:T(8,128)(2,1)S(1)}) custom-call(s32[178]{0:T(256)S(4)} %get-tuple-element.19.meta_ref, bf16[11,128,128]{2,1,0:T(8,128)(2,1)S(1)} %collective-permute-done.halo_ref, bf16[72,128,128]{2,1,0:T(8,128)(2,1)S(1)} %bitcast.5, ...), custom_call_target="tpu_custom_call", output_to_operand_aliasing={{0}: (6, {})} | custom-call | tf_op jit(solution)/shard_map/pallas_call | solution.py:644
  10.4 0.1 collective-permute-start.4
  10.5 3.5 %collective-permute-start.3 = (bf16[7,128,128]{2,1,0:T(8,128)(2,1)S(1)}, bf16[7,128,128]{2,1,0:T(8,128)(2,1)S(1)}, u32[]{:S(2)}, u32[]{:S(2)}) collective-permute-start(bf16[7,128,128]{2,1,0:T(8,128)(2,1)S(1)} %get-tuple-element.27), channel_id=1, source_target_pairs={{1,2},{3,4},{5,6},{7,8},{9,10},{11,12},{13,14},{2,1},{4,3},{6,5},{... | collective-permute-start | bytes 688136 | tf_op jit(solution)/shard_map/ppermute | solution.py:602
  14.0 0.7 %shard_map.76 = (f32[91,128,128]{2,1,0:T(8,128)S(1)}, s32[1]{0:T(128)S(4)}) custom-call(s32[178]{0:T(256)S(4)} %get-tuple-element.19.meta_ref, bf16[72,128,128]{2,1,0:T(8,128)(2,1)S(1)} %bitcast.6, bf16[12,4,128,256]{3,2,1,0:T(8,128)(2,1)S(1)} %copy-done, bf16[12,256,256]{2,1,0:T(8,128)(2,1)S(1)} %copy-done.1, ...), custom_call_target="tpu_custom_call", output_to_operand_aliasing={{0}: (5, {})} | custom-call | tf_op jit(solution)/shard_map/pallas_call | solution.py:654
  14.7 0.0 collective-permute-done.1.halo_ref
  14.7 1.0 %shard_map.77 = (bf16[13,256,256]{2,1,0:T(8,128)(2,1)S(1)}, bf16[4,128,128]{2,1,0:T(8,128)(2,1)S(1)}) custom-call(s32[178]{0:T(256)S(4)} %get-tuple-element.19.meta_ref, s32[1]{0:T(128)S(4)} %get-tuple-element.24.done_ref, bf16[11,128,128]{2,1,0:T(8,128)(2,1)S(1)} %collective-permute-done.1.halo_ref, bf16[12,4,128,256]{3,2,1,0:T(8,128)(2,1)S(1)} %copy-done, ...), custom_call_target="tpu_custom_call" | custom-call | tf_op jit(solution)/shard_map/pallas_call | solution.py:664
  15.8 3.9 %collective-permute-start.2 = (bf16[4,128,128]{2,1,0:T(8,128)(2,1)S(1)}, bf16[4,128,128]{2,1,0:T(8,128)(2,1)S(1)}, u32[]{:S(2)}, u32[]{:S(2)}) collective-permute-start(bf16[4,128,128]{2,1,0:T(8,128)(2,1)S(1)} %get-tuple-element.26), channel_id=1, source_target_pairs={{1,2},{3,4},{5,6},{7,8},{9,10},{11,12},{13,14},{2,1},{4,3},{6,5},{... | collective-permute-start | bytes 393224 | tf_op jit(solution)/shard_map/ppermute | solution.py:602
  19.7 0.0 collective-permute-done.4.first_ref
  19.7 2.2 %shard_map.78 = (f32[91,128,128]{2,1,0:T(8,128)S(1)}, f32[72,128,128]{2,1,0:T(8,128)}) custom-call(s32[178]{0:T(256)S(4)} %get-tuple-element.19.meta_ref, bf16[11,128,128]{2,1,0:T(8,128)(2,1)S(1)} %collective-permute-done.4.first_ref, bf16[72,128,128]{2,1,0:T(8,128)(2,1)S(1)} %bitcast.7, ...), custom_call_target="tpu_custom_call", output_to_operand_aliasing={{0}: (7, {})} | custom-call | tf_op jit(solution)/shard_map/pallas_call | solution.py:674
  21.9 0.0 collective-permute-done.3.early_ref
  21.9 0.9 %shard_map.79.out_in = f32[72,128,128]{2,1,0:T(8,128)} custom-call(s32[178]{0:T(256)S(4)} %get-tuple-element.19.meta_ref, bf16[7,128,128]{2,1,0:T(8,128)(2,1)S(1)} %collective-permute-done.3.early_ref, f32[91,128,128]{2,1,0:T(8,128)S(1)} %get-tuple-element.31.acc_ref, f32[72,128,128]{2,1,0:T(8,128)} %get-tuple-element.32.out_in), custom_call_target="tpu_custom_call", output_to_operand_aliasing={{}: (3, {})} | custom-call | tf_op jit(solution)/shard_map/pallas_call | solution.py:687
  22.8 0.2 collective-permute-done.2.late_ref
  23.0 0.7 %shard_map.80 = f32[72,128,128]{2,1,0:T(8,128)} custom-call(s32[178]{0:T(256)S(4)} %get-tuple-element.19.meta_ref, bf16[4,128,128]{2,1,0:T(8,128)(2,1)S(1)} %collective-permute-done.2.late_ref, bf16[7,128,128]{2,1,0:T(8,128)(2,1)S(1)} %collective-permute-done.3.early_ref, ...), custom_call_target="tpu_custom_call", output_to_operand_aliasing={{}: (4, {})} | custom-call | tf_op jit(solution)/shard_map/pallas_call | solution.py:687
Async XLA Ops:
  0.0 6.3 %copy-start = (bf16[12,4,128,256]{3,2,1,0:T(8,128)(2,1)S(1)}, bf16[12,4,128,256]{3,2,1,0:T(8,128)(2,1)}, u32[]{:S(2)}) copy-start(bf16[12,4,128,256]{3,2,1,0:T(8,128)(2,1)} %ao_ref.9) | copy-start | bytes 9437188
  0.0 6.3 %copy-start.1 = (bf16[12,256,256]{2,1,0:T(8,128)(2,1)S(1)}, bf16[12,256,256]{2,1,0:T(8,128)(2,1)}, u32[]{:S(2)}) copy-start(bf16[12,256,256]{2,1,0:T(8,128)(2,1)} %kernel_ref.9) | copy-start | bytes 4718596
  0.0 6.4 %copy-start.2 = (bf16[8,9,128,128]{3,2,1,0:T(8,128)(2,1)S(1)}, bf16[8,9,128,128]{3,2,1,0:T(8,128)(2,1)}, u32[]{:S(2)}) copy-start(bf16[8,9,128,128]{3,2,1,0:T(8,128)(2,1)} %param.7) | copy-start | bytes 7077892
  0.0 6.4 %copy-start.3 = (f32[12,256]{1,0:T(8,128)S(1)}, f32[12,256]{1,0:T(8,128)}, u32[]{:S(2)}) copy-start(f32[12,256]{1,0:T(8,128)} %weights_ref.9) | copy-start | bytes 36868
  1.6 7.1 %collective-permute-start = (bf16[11,128,128]{2,1,0:T(8,128)(2,1)S(1)}, bf16[11,128,128]{2,1,0:T(8,128)(2,1)S(1)}, u32[]{:S(2)}, u32[]{:S(2)}) collective-permute-start(bf16[11,128,128]{2,1,0:T(8,128)(2,1)S(1)} %get-tuple-element.20), channel_id=1, source_target_pairs={{0,1},{2,3},{4,5},{6,7},{8,9},{10,11},{12,13},{14,15},{1,0},{3,2},... | collective-permute-start | bytes 1081352 | tf_op jit(solution)/shard_map/ppermute | solution.py:596
  1.7 13.0 %collective-permute-start.1 = (bf16[11,128,128]{2,1,0:T(8,128)(2,1)S(1)}, bf16[11,128,128]{2,1,0:T(8,128)(2,1)S(1)}, u32[]{:S(2)}, u32[]{:S(2)}) collective-permute-start(bf16[11,128,128]{2,1,0:T(8,128)(2,1)S(1)} %get-tuple-element.25), channel_id=1, source_target_pairs={{1,2},{3,4},{5,6},{7,8},{9,10},{11,12},{13,14},{2,1},{4,3},{6,5},{... | collective-permute-start | bytes 1081352 | tf_op jit(solution)/shard_map/ppermute | solution.py:602
  10.4 9.3 %collective-permute-start.4 = (bf16[11,128,128]{2,1,0:T(8,128)(2,1)S(1)}, bf16[11,128,128]{2,1,0:T(8,128)(2,1)S(1)}, u32[]{:S(2)}, u32[]{:S(2)}) collective-permute-start(bf16[11,128,128]{2,1,0:T(8,128)(2,1)S(1)} %get-tuple-element.28), channel_id=1, source_target_pairs={{0,1},{2,3},{4,5},{6,7},{8,9},{10,11},{12,13},{14,15},{1,0},{3,2},... | collective-permute-start | bytes 1081352 | tf_op jit(solution)/shard_map/ppermute | solution.py:596
  10.5 11.5 %collective-permute-start.3 = (bf16[7,128,128]{2,1,0:T(8,128)(2,1)S(1)}, bf16[7,128,128]{2,1,0:T(8,128)(2,1)S(1)}, u32[]{:S(2)}, u32[]{:S(2)}) collective-permute-start(bf16[7,128,128]{2,1,0:T(8,128)(2,1)S(1)} %get-tuple-element.27), channel_id=1, source_target_pairs={{1,2},{3,4},{5,6},{7,8},{9,10},{11,12},{13,14},{2,1},{4,3},{6,5},{... | collective-permute-start | bytes 688136 | tf_op jit(solution)/shard_map/ppermute | solution.py:602
  15.8 7.2 %collective-permute-start.2 = (bf16[4,128,128]{2,1,0:T(8,128)(2,1)S(1)}, bf16[4,128,128]{2,1,0:T(8,128)(2,1)S(1)}, u32[]{:S(2)}, u32[]{:S(2)}) collective-permute-start(bf16[4,128,128]{2,1,0:T(8,128)(2,1)S(1)} %get-tuple-element.26), channel_id=1, source_target_pairs={{1,2},{3,4},{5,6},{7,8},{9,10},{11,12},{13,14},{2,1},{4,3},{6,5},{... | collective-permute-start | bytes 393224 | tf_op jit(solution)/shard_map/ppermute | solution.py:602

commit v14 on v13

--- a/solution.py
+++ b/solution.py
@@ -205,7 +205,8 @@
     before = BUDGET
     for which in (CROSS_MANY, CROSS_FEW, NEAR_MANY, NEAR_FEW):
         before = before - COST[which % 2] * group_count(geo, meta_ref, which)
-    waiting = jnp.where(waits(), WAIT, 0)
+    rounds = (meta_ref[geo.lengths_at + CROSS] + LATE_GROUP - 1) // LATE_GROUP
+    waiting = jnp.where(waits(), WAIT - COST[0] * jnp.maximum(rounds - 1, 0), 0)
     share = []
     for which in (INNER_MANY, INNER_FEW):
         cost, count = COST[which % 2], group_count(geo, meta_ref, which)

time: 24.1 us -> 24 us (level)
  starting transfers between devices: 12.3 us -> 11.6 us
  Pallas kernels: 11.1 us -> 11.7 us
    pallas_call x1, Pallas kernels: 1.72 us -> 2.75 us  [local(): call(functools.partial(near_kernel, geo), (acc_type, pack(geo.halo)), [SM...]
    pallas_call x1, Pallas kernels: 2.25 us -> 1.24 us  [local(): call(functools.partial(early_kernel, geo), (acc_type, pack(geo.early)), [...]
    pallas_call x1, Pallas kernels: 0.7 us -> 1.7 us  [local(): call(functools.partial(waiting_kernel, geo), (acc_type, pltpu.SMEM((1,),...]
    ppermute x3, starting transfers between devices: 12.1 us -> 11.4 us  [to_second(): got = lax.ppermute(x, 'blk', pairs + [(j, i) for i, j in pairs])]
    pallas_call x2, Pallas kernels: 1.63 us -> 1 us  [local(): call(functools.partial(kernel_of, geo), whole, [SMEM_SPEC] + [VMEM_SPEC]...]
    pallas_call x1, Pallas kernels: 2.19 us -> 2.74 us  [local(): call(functools.partial(inner_kernel, geo), (acc_type, whole), [SMEM_SPEC]...]
    pallas_call x1, Pallas kernels: 1.04 us -> 0.75 us  [local(): call(functools.partial(late_kernel, geo), (h_type, pack(geo.late)), [SMEM...]
  transfers between devices with their start and end apart: 5 -> 5, of which waited for: 1 -> 1; matrix products, arithmetic and copies ran while one was open for 0% -> 0% of each run, Pallas kernels for 37% -> 39%
where the time goes in v14:
time: 24 us; the launch traced here: 23.7 us
  Pallas kernels  11.7 us (49%)
  starting transfers between devices  11.6 us (48%)
    ppermute x3, starting transfers between devices, to_second(): got = lax.ppermute(x, 'blk', pairs + [(j, i) for i, j in pairs])  11.4 us
    pallas_call x1, Pallas kernels, local(): call(functools.partial(near_kernel, geo), (acc_type, pack(geo.halo)), [SM...  2.75 us
    pallas_call x1, Pallas kernels, local(): call(functools.partial(inner_kernel, geo), (acc_type, whole), [SMEM_SPEC]...  2.74 us
    pallas_call x1, Pallas kernels, local(): call(functools.partial(waiting_kernel, geo), (acc_type, pltpu.SMEM((1,),...  1.7 us
    pallas_call x1, Pallas kernels, local(): call(functools.partial(pack_kernel, geo), (pack(geo.halo),) * 2 + (pltpu....  1.56 us
    pallas_call x1, Pallas kernels, local(): call(functools.partial(early_kernel, geo), (acc_type, pack(geo.early)), [...  1.24 us
    pallas_call x2, Pallas kernels, local(): call(functools.partial(kernel_of, geo), whole, [SMEM_SPEC] + [VMEM_SPEC]...  1 us
    pallas_call x1, Pallas kernels, local(): call(functools.partial(late_kernel, geo), (h_type, pack(geo.late)), [SMEM...  0.75 us
  transfers between devices with their start and end apart: 5, of which 1 were waited for; matrix products, arithmetic and copies ran while one was open for 0% of the time, Pallas kernels for 39%

profile of v14, /device:TPU:1, one launch (start us, length us, event | category | flops | bytes accessed | tf_op | source)
XLA Modules:
  0.0 23.7 jit_solution(13491150310313264643)
XLA Ops:
  0.0 0.0 copy-start
  0.0 0.0 copy-start.1
  0.0 0.0 copy-start.2
  0.0 0.0 copy-start.3
  0.0 1.6 %shard_map.73 = (bf16[11,128,128]{2,1,0:T(8,128)(2,1)S(1)}, bf16[11,128,128]{2,1,0:T(8,128)(2,1)S(1)}, s32[178]{0:T(256)S(4)}, f32[91,128,128]{2,1,0:T(8,128)S(1)}) custom-call(bf16[72,128,128]{2,1,0:T(8,128)(2,1)} %bitcast.3, s32[12]{0:T(128)} %centre_in.1, s32[4,12]{1,0:T(4,128)} %bitcast.8, s32[12]{0:T(128)} %counts_in.1), custom_call_target="tpu_custom_call" | custom-call | flops 10000000000 | bytes 100000000 | tf_op jit(solution)/shard_map/pallas_call | solution.py:618
  1.6 0.1 collective-permute-start
  1.7 4.6 %collective-permute-start.1 = (bf16[11,128,128]{2,1,0:T(8,128)(2,1)S(1)}, bf16[11,128,128]{2,1,0:T(8,128)(2,1)S(1)}, u32[]{:S(2)}, u32[]{:S(2)}) collective-permute-start(bf16[11,128,128]{2,1,0:T(8,128)(2,1)S(1)} %get-tuple-element.25), channel_id=1, source_target_pairs={{1,2},{3,4},{5,6},{7,8},{9,10},{11,12},{13,14},{2,1},{4,3},{6,5},{... | collective-permute-start | bytes 1081352 | tf_op jit(solution)/shard_map/ppermute | solution.py:603
  6.3 0.0 copy-done
  6.3 0.0 copy-done.1
  6.4 0.0 copy-done.2
  6.4 0.0 copy-done.3
  6.4 1.2 %shard_map.74 = (f32[91,128,128]{2,1,0:T(8,128)S(1)}, bf16[7,128,128]{2,1,0:T(8,128)(2,1)S(1)}) custom-call(s32[178]{0:T(256)S(4)} %get-tuple-element.19.meta_ref, bf16[72,128,128]{2,1,0:T(8,128)(2,1)S(1)} %bitcast.4, bf16[12,4,128,256]{3,2,1,0:T(8,128)(2,1)S(1)} %copy-done, bf16[12,256,256]{2,1,0:T(8,128)(2,1)S(1)} %copy-done.1, ...), custom_call_target="tpu_custom_call", output_to_operand_aliasing={{0}: (5, {})} | custom-call | tf_op jit(solution)/shard_map/pallas_call | solution.py:635
  7.6 0.0 collective-permute-done.halo_ref
  7.6 2.7 %shard_map.75 = (f32[91,128,128]{2,1,0:T(8,128)S(1)}, bf16[11,128,128]{2,1,0:T(8,128)(2,1)S(1)}) custom-call(s32[178]{0:T(256)S(4)} %get-tuple-element.19.meta_ref, bf16[11,128,128]{2,1,0:T(8,128)(2,1)S(1)} %collective-permute-done.halo_ref, bf16[72,128,128]{2,1,0:T(8,128)(2,1)S(1)} %bitcast.5, ...), custom_call_target="tpu_custom_call", output_to_operand_aliasing={{0}: (6, {})} | custom-call | tf_op jit(solution)/shard_map/pallas_call | solution.py:645
  10.4 0.1 collective-permute-start.4
  10.5 3.5 %collective-permute-start.3 = (bf16[7,128,128]{2,1,0:T(8,128)(2,1)S(1)}, bf16[7,128,128]{2,1,0:T(8,128)(2,1)S(1)}, u32[]{:S(2)}, u32[]{:S(2)}) collective-permute-start(bf16[7,128,128]{2,1,0:T(8,128)(2,1)S(1)} %get-tuple-element.27), channel_id=1, source_target_pairs={{1,2},{3,4},{5,6},{7,8},{9,10},{11,12},{13,14},{2,1},{4,3},{6,5},{... | collective-permute-start | bytes 688136 | tf_op jit(solution)/shard_map/ppermute | solution.py:603
  14.0 1.7 %shard_map.76 = (f32[91,128,128]{2,1,0:T(8,128)S(1)}, s32[1]{0:T(128)S(4)}) custom-call(s32[178]{0:T(256)S(4)} %get-tuple-element.19.meta_ref, bf16[72,128,128]{2,1,0:T(8,128)(2,1)S(1)} %bitcast.6, bf16[12,4,128,256]{3,2,1,0:T(8,128)(2,1)S(1)} %copy-done, bf16[12,256,256]{2,1,0:T(8,128)(2,1)S(1)} %copy-done.1, ...), custom_call_target="tpu_custom_call", output_to_operand_aliasing={{0}: (5, {})} | custom-call | tf_op jit(solution)/shard_map/pallas_call | solution.py:655
  15.7 0.0 collective-permute-done.1.halo_ref
  15.7 0.8 %shard_map.77 = (bf16[13,256,256]{2,1,0:T(8,128)(2,1)S(1)}, bf16[4,128,128]{2,1,0:T(8,128)(2,1)S(1)}) custom-call(s32[178]{0:T(256)S(4)} %get-tuple-element.19.meta_ref, s32[1]{0:T(128)S(4)} %get-tuple-element.24.done_ref, bf16[11,128,128]{2,1,0:T(8,128)(2,1)S(1)} %collective-permute-done.1.halo_ref, bf16[12,4,128,256]{3,2,1,0:T(8,128)(2,1)S(1)} %copy-done, ...), custom_call_target="tpu_custom_call" | custom-call | tf_op jit(solution)/shard_map/pallas_call | solution.py:665
  16.4 3.3 %collective-permute-start.2 = (bf16[4,128,128]{2,1,0:T(8,128)(2,1)S(1)}, bf16[4,128,128]{2,1,0:T(8,128)(2,1)S(1)}, u32[]{:S(2)}, u32[]{:S(2)}) collective-permute-start(bf16[4,128,128]{2,1,0:T(8,128)(2,1)S(1)} %get-tuple-element.26), channel_id=1, source_target_pairs={{1,2},{3,4},{5,6},{7,8},{9,10},{11,12},{13,14},{2,1},{4,3},{6,5},{... | collective-permute-start | bytes 393224 | tf_op jit(solution)/shard_map/ppermute | solution.py:603
  19.7 0.0 collective-permute-done.4.first_ref
  19.7 2.7 %shard_map.78 = (f32[91,128,128]{2,1,0:T(8,128)S(1)}, f32[72,128,128]{2,1,0:T(8,128)}) custom-call(s32[178]{0:T(256)S(4)} %get-tuple-element.19.meta_ref, bf16[11,128,128]{2,1,0:T(8,128)(2,1)S(1)} %collective-permute-done.4.first_ref, bf16[72,128,128]{2,1,0:T(8,128)(2,1)S(1)} %bitcast.7, ...), custom_call_target="tpu_custom_call", output_to_operand_aliasing={{0}: (7, {})} | custom-call | tf_op jit(solution)/shard_map/pallas_call | solution.py:675
  22.5 0.0 collective-permute-done.3.early_ref
  22.5 0.1 shard_map.79.out_in
  22.6 0.2 collective-permute-done.2.late_ref
  22.8 0.9 %shard_map.80 = f32[72,128,128]{2,1,0:T(8,128)} custom-call(s32[178]{0:T(256)S(4)} %get-tuple-element.19.meta_ref, bf16[4,128,128]{2,1,0:T(8,128)(2,1)S(1)} %collective-permute-done.2.late_ref, bf16[7,128,128]{2,1,0:T(8,128)(2,1)S(1)} %collective-permute-done.3.early_ref, ...), custom_call_target="tpu_custom_call", output_to_operand_aliasing={{}: (4, {})} | custom-call | tf_op jit(solution)/shard_map/pallas_call | solution.py:688
Async XLA Ops:
  0.0 6.3 %copy-start = (bf16[12,4,128,256]{3,2,1,0:T(8,128)(2,1)S(1)}, bf16[12,4,128,256]{3,2,1,0:T(8,128)(2,1)}, u32[]{:S(2)}) copy-start(bf16[12,4,128,256]{3,2,1,0:T(8,128)(2,1)} %ao_ref.9) | copy-start | bytes 9437188
  0.0 6.3 %copy-start.1 = (bf16[12,256,256]{2,1,0:T(8,128)(2,1)S(1)}, bf16[12,256,256]{2,1,0:T(8,128)(2,1)}, u32[]{:S(2)}) copy-start(bf16[12,256,256]{2,1,0:T(8,128)(2,1)} %kernel_ref.9) | copy-start | bytes 4718596
  0.0 6.4 %copy-start.2 = (bf16[8,9,128,128]{3,2,1,0:T(8,128)(2,1)S(1)}, bf16[8,9,128,128]{3,2,1,0:T(8,128)(2,1)}, u32[]{:S(2)}) copy-start(bf16[8,9,128,128]{3,2,1,0:T(8,128)(2,1)} %param.7) | copy-start | bytes 7077892
  0.0 6.4 %copy-start.3 = (f32[12,256]{1,0:T(8,128)S(1)}, f32[12,256]{1,0:T(8,128)}, u32[]{:S(2)}) copy-start(f32[12,256]{1,0:T(8,128)} %weights_ref.9) | copy-start | bytes 36868
  1.6 6.0 %collective-permute-start = (bf16[11,128,128]{2,1,0:T(8,128)(2,1)S(1)}, bf16[11,128,128]{2,1,0:T(8,128)(2,1)S(1)}, u32[]{:S(2)}, u32[]{:S(2)}) collective-permute-start(bf16[11,128,128]{2,1,0:T(8,128)(2,1)S(1)} %get-tuple-element.20), channel_id=1, source_target_pairs={{0,1},{2,3},{4,5},{6,7},{8,9},{10,11},{12,13},{14,15},{1,0},{3,2},... | collective-permute-start | bytes 1081352 | tf_op jit(solution)/shard_map/ppermute | solution.py:597
  1.7 14.0 %collective-permute-start.1 = (bf16[11,128,128]{2,1,0:T(8,128)(2,1)S(1)}, bf16[11,128,128]{2,1,0:T(8,128)(2,1)S(1)}, u32[]{:S(2)}, u32[]{:S(2)}) collective-permute-start(bf16[11,128,128]{2,1,0:T(8,128)(2,1)S(1)} %get-tuple-element.25), channel_id=1, source_target_pairs={{1,2},{3,4},{5,6},{7,8},{9,10},{11,12},{13,14},{2,1},{4,3},{6,5},{... | collective-permute-start | bytes 1081352 | tf_op jit(solution)/shard_map/ppermute | solution.py:603
  10.4 9.3 %collective-permute-start.4 = (bf16[11,128,128]{2,1,0:T(8,128)(2,1)S(1)}, bf16[11,128,128]{2,1,0:T(8,128)(2,1)S(1)}, u32[]{:S(2)}, u32[]{:S(2)}) collective-permute-start(bf16[11,128,128]{2,1,0:T(8,128)(2,1)S(1)} %get-tuple-element.28), channel_id=1, source_target_pairs={{0,1},{2,3},{4,5},{6,7},{8,9},{10,11},{12,13},{14,15},{1,0},{3,2},... | collective-permute-start | bytes 1081352 | tf_op jit(solution)/shard_map/ppermute | solution.py:597
  10.5 12.0 %collective-permute-start.3 = (bf16[7,128,128]{2,1,0:T(8,128)(2,1)S(1)}, bf16[7,128,128]{2,1,0:T(8,128)(2,1)S(1)}, u32[]{:S(2)}, u32[]{:S(2)}) collective-permute-start(bf16[7,128,128]{2,1,0:T(8,128)(2,1)S(1)} %get-tuple-element.27), channel_id=1, source_target_pairs={{1,2},{3,4},{5,6},{7,8},{9,10},{11,12},{13,14},{2,1},{4,3},{6,5},{... | collective-permute-start | bytes 688136 | tf_op jit(solution)/shard_map/ppermute | solution.py:603
  16.4 6.3 %collective-permute-start.2 = (bf16[4,128,128]{2,1,0:T(8,128)(2,1)S(1)}, bf16[4,128,128]{2,1,0:T(8,128)(2,1)S(1)}, u32[]{:S(2)}, u32[]{:S(2)}) collective-permute-start(bf16[4,128,128]{2,1,0:T(8,128)(2,1)S(1)} %get-tuple-element.26), channel_id=1, source_target_pairs={{1,2},{3,4},{5,6},{7,8},{9,10},{11,12},{13,14},{2,1},{4,3},{6,5},{... | collective-permute-start | bytes 393224 | tf_op jit(solution)/shard_map/ppermute | solution.py:603

commit v15 on v14

--- a/solution.py
+++ b/solution.py
@@ -12,7 +12,7 @@
 LATE_GROUP = 4
 LISTS = 7
 BUDGET = 43
-WAIT = 18
+WAIT = (24, 18)
 COST = (10, 7)
 SMEM_SPEC = pl.BlockSpec(memory_space=pltpu.SMEM)
 VMEM_SPEC = pl.BlockSpec(memory_space=pltpu.VMEM)
@@ -206,7 +206,8 @@
     for which in (CROSS_MANY, CROSS_FEW, NEAR_MANY, NEAR_FEW):
         before = before - COST[which % 2] * group_count(geo, meta_ref, which)
     rounds = (meta_ref[geo.lengths_at + CROSS] + LATE_GROUP - 1) // LATE_GROUP
-    waiting = jnp.where(waits(), WAIT - COST[0] * jnp.maximum(rounds - 1, 0), 0)
+    room = jnp.where(meta_ref[geo.odd_at] == 1, WAIT[1], WAIT[0])
+    waiting = jnp.where(waits(), room - COST[0] * jnp.maximum(rounds - 1, 0), 0)
     share = []
     for which in (INNER_MANY, INNER_FEW):
         cost, count = COST[which % 2], group_count(geo, meta_ref, which)

time: 24 us -> 24 us (level)
  Pallas kernels: 11.7 us -> 10.7 us
  starting transfers between devices: 11.6 us -> 12.6 us
    ppermute x3, starting transfers between devices: 11.4 us -> 12.4 us  [to_second(): got = lax.ppermute(x, 'blk', pairs + [(j, i) for i, j in pairs])]
    pallas_call x1, Pallas kernels: 1.7 us -> 0.71 us  [local(): call(functools.partial(waiting_kernel, geo), (acc_type, pltpu.SMEM((1,),...]
    pallas_call x2, Pallas kernels: 1 us -> 1.64 us  [local(): call(functools.partial(kernel_of, geo), whole, [SMEM_SPEC] + [VMEM_SPEC]...]
    pallas_call x1, Pallas kernels: 2.74 us -> 2.13 us  [local(): call(functools.partial(inner_kernel, geo), (acc_type, whole), [SMEM_SPEC]...]
  transfers between devices with their start and end apart: 5 -> 5, of which waited for: 1 -> 1; matrix products, arithmetic and copies ran while one was open for 0% -> 0% of each run, Pallas kernels for 39% -> 36%
where the time goes in v15:
time: 24 us; the launch traced here: 23.7 us
  starting transfers between devices  12.6 us (52%)
  Pallas kernels  10.7 us (45%)
  waiting for transfers between devices  0.25 us (1%)
    ppermute x3, starting transfers between devices, to_second(): got = lax.ppermute(x, 'blk', pairs + [(j, i) for i, j in pairs])  12.4 us
    pallas_call x1, Pallas kernels, local(): call(functools.partial(near_kernel, geo), (acc_type, pack(geo.halo)), [SM...  2.73 us
    pallas_call x1, Pallas kernels, local(): call(functools.partial(inner_kernel, geo), (acc_type, whole), [SMEM_SPEC]...  2.13 us
    pallas_call x2, Pallas kernels, local(): call(functools.partial(kernel_of, geo), whole, [SMEM_SPEC] + [VMEM_SPEC]...  1.64 us
    pallas_call x1, Pallas kernels, local(): call(functools.partial(pack_kernel, geo), (pack(geo.halo),) * 2 + (pltpu....  1.56 us
    pallas_call x1, Pallas kernels, local(): call(functools.partial(early_kernel, geo), (acc_type, pack(geo.early)), [...  1.24 us
    pallas_call x1, Pallas kernels, local(): call(functools.partial(late_kernel, geo), (h_type, pack(geo.late)), [SMEM...  0.75 us
    pallas_call x1, Pallas kernels, local(): call(functools.partial(waiting_kernel, geo), (acc_type, pltpu.SMEM((1,),...  0.71 us
  transfers between devices with their start and end apart: 5, of which 1 were waited for; matrix products, arithmetic and copies ran while one was open for 0% of the time, Pallas kernels for 36%

profile of v15, /device:TPU:1, one launch (start us, length us, event | category | flops | bytes accessed | tf_op | source)
XLA Modules:
  0.0 23.7 jit_solution(16764474623976265256)
XLA Ops:
  0.0 0.0 copy-start
  0.0 0.0 copy-start.1
  0.0 0.0 copy-start.2
  0.0 0.0 copy-start.3
  0.0 1.6 %shard_map.73 = (bf16[11,128,128]{2,1,0:T(8,128)(2,1)S(1)}, bf16[11,128,128]{2,1,0:T(8,128)(2,1)S(1)}, s32[178]{0:T(256)S(4)}, f32[91,128,128]{2,1,0:T(8,128)S(1)}) custom-call(bf16[72,128,128]{2,1,0:T(8,128)(2,1)} %bitcast.3, s32[12]{0:T(128)} %centre_in.1, s32[4,12]{1,0:T(4,128)} %bitcast.8, s32[12]{0:T(128)} %counts_in.1), custom_call_target="tpu_custom_call" | custom-call | flops 10000000000 | bytes 100000000 | tf_op jit(solution)/shard_map/pallas_call | solution.py:619
  1.6 0.1 collective-permute-start
  1.7 4.6 %collective-permute-start.1 = (bf16[11,128,128]{2,1,0:T(8,128)(2,1)S(1)}, bf16[11,128,128]{2,1,0:T(8,128)(2,1)S(1)}, u32[]{:S(2)}, u32[]{:S(2)}) collective-permute-start(bf16[11,128,128]{2,1,0:T(8,128)(2,1)S(1)} %get-tuple-element.25), channel_id=1, source_target_pairs={{1,2},{3,4},{5,6},{7,8},{9,10},{11,12},{13,14},{2,1},{4,3},{6,5},{... | collective-permute-start | bytes 1081352 | tf_op jit(solution)/shard_map/ppermute | solution.py:604
  6.3 0.0 copy-done
  6.3 0.0 copy-done.1
  6.4 0.0 copy-done.2
  6.4 0.0 copy-done.3
  6.4 1.2 %shard_map.74 = (f32[91,128,128]{2,1,0:T(8,128)S(1)}, bf16[7,128,128]{2,1,0:T(8,128)(2,1)S(1)}) custom-call(s32[178]{0:T(256)S(4)} %get-tuple-element.19.meta_ref, bf16[72,128,128]{2,1,0:T(8,128)(2,1)S(1)} %bitcast.4, bf16[12,4,128,256]{3,2,1,0:T(8,128)(2,1)S(1)} %copy-done, bf16[12,256,256]{2,1,0:T(8,128)(2,1)S(1)} %copy-done.1, ...), custom_call_target="tpu_custom_call", output_to_operand_aliasing={{0}: (5, {})} | custom-call | tf_op jit(solution)/shard_map/pallas_call | solution.py:636
  7.6 0.0 collective-permute-done.halo_ref
  7.6 2.7 %shard_map.75 = (f32[91,128,128]{2,1,0:T(8,128)S(1)}, bf16[11,128,128]{2,1,0:T(8,128)(2,1)S(1)}) custom-call(s32[178]{0:T(256)S(4)} %get-tuple-element.19.meta_ref, bf16[11,128,128]{2,1,0:T(8,128)(2,1)S(1)} %collective-permute-done.halo_ref, bf16[72,128,128]{2,1,0:T(8,128)(2,1)S(1)} %bitcast.5, ...), custom_call_target="tpu_custom_call", output_to_operand_aliasing={{0}: (6, {})} | custom-call | tf_op jit(solution)/shard_map/pallas_call | solution.py:646
  10.4 0.1 collective-permute-start.4
  10.4 3.9 %collective-permute-start.3 = (bf16[7,128,128]{2,1,0:T(8,128)(2,1)S(1)}, bf16[7,128,128]{2,1,0:T(8,128)(2,1)S(1)}, u32[]{:S(2)}, u32[]{:S(2)}) collective-permute-start(bf16[7,128,128]{2,1,0:T(8,128)(2,1)S(1)} %get-tuple-element.27), channel_id=1, source_target_pairs={{1,2},{3,4},{5,6},{7,8},{9,10},{11,12},{13,14},{2,1},{4,3},{6,5},{... | collective-permute-start | bytes 688136 | tf_op jit(solution)/shard_map/ppermute | solution.py:604
  14.4 0.7 %shard_map.76 = (f32[91,128,128]{2,1,0:T(8,128)S(1)}, s32[1]{0:T(128)S(4)}) custom-call(s32[178]{0:T(256)S(4)} %get-tuple-element.19.meta_ref, bf16[72,128,128]{2,1,0:T(8,128)(2,1)S(1)} %bitcast.6, bf16[12,4,128,256]{3,2,1,0:T(8,128)(2,1)S(1)} %copy-done, bf16[12,256,256]{2,1,0:T(8,128)(2,1)S(1)} %copy-done.1, ...), custom_call_target="tpu_custom_call", output_to_operand_aliasing={{0}: (5, {})} | custom-call | tf_op jit(solution)/shard_map/pallas_call | solution.py:656
  15.1 0.0 collective-permute-done.1.halo_ref
  15.1 0.7 %shard_map.77 = (bf16[13,256,256]{2,1,0:T(8,128)(2,1)S(1)}, bf16[4,128,128]{2,1,0:T(8,128)(2,1)S(1)}) custom-call(s32[178]{0:T(256)S(4)} %get-tuple-element.19.meta_ref, s32[1]{0:T(128)S(4)} %get-tuple-element.24.done_ref, bf16[11,128,128]{2,1,0:T(8,128)(2,1)S(1)} %collective-permute-done.1.halo_ref, bf16[12,4,128,256]{3,2,1,0:T(8,128)(2,1)S(1)} %copy-done, ...), custom_call_target="tpu_custom_call" | custom-call | tf_op jit(solution)/shard_map/pallas_call | solution.py:666
  15.8 3.8 %collective-permute-start.2 = (bf16[4,128,128]{2,1,0:T(8,128)(2,1)S(1)}, bf16[4,128,128]{2,1,0:T(8,128)(2,1)S(1)}, u32[]{:S(2)}, u32[]{:S(2)}) collective-permute-start(bf16[4,128,128]{2,1,0:T(8,128)(2,1)S(1)} %get-tuple-element.26), channel_id=1, source_target_pairs={{1,2},{3,4},{5,6},{7,8},{9,10},{11,12},{13,14},{2,1},{4,3},{6,5},{... | collective-permute-start | bytes 393224 | tf_op jit(solution)/shard_map/ppermute | solution.py:604
  19.7 0.0 collective-permute-done.4.first_ref
  19.7 2.1 %shard_map.78 = (f32[91,128,128]{2,1,0:T(8,128)S(1)}, f32[72,128,128]{2,1,0:T(8,128)}) custom-call(s32[178]{0:T(256)S(4)} %get-tuple-element.19.meta_ref, bf16[11,128,128]{2,1,0:T(8,128)(2,1)S(1)} %collective-permute-done.4.first_ref, bf16[72,128,128]{2,1,0:T(8,128)(2,1)S(1)} %bitcast.7, ...), custom_call_target="tpu_custom_call", output_to_operand_aliasing={{0}: (7, {})} | custom-call | tf_op jit(solution)/shard_map/pallas_call | solution.py:676
  21.8 0.0 collective-permute-done.3.early_ref
  21.9 0.9 %shard_map.79.out_in = f32[72,128,128]{2,1,0:T(8,128)} custom-call(s32[178]{0:T(256)S(4)} %get-tuple-element.19.meta_ref, bf16[7,128,128]{2,1,0:T(8,128)(2,1)S(1)} %collective-permute-done.3.early_ref, f32[91,128,128]{2,1,0:T(8,128)S(1)} %get-tuple-element.31.acc_ref, f32[72,128,128]{2,1,0:T(8,128)} %get-tuple-element.32.out_in), custom_call_target="tpu_custom_call", output_to_operand_aliasing={{}: (3, {})} | custom-call | tf_op jit(solution)/shard_map/pallas_call | solution.py:689
  22.7 0.2 %collective-permute-done.2.late_ref = bf16[4,128,128]{2,1,0:T(8,128)(2,1)S(1)} collective-permute-done((bf16[4,128,128]{2,1,0:T(8,128)(2,1)S(1)}, bf16[4,128,128]{2,1,0:T(8,128)(2,1)S(1)}, u32[]{:S(2)}, u32[]{:S(2)}) %collective-permute-start.2) | collective-permute-done | bytes 131104 | tf_op jit(solution)/shard_map/ppermute | solution.py:604
  23.0 0.7 %shard_map.80 = f32[72,128,128]{2,1,0:T(8,128)} custom-call(s32[178]{0:T(256)S(4)} %get-tuple-element.19.meta_ref, bf16[4,128,128]{2,1,0:T(8,128)(2,1)S(1)} %collective-permute-done.2.late_ref, bf16[7,128,128]{2,1,0:T(8,128)(2,1)S(1)} %collective-permute-done.3.early_ref, ...), custom_call_target="tpu_custom_call", output_to_operand_aliasing={{}: (4, {})} | custom-call | tf_op jit(solution)/shard_map/pallas_call | solution.py:689
Async XLA Ops:
  0.0 6.3 %copy-start = (bf16[12,4,128,256]{3,2,1,0:T(8,128)(2,1)S(1)}, bf16[12,4,128,256]{3,2,1,0:T(8,128)(2,1)}, u32[]{:S(2)}) copy-start(bf16[12,4,128,256]{3,2,1,0:T(8,128)(2,1)} %ao_ref.9) | copy-start | bytes 9437188
  0.0 6.3 %copy-start.1 = (bf16[12,256,256]{2,1,0:T(8,128)(2,1)S(1)}, bf16[12,256,256]{2,1,0:T(8,128)(2,1)}, u32[]{:S(2)}) copy-start(bf16[12,256,256]{2,1,0:T(8,128)(2,1)} %kernel_ref.9) | copy-start | bytes 4718596
  0.0 6.4 %copy-start.2 = (bf16[8,9,128,128]{3,2,1,0:T(8,128)(2,1)S(1)}, bf16[8,9,128,128]{3,2,1,0:T(8,128)(2,1)}, u32[]{:S(2)}) copy-start(bf16[8,9,128,128]{3,2,1,0:T(8,128)(2,1)} %param.7) | copy-start | bytes 7077892
  0.0 6.4 %copy-start.3 = (f32[12,256]{1,0:T(8,128)S(1)}, f32[12,256]{1,0:T(8,128)}, u32[]{:S(2)}) copy-start(f32[12,256]{1,0:T(8,128)} %weights_ref.9) | copy-start | bytes 36868
  1.6 6.0 %collective-permute-start = (bf16[11,128,128]{2,1,0:T(8,128)(2,1)S(1)}, bf16[11,128,128]{2,1,0:T(8,128)(2,1)S(1)}, u32[]{:S(2)}, u32[]{:S(2)}) collective-permute-start(bf16[11,128,128]{2,1,0:T(8,128)(2,1)S(1)} %get-tuple-element.20), channel_id=1, source_target_pairs={{0,1},{2,3},{4,5},{6,7},{8,9},{10,11},{12,13},{14,15},{1,0},{3,2},... | collective-permute-start | bytes 1081352 | tf_op jit(solution)/shard_map/ppermute | solution.py:598
  1.7 13.4 %collective-permute-start.1 = (bf16[11,128,128]{2,1,0:T(8,128)(2,1)S(1)}, bf16[11,128,128]{2,1,0:T(8,128)(2,1)S(1)}, u32[]{:S(2)}, u32[]{:S(2)}) collective-permute-start(bf16[11,128,128]{2,1,0:T(8,128)(2,1)S(1)} %get-tuple-element.25), channel_id=1, source_target_pairs={{1,2},{3,4},{5,6},{7,8},{9,10},{11,12},{13,14},{2,1},{4,3},{6,5},{... | collective-permute-start | bytes 1081352 | tf_op jit(solution)/shard_map/ppermute | solution.py:604
  10.4 9.3 %collective-permute-start.4 = (bf16[11,128,128]{2,1,0:T(8,128)(2,1)S(1)}, bf16[11,128,128]{2,1,0:T(8,128)(2,1)S(1)}, u32[]{:S(2)}, u32[]{:S(2)}) collective-permute-start(bf16[11,128,128]{2,1,0:T(8,128)(2,1)S(1)} %get-tuple-element.28), channel_id=1, source_target_pairs={{0,1},{2,3},{4,5},{6,7},{8,9},{10,11},{12,13},{14,15},{1,0},{3,2},... | collective-permute-start | bytes 1081352 | tf_op jit(solution)/shard_map/ppermute | solution.py:598
  10.4 11.4 %collective-permute-start.3 = (bf16[7,128,128]{2,1,0:T(8,128)(2,1)S(1)}, bf16[7,128,128]{2,1,0:T(8,128)(2,1)S(1)}, u32[]{:S(2)}, u32[]{:S(2)}) collective-permute-start(bf16[7,128,128]{2,1,0:T(8,128)(2,1)S(1)} %get-tuple-element.27), channel_id=1, source_target_pairs={{1,2},{3,4},{5,6},{7,8},{9,10},{11,12},{13,14},{2,1},{4,3},{6,5},{... | collective-permute-start | bytes 688136 | tf_op jit(solution)/shard_map/ppermute | solution.py:604
  15.8 7.2 %collective-permute-start.2 = (bf16[4,128,128]{2,1,0:T(8,128)(2,1)S(1)}, bf16[4,128,128]{2,1,0:T(8,128)(2,1)S(1)}, u32[]{:S(2)}, u32[]{:S(2)}) collective-permute-start(bf16[4,128,128]{2,1,0:T(8,128)(2,1)S(1)} %get-tuple-element.26), channel_id=1, source_target_pairs={{1,2},{3,4},{5,6},{7,8},{9,10},{11,12},{13,14},{2,1},{4,3},{6,5},{... | collective-permute-start | bytes 393224 | tf_op jit(solution)/shard_map/ppermute | solution.py:604

commit v16 on v14

--- a/solution.py
+++ b/solution.py
@@ -11,7 +11,7 @@
 GROUP = 2
 LATE_GROUP = 4
 LISTS = 7
-BUDGET = 43
+BUDGET = 45
 WAIT = 18
 COST = (10, 7)
 SMEM_SPEC = pl.BlockSpec(memory_space=pltpu.SMEM)

time: 24 us -> 24.2 us (level); the launches traced: 23.7 us -> 24.2 us
  starting transfers between devices: 11.6 us -> 11.9 us
    pallas_call x1, Pallas kernels: 2.75 us -> 3.14 us  [local(): call(functools.partial(near_kernel, geo), (acc_type, pack(geo.halo)), [SM...]
    pallas_call x1, Pallas kernels: 1.7 us -> 1.31 us  [local(): call(functools.partial(waiting_kernel, geo), (acc_type, pltpu.SMEM((1,),...]
    ppermute x3, starting transfers between devices: 11.4 us -> 11.7 us  [to_second(): got = lax.ppermute(x, 'blk', pairs + [(j, i) for i, j in pairs])]
  transfers between devices with their start and end apart: 5 -> 5, of which waited for: 1 -> 1; matrix products, arithmetic and copies ran while one was open for 0% -> 0% of each run, Pallas kernels for 39% -> 38%
where the time goes in v16:
time: 24.2 us
  starting transfers between devices  11.9 us (49%)
  Pallas kernels  11.7 us (48%)
  waiting for transfers between devices  0.43 us (2%)
    ppermute x3, starting transfers between devices, to_second(): got = lax.ppermute(x, 'blk', pairs + [(j, i) for i, j in pairs])  11.7 us
    pallas_call x1, Pallas kernels, local(): call(functools.partial(near_kernel, geo), (acc_type, pack(geo.halo)), [SM...  3.14 us
    pallas_call x1, Pallas kernels, local(): call(functools.partial(inner_kernel, geo), (acc_type, whole), [SMEM_SPEC]...  2.74 us
    pallas_call x1, Pallas kernels, local(): call(functools.partial(pack_kernel, geo), (pack(geo.halo),) * 2 + (pltpu....  1.56 us
    pallas_call x1, Pallas kernels, local(): call(functools.partial(waiting_kernel, geo), (acc_type, pltpu.SMEM((1,),...  1.31 us
    pallas_call x1, Pallas kernels, local(): call(functools.partial(early_kernel, geo), (acc_type, pack(geo.early)), [...  1.24 us
    pallas_call x2, Pallas kernels, local(): call(functools.partial(kernel_of, geo), whole, [SMEM_SPEC] + [VMEM_SPEC]...  1 us
    pallas_call x1, Pallas kernels, local(): call(functools.partial(late_kernel, geo), (h_type, pack(geo.late)), [SMEM...  0.75 us
  transfers between devices with their start and end apart: 5, of which 1 were waited for; matrix products, arithmetic and copies ran while one was open for 0% of the time, Pallas kernels for 38%

profile of v16, /device:TPU:1, one launch (start us, length us, event | category | flops | bytes accessed | tf_op | source)
XLA Modules:
  0.0 24.2 jit_solution(7760325982086382863)
XLA Ops:
  0.0 0.0 copy-start
  0.0 0.0 copy-start.1
  0.0 0.0 copy-start.2
  0.0 0.0 copy-start.3
  0.0 1.6 %shard_map.73 = (bf16[11,128,128]{2,1,0:T(8,128)(2,1)S(1)}, bf16[11,128,128]{2,1,0:T(8,128)(2,1)S(1)}, s32[178]{0:T(256)S(4)}, f32[91,128,128]{2,1,0:T(8,128)S(1)}) custom-call(bf16[72,128,128]{2,1,0:T(8,128)(2,1)} %bitcast.3, s32[12]{0:T(128)} %centre_in.1, s32[4,12]{1,0:T(4,128)} %bitcast.8, s32[12]{0:T(128)} %counts_in.1), custom_call_target="tpu_custom_call" | custom-call | flops 10000000000 | bytes 100000000 | tf_op jit(solution)/shard_map/pallas_call | solution.py:618
  1.6 0.1 collective-permute-start
  1.7 4.6 %collective-permute-start.1 = (bf16[11,128,128]{2,1,0:T(8,128)(2,1)S(1)}, bf16[11,128,128]{2,1,0:T(8,128)(2,1)S(1)}, u32[]{:S(2)}, u32[]{:S(2)}) collective-permute-start(bf16[11,128,128]{2,1,0:T(8,128)(2,1)S(1)} %get-tuple-element.25), channel_id=1, source_target_pairs={{1,2},{3,4},{5,6},{7,8},{9,10},{11,12},{13,14},{2,1},{4,3},{6,5},{... | collective-permute-start | bytes 1081352 | tf_op jit(solution)/shard_map/ppermute | solution.py:603
  6.3 0.0 copy-done
  6.3 0.0 copy-done.1
  6.4 0.0 copy-done.2
  6.4 0.0 copy-done.3
  6.4 1.2 %shard_map.74 = (f32[91,128,128]{2,1,0:T(8,128)S(1)}, bf16[7,128,128]{2,1,0:T(8,128)(2,1)S(1)}) custom-call(s32[178]{0:T(256)S(4)} %get-tuple-element.19.meta_ref, bf16[72,128,128]{2,1,0:T(8,128)(2,1)S(1)} %bitcast.4, bf16[12,4,128,256]{3,2,1,0:T(8,128)(2,1)S(1)} %copy-done, bf16[12,256,256]{2,1,0:T(8,128)(2,1)S(1)} %copy-done.1, ...), custom_call_target="tpu_custom_call", output_to_operand_aliasing={{0}: (5, {})} | custom-call | tf_op jit(solution)/shard_map/pallas_call | solution.py:635
  7.6 0.0 collective-permute-done.halo_ref
  7.6 3.1 %shard_map.75 = (f32[91,128,128]{2,1,0:T(8,128)S(1)}, bf16[11,128,128]{2,1,0:T(8,128)(2,1)S(1)}) custom-call(s32[178]{0:T(256)S(4)} %get-tuple-element.19.meta_ref, bf16[11,128,128]{2,1,0:T(8,128)(2,1)S(1)} %collective-permute-done.halo_ref, bf16[72,128,128]{2,1,0:T(8,128)(2,1)S(1)} %bitcast.5, ...), custom_call_target="tpu_custom_call", output_to_operand_aliasing={{0}: (6, {})} | custom-call | tf_op jit(solution)/shard_map/pallas_call | solution.py:645
  10.8 0.1 collective-permute-start.4
  10.9 3.3 %collective-permute-start.3 = (bf16[7,128,128]{2,1,0:T(8,128)(2,1)S(1)}, bf16[7,128,128]{2,1,0:T(8,128)(2,1)S(1)}, u32[]{:S(2)}, u32[]{:S(2)}) collective-permute-start(bf16[7,128,128]{2,1,0:T(8,128)(2,1)S(1)} %get-tuple-element.27), channel_id=1, source_target_pairs={{1,2},{3,4},{5,6},{7,8},{9,10},{11,12},{13,14},{2,1},{4,3},{6,5},{... | collective-permute-start | bytes 688136 | tf_op jit(solution)/shard_map/ppermute | solution.py:603
  14.2 1.3 %shard_map.76 = (f32[91,128,128]{2,1,0:T(8,128)S(1)}, s32[1]{0:T(128)S(4)}) custom-call(s32[178]{0:T(256)S(4)} %get-tuple-element.19.meta_ref, bf16[72,128,128]{2,1,0:T(8,128)(2,1)S(1)} %bitcast.6, bf16[12,4,128,256]{3,2,1,0:T(8,128)(2,1)S(1)} %copy-done, bf16[12,256,256]{2,1,0:T(8,128)(2,1)S(1)} %copy-done.1, ...), custom_call_target="tpu_custom_call", output_to_operand_aliasing={{0}: (5, {})} | custom-call | tf_op jit(solution)/shard_map/pallas_call | solution.py:655
  15.5 0.0 collective-permute-done.1.halo_ref
  15.5 0.7 %shard_map.77 = (bf16[13,256,256]{2,1,0:T(8,128)(2,1)S(1)}, bf16[4,128,128]{2,1,0:T(8,128)(2,1)S(1)}) custom-call(s32[178]{0:T(256)S(4)} %get-tuple-element.19.meta_ref, s32[1]{0:T(128)S(4)} %get-tuple-element.24.done_ref, bf16[11,128,128]{2,1,0:T(8,128)(2,1)S(1)} %collective-permute-done.1.halo_ref, bf16[12,4,128,256]{3,2,1,0:T(8,128)(2,1)S(1)} %copy-done, ...), custom_call_target="tpu_custom_call" | custom-call | tf_op jit(solution)/shard_map/pallas_call | solution.py:665
  16.3 3.7 %collective-permute-start.2 = (bf16[4,128,128]{2,1,0:T(8,128)(2,1)S(1)}, bf16[4,128,128]{2,1,0:T(8,128)(2,1)S(1)}, u32[]{:S(2)}, u32[]{:S(2)}) collective-permute-start(bf16[4,128,128]{2,1,0:T(8,128)(2,1)S(1)} %get-tuple-element.26), channel_id=1, source_target_pairs={{1,2},{3,4},{5,6},{7,8},{9,10},{11,12},{13,14},{2,1},{4,3},{6,5},{... | collective-permute-start | bytes 393224 | tf_op jit(solution)/shard_map/ppermute | solution.py:603
  20.0 0.0 collective-permute-done.4.first_ref
  20.0 2.7 %shard_map.78 = (f32[91,128,128]{2,1,0:T(8,128)S(1)}, f32[72,128,128]{2,1,0:T(8,128)}) custom-call(s32[178]{0:T(256)S(4)} %get-tuple-element.19.meta_ref, bf16[11,128,128]{2,1,0:T(8,128)(2,1)S(1)} %collective-permute-done.4.first_ref, bf16[72,128,128]{2,1,0:T(8,128)(2,1)S(1)} %bitcast.7, ...), custom_call_target="tpu_custom_call", output_to_operand_aliasing={{0}: (7, {})} | custom-call | tf_op jit(solution)/shard_map/pallas_call | solution.py:675
  22.7 0.0 collective-permute-done.3.early_ref
  22.8 0.1 shard_map.79.out_in
  22.9 0.4 %collective-permute-done.2.late_ref = bf16[4,128,128]{2,1,0:T(8,128)(2,1)S(1)} collective-permute-done((bf16[4,128,128]{2,1,0:T(8,128)(2,1)S(1)}, bf16[4,128,128]{2,1,0:T(8,128)(2,1)S(1)}, u32[]{:S(2)}, u32[]{:S(2)}) %collective-permute-start.2) | collective-permute-done | bytes 131104 | tf_op jit(solution)/shard_map/ppermute | solution.py:603
  23.3 0.9 %shard_map.80 = f32[72,128,128]{2,1,0:T(8,128)} custom-call(s32[178]{0:T(256)S(4)} %get-tuple-element.19.meta_ref, bf16[4,128,128]{2,1,0:T(8,128)(2,1)S(1)} %collective-permute-done.2.late_ref, bf16[7,128,128]{2,1,0:T(8,128)(2,1)S(1)} %collective-permute-done.3.early_ref, ...), custom_call_target="tpu_custom_call", output_to_operand_aliasing={{}: (4, {})} | custom-call | tf_op jit(solution)/shard_map/pallas_call | solution.py:688
Async XLA Ops:
  0.0 6.3 %copy-start = (bf16[12,4,128,256]{3,2,1,0:T(8,128)(2,1)S(1)}, bf16[12,4,128,256]{3,2,1,0:T(8,128)(2,1)}, u32[]{:S(2)}) copy-start(bf16[12,4,128,256]{3,2,1,0:T(8,128)(2,1)} %ao_ref.9) | copy-start | bytes 9437188
  0.0 6.3 %copy-start.1 = (bf16[12,256,256]{2,1,0:T(8,128)(2,1)S(1)}, bf16[12,256,256]{2,1,0:T(8,128)(2,1)}, u32[]{:S(2)}) copy-start(bf16[12,256,256]{2,1,0:T(8,128)(2,1)} %kernel_ref.9) | copy-start | bytes 4718596
  0.0 6.4 %copy-start.2 = (bf16[8,9,128,128]{3,2,1,0:T(8,128)(2,1)S(1)}, bf16[8,9,128,128]{3,2,1,0:T(8,128)(2,1)}, u32[]{:S(2)}) copy-start(bf16[8,9,128,128]{3,2,1,0:T(8,128)(2,1)} %param.7) | copy-start | bytes 7077892
  0.0 6.4 %copy-start.3 = (f32[12,256]{1,0:T(8,128)S(1)}, f32[12,256]{1,0:T(8,128)}, u32[]{:S(2)}) copy-start(f32[12,256]{1,0:T(8,128)} %weights_ref.9) | copy-start | bytes 36868
  1.6 6.0 %collective-permute-start = (bf16[11,128,128]{2,1,0:T(8,128)(2,1)S(1)}, bf16[11,128,128]{2,1,0:T(8,128)(2,1)S(1)}, u32[]{:S(2)}, u32[]{:S(2)}) collective-permute-start(bf16[11,128,128]{2,1,0:T(8,128)(2,1)S(1)} %get-tuple-element.20), channel_id=1, source_target_pairs={{0,1},{2,3},{4,5},{6,7},{8,9},{10,11},{12,13},{14,15},{1,0},{3,2},... | collective-permute-start | bytes 1081352 | tf_op jit(solution)/shard_map/ppermute | solution.py:597
  1.7 13.8 %collective-permute-start.1 = (bf16[11,128,128]{2,1,0:T(8,128)(2,1)S(1)}, bf16[11,128,128]{2,1,0:T(8,128)(2,1)S(1)}, u32[]{:S(2)}, u32[]{:S(2)}) collective-permute-start(bf16[11,128,128]{2,1,0:T(8,128)(2,1)S(1)} %get-tuple-element.25), channel_id=1, source_target_pairs={{1,2},{3,4},{5,6},{7,8},{9,10},{11,12},{13,14},{2,1},{4,3},{6,5},{... | collective-permute-start | bytes 1081352 | tf_op jit(solution)/shard_map/ppermute | solution.py:603
  10.8 9.2 %collective-permute-start.4 = (bf16[11,128,128]{2,1,0:T(8,128)(2,1)S(1)}, bf16[11,128,128]{2,1,0:T(8,128)(2,1)S(1)}, u32[]{:S(2)}, u32[]{:S(2)}) collective-permute-start(bf16[11,128,128]{2,1,0:T(8,128)(2,1)S(1)} %get-tuple-element.28), channel_id=1, source_target_pairs={{0,1},{2,3},{4,5},{6,7},{8,9},{10,11},{12,13},{14,15},{1,0},{3,2},... | collective-permute-start | bytes 1081352 | tf_op jit(solution)/shard_map/ppermute | solution.py:597
  10.9 11.9 %collective-permute-start.3 = (bf16[7,128,128]{2,1,0:T(8,128)(2,1)S(1)}, bf16[7,128,128]{2,1,0:T(8,128)(2,1)S(1)}, u32[]{:S(2)}, u32[]{:S(2)}) collective-permute-start(bf16[7,128,128]{2,1,0:T(8,128)(2,1)S(1)} %get-tuple-element.27), channel_id=1, source_target_pairs={{1,2},{3,4},{5,6},{7,8},{9,10},{11,12},{13,14},{2,1},{4,3},{6,5},{... | collective-permute-start | bytes 688136 | tf_op jit(solution)/shard_map/ppermute | solution.py:603
  16.3 7.0 %collective-permute-start.2 = (bf16[4,128,128]{2,1,0:T(8,128)(2,1)S(1)}, bf16[4,128,128]{2,1,0:T(8,128)(2,1)S(1)}, u32[]{:S(2)}, u32[]{:S(2)}) collective-permute-start(bf16[4,128,128]{2,1,0:T(8,128)(2,1)S(1)} %get-tuple-element.26), channel_id=1, source_target_pairs={{1,2},{3,4},{5,6},{7,8},{9,10},{11,12},{13,14},{2,1},{4,3},{6,5},{... | collective-permute-start | bytes 393224 | tf_op jit(solution)/shard_map/ppermute | solution.py:603
